TPU v7x, 128 devices: a whole 4x4x4 slice. The times are simulated.
128 devices in a mesh: lat: 16 (over x, z), lon: 8 (over y, core).
Axes of the slice: x: 4, y: 4, z: 4, core: 2. Of those that a mesh axis runs over, the one named last changes fastest.
Arguments:
- field: bfloat16 [384, 720, 384], P('lat', 'lon'), may hold values from -6 to 6
- cotangent: bfloat16 [384, 720, 384], P('lat', 'lon'), may hold values from -6 to 6
- kernel_weights: bfloat16 [3, 384, 384], replicated, may hold values from -0.1875 to 0.1875
- spectral_weight: bfloat16 [384, 384], replicated, may hold values from -0.3125 to 0.3125
- out_weight: bfloat16 [384, 384], replicated, may hold values from -0.3125 to 0.3125
- degree_gain: float32 [192, 384], replicated, may hold values from 0.5 to 4
- kernel_basis: float32 [3, 3, 7, 384], replicated, may hold values from -2.5 to 2.5
- lon_reach: int32 [3, 384], replicated, may hold values from 1 to 3, as said below
Outputs:
- output_field: bfloat16 [384, 720, 384], P('lat', 'lon')
- grad_field: bfloat16 [384, 720, 384], P('lat', 'lon')
- weight_grads: float32 [5, 384, 384], replicated
- gain_grad: float32 [192, 384], replicated
Inputs may be any that keep to these rules, and one draw needn't show every extreme that they name: lon_reach[r, i] counts the longitude cells on each side that the kernels of output row i cover at row offset r - 1; the two polar rows cover 3.
All inputs are finite; a program needn't handle non-finite values.
Results may differ from a plain program's by a relative error of at most 0.03.
Values may be sent and summed in bfloat16 or wider, within the bound.
A program may use at most 192 MiB of HBM per device.

v0:
```python
import math

import jax
import jax.numpy as jnp
from jax import lax
from jax.sharding import PartitionSpec as P

ORDERS = 192


def padded(cells, sides, width, closed):
    for axis, dim in sides:
        count = lax.axis_size(axis)
        ends = count if closed else count - 1
        head = lax.slice_in_dim(cells, 0, width, axis=dim)
        tail = lax.slice_in_dim(cells, cells.shape[dim] - width, cells.shape[dim], axis=dim)
        cells = jnp.concatenate(
            [
                lax.ppermute(tail, axis, [(i, (i + 1) % count) for i in range(ends)]),
                cells,
                lax.ppermute(head, axis, [((i + 1) % count, i) for i in range(ends)]),
            ],
            axis=dim,
        )
    return cells


def colatitudes(row_index, lat_count):
    return (row_index.astype(jnp.float32) + 0.5) * (math.pi / lat_count)


def quadrature(colatitude, lat_count, lon_count):
    return 2.0 * math.pi / lon_count * (math.pi / lat_count) * jnp.sin(colatitude)


def legendre_table(colatitude, orders, degree_count):
    cos_rows = jnp.cos(colatitude)[:, None]
    sin_rows = jnp.sin(colatitude)[:, None]
    order_f = orders.astype(jnp.float32)[None, :]
    log_start = 0.5 * (
        lax.lgamma(order_f + 1.5)
        - lax.lgamma(order_f + 1.0)
        - lax.lgamma(jnp.float32(1.5) + 0.0 * order_f)
    ) + order_f * jnp.log(sin_rows)
    diagonal = jnp.exp(log_start) / math.sqrt(4.0 * math.pi)

    def advance(running, degree):
        previous, before, ratio_prev = running
        degree_f = degree.astype(jnp.float32)
        above = degree_f > order_f
        denominator = jnp.where(above, degree_f * degree_f - order_f * order_f, 1.0)
        ratio_now = jnp.where(above, jnp.sqrt((4.0 * degree_f * degree_f - 1.0) / denominator), 1.0)
        current = jnp.where(
            degree_f == order_f,
            diagonal,
            jnp.where(above, ratio_now * (cos_rows * previous - before / ratio_prev), 0.0),
        )
        return ((current, previous, ratio_now), current)

    blank = jnp.zeros((colatitude.shape[0], orders.shape[0]), jnp.float32)
    initial = (blank, blank, jnp.ones((1, orders.shape[0]), jnp.float32))
    final_state, legendre_values = lax.scan(
        advance, initial, jnp.arange(degree_count, dtype=jnp.int32)
    )
    return legendre_values


def fourier_table(lon_count, order_count):
    columns = jnp.arange(2 * order_count, dtype=jnp.int32)
    orders = columns % order_count
    row_index = jnp.arange(lon_count, dtype=jnp.int32)
    angles = (row_index[:, None] * orders[None, :] % lon_count).astype(jnp.float32) * (
        2.0 * math.pi / lon_count
    )
    return jnp.where(columns[None, :] < order_count, jnp.cos(angles), -jnp.sin(angles)).astype(
        jnp.bfloat16
    )


def tap_table(kernel_basis, lon_reach):
    tap_count = kernel_basis.shape[2]
    offsets = jnp.abs(jnp.arange(tap_count, dtype=jnp.int32) - tap_count // 2)
    reach_mask = offsets[None, :, None] <= lon_reach[:, None, :]
    return kernel_basis * reach_mask[None].astype(jnp.float32)


def gelu_value(pre_act):
    inside = 0.7978845608 * (pre_act + 0.044715 * pre_act * pre_act * pre_act)
    return 0.5 * pre_act * (1.0 + jnp.tanh(inside))


def gelu_slope(pre_act):
    inside = 0.7978845608 * (pre_act + 0.044715 * pre_act * pre_act * pre_act)
    tangent = jnp.tanh(inside)
    return 0.5 * (1.0 + tangent) + 0.5 * pre_act * (1.0 - tangent * tangent) * 0.7978845608 * (
        1.0 + 3.0 * 0.044715 * pre_act * pre_act
    )


def widen(stacked, lon_span):
    widened = padded(stacked, (("lon", 2),), lon_span, True)
    return padded(widened, (("lat", 1),), 1, False)


def kernel_forward(extended, own_taps, lat_rows, lon_cells):
    tap_count = own_taps.shape[2]
    source = extended[0].astype(jnp.float32)
    outputs = []
    for kernel in range(own_taps.shape[0]):
        summed = jnp.zeros((lat_rows, lon_cells, source.shape[-1]), jnp.float32)
        for lat_step in range(3):
            for lon_step in range(tap_count):
                window = source[lat_step : lat_step + lat_rows, lon_step : lon_step + lon_cells, :]
                summed = summed + own_taps[kernel, lat_step, lon_step, :, None, None] * window
        outputs.append(summed.astype(jnp.bfloat16))
    return jnp.stack(outputs)


def kernel_backward(extended, near_taps, lat_rows, lon_cells):
    tap_count = near_taps.shape[2]
    summed = jnp.zeros((lat_rows, lon_cells, extended.shape[-1]), jnp.float32)
    for kernel in range(near_taps.shape[0]):
        source = extended[kernel].astype(jnp.float32)
        for lat_step in range(3):
            row_first = 2 - lat_step
            for lon_step in range(tap_count):
                col_first = tap_count - 1 - lon_step
                window = source[
                    row_first : row_first + lat_rows, col_first : col_first + lon_cells, :
                ]
                summed = (
                    summed
                    + near_taps[
                        kernel, lat_step, lon_step, row_first : row_first + lat_rows, None, None
                    ]
                    * window
                )
    return summed


def local(
    field,
    cotangent,
    kernel_weights,
    spectral_weight,
    out_weight,
    degree_gain,
    kernel_basis,
    lon_reach,
):
    lat_rows, lon_cells, channels = field.shape
    lat_parts = lax.axis_size("lat")
    lon_parts = lax.axis_size("lon")
    lat_index = lax.axis_index("lat")
    lon_index = lax.axis_index("lon")
    lat_count = lat_rows * lat_parts
    lon_count = lon_cells * lon_parts
    chan_slice = channels // lon_parts
    degree_count = degree_gain.shape[0]
    lon_span = kernel_basis.shape[2] // 2
    tap_weights = tap_table(kernel_basis, lon_reach)
    padded_taps = jnp.pad(tap_weights, ((0, 0), (0, 0), (0, 0), (1, 1)))
    near_taps = lax.dynamic_slice_in_dim(padded_taps, lat_index * lat_rows, lat_rows + 2, 3)
    own_taps = near_taps[:, :, :, 1 : lat_rows + 1]
    table_values = fourier_table(lon_count, ORDERS)
    orders_all = jnp.arange(2 * ORDERS, dtype=jnp.int32) % ORDERS
    mode_weight = jnp.where(orders_all == 0, 1.0, 2.0).astype(jnp.float32)
    own_rows = lat_index * lat_rows + jnp.arange(lat_rows, dtype=jnp.int32)
    own_colat = colatitudes(own_rows, lat_count)
    own_quad = quadrature(own_colat, lat_count, lon_count)
    gain_cols = lax.dynamic_slice_in_dim(degree_gain, lon_index * chan_slice, chan_slice, 1)
    share_rows = degree_count // lat_parts
    row_offset = lat_index * share_rows
    own_table = legendre_table(own_colat, orders_all, degree_count)
    gain_rows = lax.dynamic_slice_in_dim(gain_cols, row_offset, share_rows, 0)

    def spectral_core(inputs, weighted):
        table_rows = own_table
        band_sums = lax.psum_scatter(
            jnp.einsum("lag,cag->lcg", table_rows, inputs, precision=lax.Precision.HIGHEST).astype(
                jnp.bfloat16
            ),
            "lat",
            scatter_dimension=0,
            tiled=True,
        ).astype(jnp.float32)
        filtered = (gain_rows[:, :, None] * band_sums).astype(jnp.bfloat16)
        table_rows = own_table
        synthesized = jnp.einsum(
            "lag,lcg->cag",
            table_rows,
            lax.all_gather(filtered, "lat", axis=0, tiled=True).astype(jnp.float32),
            precision=lax.Precision.HIGHEST,
        )
        if weighted:
            synthesized = own_quad[None, :, None] * synthesized
        return (band_sums, synthesized.astype(jnp.bfloat16))

    def to_modes(grid):
        columns = lax.all_to_all(grid, "lon", split_axis=2, concat_axis=1, tiled=True)
        return jnp.einsum("ajc,jq->caq", columns, table_values, preferred_element_type=jnp.float32)

    def to_grid(coeffs):
        grid_cols = jnp.einsum(
            "caq,jq->ajc", coeffs, table_values, preferred_element_type=jnp.float32
        ).astype(jnp.bfloat16)
        return lax.all_to_all(grid_cols, "lon", split_axis=1, concat_axis=2, tiled=True)

    extended = widen(field[None], lon_span)
    kernel_out = kernel_forward(extended, own_taps, lat_rows, lon_cells)
    kernel_mix = jnp.einsum(
        "kajc,kcd->ajd", kernel_out, kernel_weights, preferred_element_type=jnp.float32
    )
    field_rows = field.reshape(-1, channels)
    mixed_in = (
        jnp.dot(field_rows, spectral_weight, preferred_element_type=jnp.float32)
        .astype(jnp.bfloat16)
        .reshape(field.shape)
    )
    forward_modes = to_modes(mixed_in)
    forward_sums, synth_rows = spectral_core(own_quad[None, :, None] * forward_modes, False)
    spectral_out = to_grid(synth_rows * mode_weight.astype(jnp.bfloat16)[None, None, :])
    pre_act = kernel_mix + spectral_out.astype(jnp.float32)
    hidden = gelu_value(pre_act).astype(jnp.bfloat16)
    hidden_rows = hidden.reshape(-1, channels)
    output_field = (
        (
            field_rows.astype(jnp.float32)
            + jnp.dot(hidden_rows, out_weight, preferred_element_type=jnp.float32)
        )
        .astype(jnp.bfloat16)
        .reshape(field.shape)
    )
    cotangent_rows = cotangent.reshape(-1, channels)
    grad_hidden = jnp.dot(cotangent_rows, out_weight.T, preferred_element_type=jnp.float32).astype(
        jnp.bfloat16
    )
    grad_pre_rows = (
        grad_hidden.astype(jnp.float32) * gelu_slope(pre_act.reshape(-1, channels))
    ).astype(jnp.bfloat16)
    grad_out_w = jnp.dot(hidden_rows.T, cotangent_rows, preferred_element_type=jnp.float32)
    grad_pre = grad_pre_rows.reshape(field.shape)
    grad_modes = mode_weight[None, None, :] * to_modes(grad_pre)
    grad_sums, grad_synth = spectral_core(grad_modes, True)
    gain_part = jnp.sum(forward_sums * grad_sums, axis=2)
    grad_mixed = to_grid(grad_synth).reshape(-1, channels)
    grad_mix_w = jnp.dot(field_rows.T, grad_mixed, preferred_element_type=jnp.float32)
    grad_kernel = jnp.einsum(
        "ajd,kcd->kajc", grad_pre, kernel_weights, preferred_element_type=jnp.float32
    ).astype(jnp.bfloat16)
    grad_kernel_w = jnp.einsum(
        "kajc,ajd->kcd", kernel_out, grad_pre, preferred_element_type=jnp.float32
    )
    extended_grad = widen(grad_kernel, lon_span)
    adjoint = kernel_backward(extended_grad, near_taps, lat_rows, lon_cells).reshape(-1, channels)
    grad_field = (
        (
            cotangent_rows.astype(jnp.float32)
            + adjoint
            + jnp.dot(grad_mixed, spectral_weight.T, preferred_element_type=jnp.float32)
        )
        .astype(jnp.bfloat16)
        .reshape(field.shape)
    )
    stacked = jnp.concatenate([grad_kernel_w, grad_mix_w[None], grad_out_w[None]], axis=0)
    gain_place = lax.dynamic_update_slice(
        jnp.zeros((degree_count, channels), jnp.float32),
        gain_part,
        (row_offset, lon_index * chan_slice),
    )
    weight_total, gain_total = lax.psum((stacked, gain_place), ("lat", "lon"))
    weight_grads = weight_total / math.sqrt(lat_count * lon_count)
    return (output_field, grad_field, weight_grads, gain_total)


def solution(mesh):
    placed = (P("lat", "lon", None), P("lat", "lon", None), P(), P(), P(), P(), P(), P())
    return jax.shard_map(
        local,
        mesh=mesh,
        in_specs=placed,
        out_specs=(P("lat", "lon", None), P("lat", "lon", None), P(), P()),
        check_vma=False,
    )
```

profile of v0, /device:TPU:1, one launch (start us, length us, event | category | flops | bytes accessed | tf_op | source)
XLA Modules:
  0.0 1371.6 jit_solution(5922243071911205965)
XLA Ops:
  15.1 3.6 reshape.679
  18.7 4.2 copy.85
  22.9 6.0 all-to-all-start
  29.6 386.3 %while.20 = (s32[]{:T(128)}, f32[24,384]{1,0:T(8,128)S(1)}, f32[24,384]{1,0:T(8,128)S(1)}, f32[1,384]{1,0:T(1,128)S(1)}, f32[192,24,384]{2,1,0:T(8,128)}, /*inde...) while((s32[]{:T(128)}, f32[24,384]{1,0:T(8,128)S(1)}, ...), condition=%wide.region_1.2_spmd.clone.clone, body=%wide.region_0.1_spmd.clone.clone.sunk | while | flops 102248 | bytes 202636 | solution.py:62
  415.9 9.6 copy.89
  428.5 3.6 all_to_all.47
  432.1 5.4 fusion.126
  437.7 3.4 copy.88
  441.0 20.1 %convert_bitcast_fusion.1 = bf16[192,48,384]{0,1,2:T(8,128)(2,1)} fusion(f32[48,24,384]{0,1,2:T(8,128)} %copy.88, f32[192,24,384]{0,1,2:T(8,128)} %copy.89), kind=kOutput, calls=%fused_computation.19 | convolution fusion | flops 1022754816 | bytes 15925248 | tf_op jit(solution)/shard_map/lag,cag->lcg/dot_general | solution.py:180
  461.1 13.5 copy.90
  475.7 82.8 %reduce-scatter.3.cloned.1.call-done = bf16[12,48,384]{2,1,0:T(8,128)(2,1)} async-done(((bf16[192,48,384]{2,1,0:T(8,128)(2,1)}), bf16[12,48,384]{2,1,0:T(8,128)(2,1)}) %reduce-scatter.3.cloned.1.call-update) | async-done | bytes 442384 | tf_op jit(solution)/shard_map/reduce_scatter | solution.py:179
  571.5 3.7 reshape.682
  579.6 3.8 collective-permute-done.2
  586.6 5.0 fusion.94
  591.6 41.8 %fusion.110 = bf16[1,24,90,384]{3,1,2,0:T(8,128)(2,1)} fusion(f32[26,96,384]{2,0,1:T(8,128)} %fusion.94, f32[24]{0:T(128)S(1)} %get-tuple-element.350, f32[24]{0:T(128)S(1)} %get-tuple-element.322, f32[24]{0:T(128)S(1)} %get-tuple-element.319, f32[24]{0:T(128)S(1)} %get-tuple-element.318, f32[24]{0:T(128)S(1)} %get-tuple-element.317, ...), kind=kLoop, calls=%fused_computation.202 | loop fusion | flops 34836480 | bytes 71333856 | tf_op jit(solution)/shard_map/stack | solution.py:116
  633.6 41.9 %fusion.108 = bf16[1,24,90,384]{3,1,2,0:T(8,128)(2,1)} fusion(f32[26,96,384]{2,0,1:T(8,128)} %fusion.94, f32[24]{0:T(128)S(1)} %get-tuple-element.271, f32[24]{0:T(128)S(1)} %get-tuple-element.270, f32[24]{0:T(128)S(1)} %get-tuple-element.269, f32[24]{0:T(128)S(1)} %get-tuple-element.268, f32[24]{0:T(128)S(1)} %get-tuple-element.267, ...), kind=kLoop, calls=%fused_computation.200 | loop fusion | flops 34836480 | bytes 71333856 | tf_op jit(solution)/shard_map/stack | solution.py:116
  675.5 25.8 %copy.91 = bf16[192,48,384]{1,0,2:T(8,128)(2,1)} copy(bf16[192,48,384]{2,1,0:T(8,128)(2,1)} %all-gather.3.cloned.1.call-done) | data formatting | bytes 14155776 | tf_op jit(solution)/shard_map/all_gather | solution.py:192
  701.3 18.8 %multiply_bitcast_fusion = bf16[48,24,384]{0,1,2:T(8,128)(2,1)S(1)} fusion(bf16[192,48,384]{1,0,2:T(8,128)(2,1)} %copy.91, f32[192,24,384]{0,1,2:T(8,128)} %copy.89, bf16[384]{0:T(512)(128)(2,1)S(1)} %fusion.148), kind=kOutput, calls=%fused_computation.191 | convolution fusion | flops 1020100608 | bytes 15041280 | tf_op jit(solution)/shard_map/lag,lcg->cag/dot_general | solution.py:189
  720.1 6.6 convert_bitcast_fusion.4
  726.8 6.0 copy.94
  732.8 9.8 reshape.709
  742.6 6.0 all-to-all-start.1
  748.6 42.3 %fusion.109 = bf16[1,24,90,384]{3,1,2,0:T(8,128)(2,1)} fusion(f32[26,96,384]{2,0,1:T(8,128)} %fusion.94, f32[24]{0:T(128)S(1)} %get-tuple-element.303, f32[24]{0:T(128)S(1)} %get-tuple-element.302, f32[24]{0:T(128)S(1)} %get-tuple-element.310, f32[24]{0:T(128)S(1)} %get-tuple-element.301, f32[24]{0:T(128)S(1)} %get-tuple-element.300, ...), kind=kLoop, calls=%fused_computation.201 | loop fusion | flops 34836480 | bytes 71333856 | tf_op jit(solution)/shard_map/stack | solution.py:116
  790.8 5.3 pad_maximum_fusion.1
  796.2 7.2 reshape.710
  803.4 7.0 copy.95
  810.4 5.7 copy.96
  816.1 9.8 fusion.22
  825.9 4.8 reshape.683
  830.7 5.2 fusion.16
  835.9 3.6 reshape.684
  839.5 4.2 copy.102
  843.7 34.3 %all_to_all.60 = bf16[24,90,384]{1,0,2:T(8,128)(2,1)S(1)} all-to-all(bf16[24,90,384]{1,0,2:T(8,128)(2,1)} %copy.102), channel_id=1, replica_groups=mesh['lat'=16,'lon'=8] {'lon'}, dimensions={2} | all-to-all | bytes 3317760 | tf_op jit(solution)/shard_map/all_to_all | solution.py:200
  880.9 4.6 all_to_all.52
  885.5 6.9 fusion.127
  893.7 4.6 copy.105
  898.4 19.9 %convert_bitcast_fusion = bf16[192,48,384]{0,1,2:T(8,128)(2,1)} fusion(f32[48,24,384]{0,1,2:T(8,128)} %copy.105, f32[192,24,384]{0,1,2:T(8,128)} %copy.89), kind=kOutput, calls=%fused_computation.18 | convolution fusion | flops 1022754816 | bytes 15925248 | tf_op jit(solution)/shard_map/lag,cag->lcg/dot_general | solution.py:180
  918.3 13.5 copy.107
  931.9 81.7 %reduce-scatter.5.cloned.1.call-done = bf16[12,48,384]{2,1,0:T(8,128)(2,1)} async-done(((bf16[192,48,384]{2,1,0:T(8,128)(2,1)}), bf16[12,48,384]{2,1,0:T(8,128)(2,1)}) %reduce-scatter.5.cloned.1.call-update) | async-done | bytes 442384 | tf_op jit(solution)/shard_map/reduce_scatter | solution.py:179
  1018.2 4.7 convert_bitcast_fusion.2
  1028.0 3.6 reshape.680
  1034.5 6.3 fusion.111
  1043.3 3.6 reshape.681
  1050.1 4.2 pad_maximum_fusion.5
  1054.3 3.7 collective-permute-start.6
  1059.5 29.9 %all-gather.5.cloned.1.call-done = bf16[192,48,384]{2,1,0:T(8,128)(2,1)} async-done(((bf16[12,48,384]{2,1,0:T(8,128)(2,1)}), bf16[192,48,384]{2,1,0:T(8,128)(2,1)}) %all-gather.5.cloned.1.call-update) | async-done | bytes 7077904 | tf_op jit(solution)/shard_map/all_gather | solution.py:192
  1089.3 26.0 %copy.108 = bf16[192,48,384]{1,0,2:T(8,128)(2,1)} copy(bf16[192,48,384]{2,1,0:T(8,128)(2,1)} %all-gather.5.cloned.1.call-done) | data formatting | bytes 14155776 | tf_op jit(solution)/shard_map/all_gather | solution.py:192
  1115.3 18.7 %fusion.90 = bf16[48,24,384]{0,1,2:T(8,128)(2,1)S(1)} fusion(f32[24]{0:T(128)S(1)} %copy-done.23, bf16[192,48,384]{1,0,2:T(8,128)(2,1)} %copy.108, f32[192,24,384]{0,1,2:T(8,128)} %copy.89), kind=kOutput, calls=%fused_computation.178 | convolution fusion | flops 1020100608 | bytes 15040608 | tf_op jit(solution)/shard_map/lag,lcg->cag/dot_general | solution.py:189
  1134.0 6.6 convert_bitcast_fusion.3
  1140.6 5.9 copy.111
  1146.5 10.0 reshape.711
  1156.6 5.0 all-to-all-start.3
  1161.5 9.7 pad_maximum_fusion
  1171.2 5.7 fusion.93
  1177.9 5.4 all-to-all-done.3
  1183.3 9.0 reshape.712
  1192.3 6.5 copy.112
  1198.8 4.6 reshape.686
  1208.7 112.1 %fusion.28 = f32[24,90,384]{2,0,1:T(8,128)} fusion(f32[26,96,384]{2,0,1:T(8,128)} %get-tuple-element.242, f32[26,96,384]{2,0,1:T(8,128)} %get-tuple-element.243, f32[26,96,384]{2,0,1:T(8,128)} %get-tuple-element.241, f32[24]{0:T(128)S(1)} %get-tuple-element.337, f32[24]{0:T(128)S(1)} %get-tuple-element.338, f32[24]{0:T(128)S(1)} %get-tuple-element.339, ...), kind=kLoop, calls=%fused_computation.50 | loop fusion | flops 103680000 | bytes 212342688 | tf_op jit(solution)/shard_map/add | solution.py:132
  1320.8 4.4 copy.101
  1325.1 4.8 reshape.685
  1330.0 5.0 fusion.13
  1339.2 21.0 %all-reduce.4.cloned.1.call-done = (f32[5,384,384]{2,1,0:T(8,128)}, f32[192,384]{1,0:T(8,128)}) async-done(((f32[5,384,384]{2,1,0:T(8,128)}, f32[192,384]{1,0:T(8,128)}), (f32[5,384,384]{2,1,0:T(8,128)}, f32[192,384]{1,0:T(8,128)})) %all-reduce.4.cloned.1.call-update) | async-done | bytes 3244048 | tf_op jit(solution)/shard_map/psum | solution.py:271
  1360.2 3.7 broadcast_multiply_fusion
  (1571 shorter events, 341.4 us)
Async XLA Ops:
  7.2 808.9 %copy-start = (bf16[3,384,384]{2,1,0:T(8,128)(2,1)S(1)}, bf16[3,384,384]{2,1,0:T(8,128)(2,1)}, u32[]{:S(2)}) copy-start(bf16[3,384,384]{2,1,0:T(8,128)(2,1)} %param.12) | copy-start | bytes 2654212
  7.2 5.4 copy-start.15
  12.6 6.1 copy-start.2
  22.9 402.6 %all-to-all-start = ((bf16[24,90,384]{1,0,2:T(8,128)(2,1)}), bf16[24,90,384]{1,0,2:T(8,128)(2,1)S(1)}, u32[]{:S(2)}, u32[]{:S(2)}) async-start(bf16[24,90,384]{1,0,2:T(8,128)(2,1)} %copy.85), calls=%async_computation | async-start | bytes 4718592 | tf_op jit(solution)/shard_map/all_to_all | solution.py:200
  28.9 529.7 %reduce-scatter.3.cloned.1.call-start = ((), (), s32[]{:S(2)}) async-start(), calls=%async_computation.6 | async-start | bytes 7520256 | tf_op jit(solution)/shard_map/reduce_scatter | solution.py:179
  29.6 407.9 %copy-start.22 = (f32[24]{0:T(128)}, f32[24]{0:T(128)S(1)}, u32[]{:S(2)}) copy-start(f32[24]{0:T(128)S(1)} %get-tuple-element.365) | copy-start | bytes 292
  474.7 85.8 %copy-start.5 = (bf16[24,90,384]{2,0,1:T(8,128)(2,1)S(1)}, bf16[24,90,384]{2,0,1:T(8,128)(2,1)}, u32[]{:S(2)}) copy-start(bf16[24,90,384]{2,0,1:T(8,128)(2,1)} %param.10) | copy-start | bytes 4976644
  474.7 88.8 %copy-start.21 = (s32[3,384]{1,0:T(4,128)S(1)}, s32[3,384]{1,0:T(4,128)}, u32[]{:S(2)}) copy-start(s32[3,384]{1,0:T(4,128)} %param.17) | copy-start | bytes 13828
  474.7 88.8 %copy-start.20 = (f32[3,3,7,384]{3,2,1,0:T(8,128)S(1)}, f32[3,3,7,384]{3,2,1,0:T(8,128)}, u32[]{:S(2)}) copy-start(f32[3,3,7,384]{3,2,1,0:T(8,128)} %param.16) | copy-start | bytes 290308
  474.7 200.8 %all-gather.3.cloned.1.call-start = ((), (), s32[]{:S(2)}) async-start(), calls=%async_computation.7 | async-start | bytes 7520256 | tf_op jit(solution)/shard_map/all_gather | solution.py:192
  560.5 14.7 %collective-permute-start = (bf16[1,24,3,384]{3,1,2,0:T(8,128)(2,1)S(1)}, bf16[1,24,3,384]{3,1,2,0:T(8,128)(2,1)S(1)}, u32[]{:S(2)}, u32[]{:S(2)}) collective-permute-start(bf16[1,24,3,384]{3,1,2,0:T(8,128)(2,1)S(1)} %get-tuple-element.250), channel_id=1, source_target_pairs={{0,1},{1,2},{2,3},{3,4},{4,5},{5,6},{6,7},{7,0},{8,9},{9,10},{10,1... | collective-permute-start | bytes 165896 | tf_op jit(solution)/shard_map/ppermute | solution.py:19
  563.4 11.8 collective-permute-start.1
  564.3 27.3 %copy-start.24 = (f32[24]{0:T(128)}, f32[24]{0:T(128)S(1)}, u32[]{:S(2)}) copy-start(f32[24]{0:T(128)S(1)} %get-tuple-element.321) | copy-start | bytes 292
  564.9 26.7 %copy-start.26 = (f32[24]{0:T(128)}, f32[24]{0:T(128)S(1)}, u32[]{:S(2)}) copy-start(f32[24]{0:T(128)S(1)} %get-tuple-element.307) | copy-start | bytes 292
  564.9 26.7 %copy-start.28 = (f32[24]{0:T(128)}, f32[24]{0:T(128)S(1)}, u32[]{:S(2)}) copy-start(f32[24]{0:T(128)S(1)} %get-tuple-element.308) | copy-start | bytes 292
  565.5 26.1 %copy-start.30 = (f32[24]{0:T(128)}, f32[24]{0:T(128)S(1)}, u32[]{:S(2)}) copy-start(f32[24]{0:T(128)S(1)} %get-tuple-element.311) | copy-start | bytes 292
  565.5 26.2 %copy-start.32 = (f32[24]{0:T(128)}, f32[24]{0:T(128)S(1)}, u32[]{:S(2)}) copy-start(f32[24]{0:T(128)S(1)} %get-tuple-element.312) | copy-start | bytes 292
  565.5 26.2 %copy-start.34 = (f32[24]{0:T(128)}, f32[24]{0:T(128)S(1)}, u32[]{:S(2)}) copy-start(f32[24]{0:T(128)S(1)} %get-tuple-element.313) | copy-start | bytes 292
  565.5 26.2 %copy-start.36 = (f32[24]{0:T(128)}, f32[24]{0:T(128)S(1)}, u32[]{:S(2)}) copy-start(f32[24]{0:T(128)S(1)} %get-tuple-element.314) | copy-start | bytes 292
  566.7 66.8 %copy-start.38 = (f32[24]{0:T(128)}, f32[24]{0:T(128)S(1)}, u32[]{:S(2)}) copy-start(f32[24]{0:T(128)S(1)} %get-tuple-element.262) | copy-start | bytes 292
  566.7 66.8 %copy-start.40 = (f32[24]{0:T(128)}, f32[24]{0:T(128)S(1)}, u32[]{:S(2)}) copy-start(f32[24]{0:T(128)S(1)} %get-tuple-element.263) | copy-start | bytes 292
  566.7 66.8 %copy-start.42 = (f32[24]{0:T(128)}, f32[24]{0:T(128)S(1)}, u32[]{:S(2)}) copy-start(f32[24]{0:T(128)S(1)} %get-tuple-element.264) | copy-start | bytes 292
  567.4 66.2 %copy-start.44 = (f32[24]{0:T(128)}, f32[24]{0:T(128)S(1)}, u32[]{:S(2)}) copy-start(f32[24]{0:T(128)S(1)} %get-tuple-element.277) | copy-start | bytes 292
  567.4 66.2 %copy-start.46 = (f32[24]{0:T(128)}, f32[24]{0:T(128)S(1)}, u32[]{:S(2)}) copy-start(f32[24]{0:T(128)S(1)} %get-tuple-element.278) | copy-start | bytes 292
  567.4 66.2 %copy-start.48 = (f32[24]{0:T(128)}, f32[24]{0:T(128)S(1)}, u32[]{:S(2)}) copy-start(f32[24]{0:T(128)S(1)} %get-tuple-element.279) | copy-start | bytes 292
  567.4 66.2 %copy-start.50 = (f32[24]{0:T(128)}, f32[24]{0:T(128)S(1)}, u32[]{:S(2)}) copy-start(f32[24]{0:T(128)S(1)} %get-tuple-element.280) | copy-start | bytes 292
  575.5 7.9 collective-permute-start.2
  578.3 8.3 collective-permute-start.3
  742.6 53.6 %all-to-all-start.1 = ((bf16[8,2,51840]{2,1,0:T(2,128)(2,1)}), bf16[8,2,51840]{2,1,0:T(2,128)(2,1)S(1)}, u32[]{:S(2)}, u32[]{:S(2)}) async-start(bf16[8,2,51840]{2,1,0:T(2,128)(2,1)} %reshape.709), calls=%async_computation.2 | async-start | bytes 3317760 | tf_op jit(solution)/shard_map/all_to_all | solution.py:207
  748.6 265.1 %reduce-scatter.5.cloned.1.call-start = ((), (), s32[]{:S(2)}) async-start(), calls=%async_computation.8 | async-start | bytes 7520256 | tf_op jit(solution)/shard_map/reduce_scatter | solution.py:179
  825.8 4.8 copy-start.8
  825.8 4.8 copy-start.18
  885.5 6.9 copy-start.52
  931.8 81.8 %copy-start.14 = (bf16[12,48,384]{2,1,0:T(8,128)(2,1)S(1)}, bf16[12,48,384]{2,1,0:T(8,128)(2,1)}, u32[]{:S(2)}) copy-start(bf16[12,48,384]{2,1,0:T(8,128)(2,1)} %reduce-scatter.3.cloned.1.call-done) | copy-start | bytes 1327108
  931.8 84.1 %copy-start.9 = (bf16[2160,384]{1,0:T(8,128)(2,1)S(1)}, bf16[2160,384]{1,0:T(8,128)(2,1)}, u32[]{:S(2)}) copy-start(bf16[2160,384]{1,0:T(8,128)(2,1)} %fusion.16) | copy-start | bytes 4976644
  931.9 157.5 %all-gather.5.cloned.1.call-start = ((), (), s32[]{:S(2)}) async-start(), calls=%async_computation.9 | async-start | bytes 7520256 | tf_op jit(solution)/shard_map/all_gather | solution.py:192
  1022.9 2.2 copy-start.4
  1025.1 6.6 copy-start.6
  1025.1 25.0 %collective-permute-start.4 = (bf16[3,24,3,384]{3,1,0,2:T(8,128)(2,1)S(1)}, bf16[3,24,3,384]{3,1,0,2:T(8,128)(2,1)S(1)}, u32[]{:S(2)}, u32[]{:S(2)}) collective-permute-start(bf16[3,24,3,384]{3,1,0,2:T(8,128)(2,1)S(1)} %get-tuple-element.246), channel_id=1, source_target_pairs={{0,1},{1,2},{2,3},{3,4},{4,5},{5,6},{6,7},{7,0},{8,9},{9,10},{10,1... | collective-permute-start | bytes 497672 | tf_op jit(solution)/shard_map/ppermute | solution.py:19
  1028.0 22.1 %collective-permute-start.5 = (bf16[3,24,3,384]{3,1,0,2:T(8,128)(2,1)S(1)}, bf16[3,24,3,384]{3,1,0,2:T(8,128)(2,1)S(1)}, u32[]{:S(2)}, u32[]{:S(2)}) collective-permute-start(bf16[3,24,3,384]{3,1,0,2:T(8,128)(2,1)S(1)} %get-tuple-element.247), channel_id=1, source_target_pairs={{1,0},{2,1},{3,2},{4,3},{5,4},{6,5},{7,6},{0,7},{9,8},{10,9},{11,1... | collective-permute-start | bytes 497672 | tf_op jit(solution)/shard_map/ppermute | solution.py:21
  1031.6 2.8 copy-start.11
  1031.6 2.8 copy-start.12
  1034.4 6.4 copy-start.3
  1034.4 6.4 copy-start.10
  1054.3 107.2 %collective-permute-start.6 = (bf16[3,1,96,384]{3,1,0,2:T(2,128)(2,1)}, bf16[3,1,96,384]{3,1,0,2:T(2,128)(2,1)}, u32[]{:S(2)}, u32[]{:S(2)}) collective-permute-start(bf16[3,1,96,384]{3,1,0,2:T(2,128)(2,1)} %get-tuple-element.244), channel_id=1, source_target_pairs={{0,8},{8,16},{16,24},{24,32},{32,40},{40,48},{48,56},{56,64},{64,7... | collective-permute-start | bytes 663560 | tf_op jit(solution)/shard_map/ppermute | solution.py:19
  1058.0 57.2 %copy-start.23 = (f32[24]{0:T(128)S(1)}, f32[24]{0:T(128)}, u32[]{:S(2)}) copy-start(f32[24]{0:T(128)} %copy-done.22) | copy-start | bytes 292
  1058.0 103.5 %collective-permute-start.7 = (bf16[3,1,96,384]{3,1,0,2:T(2,128)(2,1)S(1)}, bf16[3,1,96,384]{3,1,0,2:T(2,128)(2,1)}, u32[]{:S(2)}, u32[]{:S(2)}) collective-permute-start(bf16[3,1,96,384]{3,1,0,2:T(2,128)(2,1)S(1)} %get-tuple-element.245), channel_id=1, source_target_pairs={{8,0},{16,8},{24,16},{32,24},{40,32},{48,40},{56,48},{64,56},{72,6... | collective-permute-start | bytes 663560 | tf_op jit(solution)/shard_map/ppermute | solution.py:21
  1156.6 26.7 %all-to-all-start.3 = ((bf16[8,2,51840]{2,1,0:T(2,128)(2,1)}), bf16[8,2,51840]{2,1,0:T(2,128)(2,1)}, u32[]{:S(2)}, u32[]{:S(2)}) async-start(bf16[8,2,51840]{2,1,0:T(2,128)(2,1)} %reshape.711), calls=%async_computation.5 | async-start | bytes 3317760 | tf_op jit(solution)/shard_map/all_to_all | solution.py:207
  1161.5 198.6 %all-reduce.4.cloned.1.call-start = ((), (), s32[]{:S(2)}) async-start(), calls=%async_computation.10 | async-start | bytes 6488064 | tf_op jit(solution)/shard_map/psum | solution.py:271
  1177.9 20.9 %copy-start.17 = (f32[192,384]{1,0:T(8,128)}, f32[192,384]{1,0:T(8,128)S(1)}, u32[]{:S(2)}) copy-start(f32[192,384]{1,0:T(8,128)S(1)} %dynamic_update_slice.10) | copy-start | bytes 884740
  1203.4 2.7 copy-start.13
  1206.1 2.2 copy-start.25
  1206.1 2.2 copy-start.27
  1206.1 2.2 copy-start.29
  1206.1 2.2 copy-start.31
  1206.2 2.2 copy-start.33
  1206.2 2.2 copy-start.35
  1206.2 2.2 copy-start.37
  1206.2 2.2 copy-start.39
  1206.2 2.2 copy-start.41
  1325.1 4.8 copy-start.7
  1325.1 4.8 copy-start.16
  1337.4 27.2 %copy-start.1 = (bf16[3,384,384]{2,1,0:T(8,128)(2,1)S(1)}, bf16[3,384,384]{2,1,0:T(8,128)(2,1)}, u32[]{:S(2)}) copy-start(bf16[3,384,384]{2,1,0:T(8,128)(2,1)} %param.12) | copy-start | bytes 2654212
  1360.1 3.7 copy-start.19
  (28 other events, 61.2 us)
Sparse Core Ops, SparseCore 0:
  474.8 83.6 reduce-scatter.2
  561.6 68.4 all-gather.2
  932.0 81.6 reduce-scatter.4
  1015.8 73.4 all-gather.4
  1208.4 151.6 all-reduce.3
where the time goes:
time: 1390 us; the launch traced here: 1370 us
  other arithmetic  443 us (32%)
  local copies, waits for them, and re-layouts  362 us (26%)
  waiting for transfers between devices  228 us (16%)
  matrix products  144 us (10%)
  loops' own time  113 us (8%)
  blocking collectives  34.3 us (2%)
  starting transfers between devices  32 us (2%)
  between operations  15.3 us (1%)
    reduce_scatter x2, waiting for transfers between devices, spectral_core(): lax.psum_scatter(jnp.einsum('lag,cag->lcg', table_rows, inputs, precision...  165 us
    dynamic_update_slice x192, other arithmetic, legendre_table(): lax.scan(advance, initial, jnp.arange(degree_count, dtype=jnp.int32))  135 us
    another operation x4, other arithmetic, kernel_forward(): return jnp.stack(outputs)  131 us
    another operation x1, loops' own time, legendre_table(): lax.scan(advance, initial, jnp.arange(degree_count, dtype=jnp.int32))  113 us
    add x1, other arithmetic, kernel_backward(): summed + near_taps[kernel, lat_step, lon_step, row_first:row_first + lat_...  112 us
    dynamic_slice x192, local copies, waits for them, and re-layouts, legendre_table(): lax.scan(advance, initial, jnp.arange(degree_count, dtype=jnp.int32))  110 us
    all_gather x2, local copies, waits for them, and re-layouts, spectral_core(): lax.all_gather(filtered, 'lat', axis=0, tiled=True).astype(jnp.float32)  51.8 us
    unnamed x161, local copies, waits for them, and re-layouts  50.1 us
  transfers between devices with their start and end apart: 16, of which 7 were waited for; matrix products, arithmetic and copies ran while one was open for 50% of the time, Pallas kernels for 0%

commit v1 on v0

v1 whole, which is shorter than its diff:
```python
import functools
import math

import jax
import jax.numpy as jnp
from jax import lax
from jax.experimental import pallas as pl
from jax.experimental.pallas import tpu as pltpu
from jax.sharding import PartitionSpec as P

ORDERS = 192
BF = jnp.bfloat16
F32 = jnp.float32
VMEM = pl.BlockSpec(memory_space=pltpu.VMEM)
ROWS = 96
EXT = 128


def dot(a, b, dims=((1,), (0,))):
    return lax.dot_general(a, b, (dims, ((), ())), preferred_element_type=F32)


def ring(x, axis, step, closed):
    n = lax.axis_size(axis)
    pairs = [(i, (i + step) % n) for i in range(n)]
    if not closed:
        pairs = [(a, b) for a, b in pairs if b - a == step]
    return lax.ppermute(x, axis, pairs)


def extend(x):
    rows, cells, chans = x.shape
    left = ring(x[:, cells - 3 :], "lon", 1, True)
    right = ring(x[:, :3], "lon", -1, True)
    gap = jnp.zeros((rows, EXT - cells - 6, chans), x.dtype)
    wide = jnp.concatenate([x, right, gap, left], axis=1)
    above = ring(wide[rows - 1 :], "lat", 1, False)
    below = ring(wide[:1], "lat", -1, False)
    return jnp.concatenate([above, wide, below], axis=0)


def tap_rows(taps):
    k, r, t, n = taps.shape
    flat = jnp.transpose(taps, (3, 0, 1, 2)).reshape(n, k * r, t)
    wide = jnp.concatenate([flat[:, :, 3:], jnp.zeros((n, k * r, EXT - t), F32), flat[:, :, :3]], axis=2)
    return jnp.pad(wide, ((0, 0), (0, 16 - k * r), (0, 0)))


def band_matrix(taps_ref, i, band_ref, cells):
    keep = lax.broadcasted_iota(jnp.int32, (ROWS, EXT), 0) < cells
    rows = taps_ref[i]
    for k in range(3):
        for r in range(3):
            row = jnp.broadcast_to(rows[3 * k + r : 3 * k + r + 1], (ROWS, EXT))
            block = pltpu.roll(row, 0, 1, stride=1, stride_axis=0)
            band_ref[k * ROWS : (k + 1) * ROWS, r * EXT : (r + 1) * EXT] = jnp.where(keep, block, 0.0).astype(BF)


def stencil_forward(cells, ext_ref, taps_ref, w_ref, out_ref, band_ref):
    def step(i, carry):
        band_matrix(taps_ref, i, band_ref, cells)
        source = ext_ref[pl.ds(i, 3)].reshape(3 * EXT, -1)
        total = None
        for k in range(3):
            part = dot(band_ref[k * ROWS : (k + 1) * ROWS], source).astype(BF)
            part = dot(part, w_ref[k])
            total = part if total is None else total + part
        out_ref[i] = total
        return carry

    lax.fori_loop(0, out_ref.shape[0], step, 0)


def stencil_backward(cells, ext_ref, taps_ref, wt_ref, field_ref, adj_ref, grad_ref, band_ref, part_ref):
    grad_ref[...] = jnp.zeros_like(grad_ref)
    group = 4

    def outer(o, carry):
        def step(a, inner):
            i = o * group + a
            band_matrix(taps_ref, i, band_ref, cells)
            source = ext_ref[pl.ds(i, 3)].reshape(3 * EXT, -1)
            total = None
            for k in range(3):
                part = dot(band_ref[k * ROWS : (k + 1) * ROWS], source).astype(BF)
                part_ref[k, a] = part
                part = dot(part, wt_ref[k])
                total = part if total is None else total + part
            adj_ref[i] = total
            return inner

        lax.fori_loop(0, group, step, 0)
        rows = field_ref[pl.ds(o * group, group)].reshape(group * ROWS, -1)
        for k in range(3):
            grad_ref[k] += dot(rows, part_ref[k].reshape(group * ROWS, -1), ((0,), (0,)))
        return carry

    lax.fori_loop(0, adj_ref.shape[0] // group, outer, 0)


def pointwise(cells, km_ref, so_ref, f_ref, ct_ref, w_ref, wt_ref, out_ref, gp_ref, gow_ref):
    @pl.when(pl.program_id(0) == 0)
    def _():
        gow_ref[...] = jnp.zeros_like(gow_ref)

    group, rows, chans = km_ref.shape
    flat = (group * rows, chans)
    v = (km_ref[...] + so_ref[...].astype(F32)).reshape(flat)
    ct = ct_ref[...].reshape(flat)
    square = v * v
    s = jnp.tanh(0.7978845608 * v * (1.0 + 0.044715 * square))
    half = 0.5 * (1.0 + s)
    hidden = (v * half).astype(BF)
    slope = half + 0.5 * v * (1.0 - s * s) * (0.7978845608 * (1.0 + 3.0 * 0.044715 * square))
    out = f_ref[...].astype(F32) + dot(hidden, w_ref[...]).reshape(km_ref.shape)
    out_ref[...] = out.astype(BF)[:, :cells]
    gp_ref[...] = (dot(ct, wt_ref[...]) * slope).astype(BF).reshape(km_ref.shape)
    gow_ref[...] += dot(hidden, ct, ((0,), (0,)))


def finish(cells, adj_ref, gm_ref, f_ref, ct_ref, wt_ref, out_ref, gmw_ref):
    @pl.when(pl.program_id(0) == 0)
    def _():
        gmw_ref[...] = jnp.zeros_like(gmw_ref)

    group, rows, chans = adj_ref.shape
    flat = (group * rows, chans)
    gm = gm_ref[...].reshape(flat)
    out = ct_ref[...].astype(F32) + adj_ref[...] + dot(gm, wt_ref[...]).reshape(adj_ref.shape)
    out_ref[...] = out.astype(BF)[:, :cells]
    gmw_ref[...] += dot(f_ref[...].reshape(flat), gm, ((0,), (0,)))


def legendre_kernel(m_ref, x_ref, diag_ref, out_ref):
    m = m_ref[...]
    x = x_ref[...]
    diag = diag_ref[...]
    reps = x.shape[1] // m.shape[1]

    def wide(a):
        return jnp.concatenate([a] * reps, axis=1)

    mw = wide(m)

    def step(l, carry):
        prev, before, a_prev = carry
        lf = l.astype(F32)
        above = lf > m
        den = jnp.where(above, lf * lf - m * m, 1.0)
        a = jnp.where(above, jnp.sqrt((4.0 * lf * lf - 1.0) / den), 1.0)
        cur = wide(a) * (x * prev - before * wide(1.0 / a_prev))
        cur = jnp.where(lf == mw, diag, jnp.where(lf > mw, cur, 0.0))
        out_ref[l] = cur.astype(BF)
        return cur, prev, a

    blank = x * 0.0
    lax.fori_loop(0, out_ref.shape[0], step, (blank, blank, m * 0.0 + 1.0), unroll=4)


def colatitudes(row_index, lat_count):
    return (row_index.astype(F32) + 0.5) * (math.pi / lat_count)


def legendre_rows(orders, lat_count, degrees):
    slots = 16
    m = jnp.pad(orders, (0, slots - orders.shape[0])).astype(F32)[:, None]
    colat = colatitudes(jnp.arange(lat_count, dtype=jnp.int32), lat_count)[None, :]
    log_start = 0.5 * (lax.lgamma(m + 1.5) - lax.lgamma(m + 1.0) - lax.lgamma(F32(1.5) + 0.0 * m))
    diag = jnp.exp(log_start + m * jnp.log(jnp.sin(colat))) / math.sqrt(4.0 * math.pi)
    x = jnp.broadcast_to(jnp.cos(colat), diag.shape)
    table = pl.pallas_call(
        legendre_kernel,
        out_shape=jax.ShapeDtypeStruct((degrees, slots, lat_count), BF),
        in_specs=[VMEM] * 3,
        out_specs=VMEM,
        compiler_params=pltpu.CompilerParams(vmem_limit_bytes=40 << 20),
    )(jnp.broadcast_to(m, (slots, 128)), x, diag)
    return jnp.transpose(table[:, : orders.shape[0]], (1, 0, 2))


def fourier(lon_count, orders):
    j = jnp.arange(lon_count, dtype=jnp.int32)
    angles = (j[:, None] * orders[None, :] % lon_count).astype(F32) * (2.0 * math.pi / lon_count)
    return jnp.stack([jnp.cos(angles), -jnp.sin(angles)], axis=-1).astype(BF)


def tap_table(kernel_basis, lon_reach):
    count = kernel_basis.shape[2]
    offsets = jnp.abs(jnp.arange(count, dtype=jnp.int32) - count // 2)
    mask = offsets[None, :, None] <= lon_reach[:, None, :]
    return kernel_basis * mask[None].astype(F32)


def call(body, outs, scratch, limit=56, **kw):
    return pl.pallas_call(
        body,
        out_shape=outs,
        out_specs=jax.tree.map(lambda _: VMEM, outs),
        scratch_shapes=scratch,
        compiler_params=pltpu.CompilerParams(vmem_limit_bytes=limit << 20),
        **kw,
    )


def by_rows(body, args, whole, outs, totals, group=4):
    def cut(a):
        return pl.BlockSpec((group,) + a.shape[1:], lambda g: (g, 0, 0))

    def full(a):
        return pl.BlockSpec(a.shape, lambda g: (0,) * len(a.shape))

    return pl.pallas_call(
        body,
        grid=(args[0].shape[0] // group,),
        in_specs=[cut(a) for a in args] + [full(a) for a in whole],
        out_specs=[cut(a) for a in outs] + [full(a) for a in totals],
        out_shape=list(outs) + list(totals),
        compiler_params=pltpu.CompilerParams(vmem_limit_bytes=56 << 20),
    )(*args, *whole)


def local(field, cotangent, kernel_weights, spectral_weight, out_weight, degree_gain, kernel_basis, lon_reach):
    rows, cells, chans = field.shape
    lat_parts, lon_parts = lax.axis_size("lat"), lax.axis_size("lon")
    lat, lon = lax.axis_index("lat"), lax.axis_index("lon")
    lat_count, lon_count = rows * lat_parts, cells * lon_parts
    share = chans // lon_parts
    degrees = degree_gain.shape[0]
    slots = ORDERS // lat_parts
    shape = jax.ShapeDtypeStruct

    taps = tap_table(kernel_basis, lon_reach)
    near = lax.dynamic_slice_in_dim(jnp.pad(taps, ((0, 0), (0, 0), (0, 0), (1, 1))), lat * rows, rows + 2, 3)
    own_taps = tap_rows(near[:, :, :, 1 : rows + 1])
    turned = near[:, ::-1, ::-1]
    adj_taps = tap_rows(jnp.stack([turned[:, r, :, r : r + rows] for r in range(3)], axis=1))

    all_orders = jnp.arange(ORDERS, dtype=jnp.int32).reshape(lat_parts, slots)
    my_orders = lat * slots + jnp.arange(slots, dtype=jnp.int32)
    table = legendre_rows(my_orders, lat_count, degrees)
    waves = fourier(lon_count, all_orders.reshape(-1)).reshape(lon_count, 2 * ORDERS)
    quad = 2.0 * math.pi / lon_count * (math.pi / lat_count) * jnp.sin(
        colatitudes(jnp.arange(lat_count, dtype=jnp.int32), lat_count)
    )
    quad = quad.reshape(1, lat_count, 1, 1)
    mode_weight = jnp.where(my_orders == 0, 1.0, 2.0).astype(F32)[:, None, None, None]
    gain = lax.dynamic_slice_in_dim(degree_gain, lon * share, share, 1)[None, :, None, :]

    def spectral(grid, scale_in, scale_out):
        send = grid.reshape(rows, cells, lon_parts, share).transpose(2, 1, 0, 3).reshape(lon_parts, cells, rows * share)
        columns = lax.all_to_all(send, "lon", 0, 0, tiled=True).reshape(lon_count, rows * share)
        modes = dot(waves, columns, ((0,), (0,))).astype(BF)
        modes = lax.all_to_all(modes.reshape(lat_parts, 2 * slots, rows * share), "lat", 0, 0, tiled=True)
        modes = modes.reshape(lat_parts, slots, 2, rows, share).transpose(1, 0, 3, 2, 4)
        modes = modes.reshape(slots, lat_count, 2, share)
        modes = (modes.astype(F32) * scale_in).astype(BF)
        bands = jnp.einsum("sli,sipc->slpc", table, modes, preferred_element_type=F32)
        filtered = (gain * bands).astype(BF)
        synth = jnp.einsum("sli,slpc->sipc", table, filtered, preferred_element_type=F32)
        synth = (synth * scale_out).astype(BF)
        synth = synth.reshape(slots, lat_parts, rows, 2, share).transpose(1, 0, 3, 2, 4)
        synth = lax.all_to_all(synth.reshape(lat_parts, 2 * slots, rows * share), "lat", 0, 0, tiled=True)
        back = dot(waves, synth.reshape(2 * ORDERS, rows * share)).astype(BF)
        back = lax.all_to_all(back.reshape(lon_parts, cells, rows * share), "lon", 0, 0, tiled=True)
        back = back.reshape(lon_parts, cells, rows, share).transpose(2, 1, 0, 3).reshape(rows, cells, chans)
        return bands, back

    padding = ((0, 0), (0, ROWS - cells), (0, 0))
    field_pad = jnp.pad(field, padding)
    cot_pad = jnp.pad(cotangent, padding)
    ext = extend(field)
    kernel_mix = call(
        functools.partial(stencil_forward, cells),
        shape((rows, ROWS, chans), F32),
        [pltpu.VMEM((3 * ROWS, 3 * EXT), BF)],
        in_specs=[VMEM] * 3,
    )(ext, own_taps, kernel_weights)
    mixed = jnp.dot(field.reshape(-1, chans), spectral_weight, preferred_element_type=F32).astype(BF).reshape(field.shape)
    bands, spec_out = spectral(mixed, quad, mode_weight)
    output_field, grad_pre, grad_out_w = by_rows(
        functools.partial(pointwise, cells),
        [kernel_mix, jnp.pad(spec_out, padding), field_pad, cot_pad],
        [out_weight, out_weight.T],
        [shape(field.shape, BF), shape((rows, ROWS, chans), BF)],
        [shape((chans, chans), F32)],
    )
    grad_pre_cut = grad_pre[:, :cells]
    adj, grad_kernel_w = call(
        functools.partial(stencil_backward, cells),
        [shape((rows, ROWS, chans), F32), shape((3, chans, chans), F32)],
        [pltpu.VMEM((3 * ROWS, 3 * EXT), BF), pltpu.VMEM((3, 4, ROWS, chans), BF)],
        in_specs=[VMEM] * 4,
    )(extend(grad_pre_cut), adj_taps, jnp.transpose(kernel_weights, (0, 2, 1)), field_pad)
    grad_bands, grad_mixed = spectral(grad_pre_cut, mode_weight, quad)
    gain_part = jnp.sum(bands * grad_bands, axis=(0, 2))
    gain_place = lax.dynamic_update_slice(jnp.zeros((degrees, chans), F32), gain_part, (0, lon * share))
    early = lax.psum((jnp.concatenate([grad_kernel_w, grad_out_w[None]]), gain_place), ("lat", "lon"))
    grad_field, grad_mix_w = by_rows(
        functools.partial(finish, cells),
        [adj, jnp.pad(grad_mixed, padding), field_pad, cot_pad],
        [spectral_weight.T],
        [shape(field.shape, BF)],
        [shape((chans, chans), F32)],
    )
    grad_mix_w = lax.psum(grad_mix_w, ("lat", "lon"))
    weight_grads = jnp.concatenate([early[0][:3], grad_mix_w[None], early[0][3:]]) / math.sqrt(lat_count * lon_count)
    return output_field, grad_field, weight_grads, early[1]


def solution(mesh):
    placed = (P("lat", "lon", None), P("lat", "lon", None), P(), P(), P(), P(), P(), P())
    return jax.shard_map(
        local,
        mesh=mesh,
        in_specs=placed,
        out_specs=(P("lat", "lon", None), P("lat", "lon", None), P(), P()),
        check_vma=False,
    )
```

time: 1390 us -> 561 us (0.40); the launches traced: 1370 us -> 559 us
  other arithmetic: 443 us -> 21.2 us
  local copies, waits for them, and re-layouts: 362 us -> 126 us
  matrix products: 144 us -> 14.9 us
  loops' own time: 113 us -> 0 us
  Pallas kernels: 0 us -> 66.6 us
  blocking collectives: 34.3 us -> 62 us
  waiting for transfers between devices: 228 us -> 204 us
  starting transfers between devices: 32 us -> 49.7 us
    reduce_scatter x2 -> x0, waiting for transfers between devices: 165 us -> none  [spectral_core(): lax.psum_scatter(jnp.einsum('lag,cag->lcg', table_rows, inputs, precision...]
    dynamic_update_slice x192 -> x0, other arithmetic: 135 us -> none  [legendre_table(): lax.scan(advance, initial, jnp.arange(degree_count, dtype=jnp.int32))]
    another operation x4 -> x3, other arithmetic: 131 us -> 2.63 us  [kernel_forward(): return jnp.stack(outputs)]
    psum x1, waiting for transfers between devices: 21 us -> 147 us  [local(): lax.psum((jnp.concatenate([grad_kernel_w, grad_out_w[None]]), gain_place)...]
    dot_general x15 -> x5, matrix products: 132 us -> 11.6 us  [the longest x4 7.71 us: dot(): return lax.dot_general(a, b, (dims, ((), ())), preferred_element_type=F32)]
    another operation x1 -> x0, loops' own time: 113 us -> none  [legendre_table(): lax.scan(advance, initial, jnp.arange(degree_count, dtype=jnp.int32))]
    add x1, other arithmetic: 112 us -> 0.01 us  [local(): my_orders = lat * slots + jnp.arange(slots, dtype=jnp.int32)]
    dynamic_slice x193 -> x2, local copies, waits for them, and re-layouts: 111 us -> 0.86 us  [local(): lax.dynamic_slice_in_dim(degree_gain, lon * share, share, 1)]
  transfers between devices with their start and end apart: 16 -> 14, of which waited for: 7 -> 6; matrix products, arithmetic and copies ran while one was open for 50% -> 7% of each run, Pallas kernels for 0% -> 9%
where the time goes in v1:
time: 561 us; the launch traced here: 559 us
  waiting for transfers between devices  204 us (36%)
  local copies, waits for them, and re-layouts  126 us (22%)
  Pallas kernels  66.6 us (12%)
  blocking collectives  62 us (11%)
  starting transfers between devices  49.7 us (9%)
  other arithmetic  21.2 us (4%)
  matrix products  14.9 us (3%)
  between operations  14.7 us (3%)
    psum x1, waiting for transfers between devices, local(): lax.psum((jnp.concatenate([grad_kernel_w, grad_out_w[None]]), gain_place)...  147 us
    all_to_all x1, blocking collectives, spectral(): lax.all_to_all(send, 'lon', 0, 0, tiled=True)  28.3 us
    pallas_call x1, Pallas kernels, local(): call(functools.partial(stencil_backward, cells), [shape((rows, ROWS, chan...  26.6 us
    convert_element_type x6, local copies, waits for them, and re-layouts, spectral(): modes = (modes.astype(F32) * scale_in).astype(BF)  23.8 us
    pallas_call x1, Pallas kernels, local(): call(functools.partial(stencil_forward, cells), shape((rows, ROWS, chans)...  21.6 us
    ppermute x8, waiting for transfers between devices, ring(): return lax.ppermute(x, axis, pairs)  21 us
    all_to_all x1, waiting for transfers between devices, spectral(): lax.all_to_all(send, 'lon', 0, 0, tiled=True)  18.3 us
    all_to_all x1, blocking collectives, spectral(): lax.all_to_all(modes.reshape(lat_parts, 2 * slots, rows * share), 'lat',...  17.8 us
  transfers between devices with their start and end apart: 14, of which 6 were waited for; matrix products, arithmetic and copies ran while one was open for 7% of the time, Pallas kernels for 9%

profile of v1, /device:TPU:1, one launch (start us, length us, event | category | flops | bytes accessed | tf_op | source)
XLA Modules:
  0.0 559.1 jit_solution(6377800503533640257)
XLA Ops:
  7.2 1.7 copy.113
  8.9 1.9 reshape.380
  10.8 3.9 convolution_convert_fusion
  14.8 3.8 copy.119
  18.5 5.4 reshape_reshape.3
  23.9 3.4 copy.120
  27.3 4.2 copy.121
  31.5 6.0 %all-to-all-start = ((bf16[8,90,1152]{2,1,0:T(8,128)(2,1)}), bf16[8,90,1152]{2,1,0:T(8,128)(2,1)}, u32[]{:S(2)}, u32[]{:S(2)}) async-start(bf16[8,90,1152]{2,1,0:T(8,128)(2,1)} %copy.121), calls=%async_computation | async-start | bytes 3538944 | tf_op jit(solution)/shard_map/all_to_all | solution.py:251
  37.5 2.6 negate_convert_fusion
  42.1 18.3 %all-to-all-done = bf16[8,90,1152]{2,1,0:T(8,128)(2,1)} async-done(((bf16[8,90,1152]{2,1,0:T(8,128)(2,1)}), bf16[8,90,1152]{2,1,0:T(8,128)(2,1)}, u32[]{:S(2)}, u32[]{:S(2)}) %all-to-all-start) | async-done | bytes 1658912 | tf_op jit(solution)/shard_map/all_to_all | solution.py:251
  60.4 2.6 reshape.382
  63.0 3.3 convolution_convert_fusion.4
  66.3 7.6 %all-to-all-start.1 = ((bf16[16,24,1152]{2,1,0:T(8,128)(2,1)}), bf16[16,24,1152]{2,1,0:T(8,128)(2,1)S(1)}, u32[]{:S(2)}, u32[]{:S(2)}) async-start(bf16[16,24,1152]{2,1,0:T(8,128)(2,1)} %bitcast.107), calls=%async_computation.1 | async-start | bytes 1769472 | tf_op jit(solution)/shard_map/all_to_all | solution.py:253
  74.2 2.3 shard_map.112
  76.6 1.6 slice_bitcast_fusion
  78.3 9.3 %all-to-all-done.1 = bf16[16,24,1152]{2,1,0:T(8,128)(2,1)S(1)} async-done(((bf16[16,24,1152]{2,1,0:T(8,128)(2,1)}), bf16[16,24,1152]{2,1,0:T(8,128)(2,1)S(1)}, u32[]{:S(2)}, u32[]{:S(2)}) %all-to-all-start.1) | async-done | bytes 884768 | tf_op jit(solution)/shard_map/all_to_all | solution.py:253
  88.9 5.0 reshape.403
  93.9 5.0 copy.123
  98.9 1.8 multiply_convert_fusion.3
  103.2 2.4 copy.126
  105.6 3.5 reshape.413
  110.2 3.9 all-to-all-start.2
  114.8 2.9 collective-permute-start.1
  117.8 9.1 %all-to-all-done.2 = bf16[16,24,1152]{2,1,0:T(8,128)(2,1)S(1)} async-done(((bf16[16,24,1152]{2,1,0:T(8,128)(2,1)}), bf16[16,24,1152]{2,1,0:T(8,128)(2,1)S(1)}, u32[]{:S(2)}, u32[]{:S(2)}) %all-to-all-start.2) | async-done | bytes 884768 | tf_op jit(solution)/shard_map/all_to_all | solution.py:262
  126.9 2.3 convolution_convert_fusion.2
  129.2 2.6 reshape.387
  131.8 7.8 %all-to-all-start.3 = ((bf16[8,90,1152]{2,1,0:T(8,128)(2,1)}), bf16[8,90,1152]{2,1,0:T(8,128)(2,1)}, u32[]{:S(2)}, u32[]{:S(2)}) async-start(bf16[8,90,1152]{2,1,0:T(8,128)(2,1)} %reshape.387), calls=%async_computation.3 | async-start | bytes 3538944 | tf_op jit(solution)/shard_map/all_to_all | solution.py:264
  143.4 4.8 collective-permute-start.2
  153.7 4.0 fusion.2.ext_ref
  157.7 21.6 %shard_map.111.km_ref = f32[24,96,384]{2,1,0:T(8,128)} custom-call(bf16[26,128,384]{2,1,0:T(8,128)(2,1)} %fusion.2.ext_ref, f32[24,16,128]{2,1,0:T(8,128)} %pad.29.taps_ref, bf16[3,384,384]{2,1,0:T(8,128)(2,1)} %w_ref.2), custom_call_target="tpu_custom_call" | custom-call | tf_op jit(solution)/shard_map/pallas_call | solution.py:272
  179.3 4.1 copy.128
  183.3 3.8 copy.129
  187.1 3.0 copy.130
  191.5 8.4 %shard_map.113 = (bf16[24,90,384]{2,1,0:T(8,128)(2,1)}, bf16[24,96,384]{2,1,0:T(8,128)(2,1)}, f32[384,384]{1,0:T(8,128)}) custom-call(f32[24,96,384]{2,1,0:T(8,128)} %shard_map.111.km_ref, bf16[24,96,384]{2,1,0:T(8,128)(2,1)} %pad.31.so_ref, bf16[24,96,384]{2,1,0:T(8,128)(2,1)} %pad.32.f_ref.field_ref, bf16[24,96,384]{2,1,0:T(8,128)(2,1)} %pad.33.ct_ref, ...), custom_call_target="tpu_custom_call" | custom-call | tf_op jit(solution)/shard_map/pallas_call | solution.py:212
  200.0 4.0 copy.137
  204.0 3.5 copy.138
  207.5 3.0 copy.139
  210.5 28.3 %all_to_all.40 = bf16[8,90,1152]{2,1,0:T(8,128)(2,1)} all-to-all(bf16[8,90,1152]{2,1,0:T(8,128)(2,1)S(1)} %copy.139), channel_id=1, replica_groups=mesh['lat'=16,'lon'=8] {'lon'}, dimensions={0} | all-to-all | bytes 3317760 | tf_op jit(solution)/shard_map/all_to_all | solution.py:251
  238.8 1.7 reshape.393
  241.5 17.8 %all_to_all.41 = bf16[16,24,1152]{2,1,0:T(8,128)(2,1)S(1)} all-to-all(bf16[16,24,1152]{2,1,0:T(8,128)(2,1)S(1)} %bitcast.110), channel_id=1, replica_groups=mesh['lat'=16,'lon'=8] {'lat'}, dimensions={0} | all-to-all | bytes 1769472 | tf_op jit(solution)/shard_map/all_to_all | solution.py:253
  259.3 3.7 reshape.404
  263.0 5.1 copy.140
  268.1 3.7 copy.141
  276.2 2.4 copy.144
  278.6 3.5 reshape.414
  282.3 15.9 %all_to_all.42 = bf16[16,24,1152]{2,1,0:T(8,128)(2,1)S(1)} all-to-all(bf16[16,24,1152]{2,1,0:T(8,128)(2,1)S(1)} %copy.154), channel_id=1, replica_groups=mesh['lat'=16,'lon'=8] {'lat'}, dimensions={0} | all-to-all | bytes 1769472 | tf_op jit(solution)/shard_map/all_to_all | solution.py:262
  300.8 7.9 %all-to-all-start.7 = ((bf16[8,90,1152]{2,1,0:T(8,128)(2,1)}), bf16[8,90,1152]{2,1,0:T(8,128)(2,1)}, u32[]{:S(2)}, u32[]{:S(2)}) async-start(bf16[8,90,1152]{2,1,0:T(8,128)(2,1)} %reshape.398), calls=%async_computation.7 | async-start | bytes 3538944 | tf_op jit(solution)/shard_map/all_to_all | solution.py:264
  308.8 1.6 collective-permute-start.5
  310.4 18.8 %collective-permute-done.5 = bf16[24,3,384]{2,1,0:T(4,128)(2,1)S(1)} collective-permute-done((bf16[24,3,384]{2,1,0:T(4,128)(2,1)S(1)}, bf16[24,3,384]{2,1,0:T(4,128)(2,1)S(1)}, u32[]{:S(2)}, u32[]{:S(2)}) %collective-permute-start.5) | collective-permute-done | bytes 55328 | tf_op jit(solution)/shard_map/ppermute | solution.py:28
  329.2 2.2 collective-permute-done.4
  334.0 4.6 collective-permute-start.6
  338.6 2.1 copy.136
  341.7 1.6 pad.34.taps_ref
  343.3 4.0 fusion.5.ext_ref
  347.3 26.6 %shard_map.114 = (f32[24,96,384]{2,1,0:T(8,128)}, f32[3,384,384]{2,1,0:T(8,128)}) custom-call(bf16[26,128,384]{2,1,0:T(8,128)(2,1)} %fusion.5.ext_ref, f32[24,16,128]{2,1,0:T(8,128)} %pad.34.taps_ref, bf16[3,384,384]{2,1,0:T(8,128)(2,1)} %bitcast.102, bf16[24,96,384]{2,1,0:T(8,128)(2,1)} %pad.32.f_ref.field_ref), custom_call_target="tpu_custom_call" | custom-call | tf_op jit(solution)/shard_map/pallas_call | solution.py:288
  373.9 3.1 pad_maximum_fusion.4
  378.3 3.0 copy.146
  381.3 2.1 copy.147
  383.4 3.0 copy.148
  387.8 7.6 %shard_map.115 = (bf16[24,90,384]{2,1,0:T(8,128)(2,1)}, f32[384,384]{1,0:T(8,128)}) custom-call(f32[24,96,384]{2,1,0:T(8,128)} %get-tuple-element.13.adj_ref, bf16[24,96,384]{2,1,0:T(8,128)(2,1)} %pad.35.gm_ref, bf16[24,96,384]{2,1,0:T(8,128)(2,1)} %pad.32.f_ref.field_ref, bf16[24,96,384]{2,1,0:T(8,128)(2,1)} %pad.33.ct_ref, bf16[384,384]{1,0:T(8,128)(2,1)} %bitcast.105), custom_call_target="tpu_custom_call" | custom-call | tf_op jit(solution)/shard_map/pallas_call | solution.py:212
  396.9 1.7 copy.151
  398.6 1.7 copy.152
  400.4 146.5 %all-reduce.11.cloned.1.call-done = (f32[4,384,384]{2,1,0:T(8,128)}, f32[1,384,384]{2,1,0:T(8,128)}, f32[192,384]{1,0:T(8,128)}) async-done(((f32[4,384,384]{2,1,0:T(8,128)}, f32[1,384,384]{2,1,0:T(8,128)}, f32[192,384]{1,0:T(8,128)}), (f32[4,384,384]{2,1,0:T(8,128)}, f32[1,384,384]{2,1,0:T(8,128)}, f32[192,384]{1,0:T(8,128)})) %all-reduce.11.cloned.1.call-update) | async-done | bytes 3244048 | tf_op jit(solution)/shard_map/psum | solution.py:297
  549.7 1.9 maximum_multiply_fusion
  (149 shorter events, 37.9 us)
Async XLA Ops:
  7.2 34.2 %copy-start = (f32[192,384]{1,0:T(8,128)S(1)}, f32[192,384]{1,0:T(8,128)}, u32[]{:S(2)}) copy-start(f32[192,384]{1,0:T(8,128)} %param.13) | copy-start | bytes 884740
  8.9 1.9 copy-start.12
  31.5 28.9 %all-to-all-start = ((bf16[8,90,1152]{2,1,0:T(8,128)(2,1)}), bf16[8,90,1152]{2,1,0:T(8,128)(2,1)}, u32[]{:S(2)}, u32[]{:S(2)}) async-start(bf16[8,90,1152]{2,1,0:T(8,128)(2,1)} %copy.121), calls=%async_computation | async-start | bytes 3538944 | tf_op jit(solution)/shard_map/all_to_all | solution.py:251
  41.2 85.7 %copy-start.17 = (bf16[720,384]{0,1:T(8,128)(2,1)}, bf16[720,384]{0,1:T(8,128)(2,1)S(1)}, u32[]{:S(2)}) copy-start(bf16[720,384]{0,1:T(8,128)(2,1)S(1)} %convert_element_type.140) | copy-start | bytes 1658884
  63.0 11.0 %copy-start.21 = (f32[192,48]{1,0:T(8,128)S(1)}, f32[192,48]{1,0:T(8,128)}, u32[]{:S(2)}) copy-start(f32[192,48]{1,0:T(8,128)} %constant_dynamic-slice_fusion) | copy-start | bytes 110596
  66.3 21.3 %all-to-all-start.1 = ((bf16[16,24,1152]{2,1,0:T(8,128)(2,1)}), bf16[16,24,1152]{2,1,0:T(8,128)(2,1)S(1)}, u32[]{:S(2)}, u32[]{:S(2)}) async-start(bf16[16,24,1152]{2,1,0:T(8,128)(2,1)} %bitcast.107), calls=%async_computation.1 | async-start | bytes 1769472 | tf_op jit(solution)/shard_map/all_to_all | solution.py:253
  74.1 27.9 %copy-start.19 = (f32[192,48]{0,1:T(8,128)}, f32[192,48]{0,1:T(8,128)S(1)}, u32[]{:S(2)}) copy-start(f32[192,48]{0,1:T(8,128)S(1)} %copy.117) | copy-start | bytes 110596
  98.9 2.2 copy-start.2
  102.0 1.0 copy-start.5
  109.2 8.6 %copy-start.31 = (s32[3,384]{1,0:T(4,128)S(1)}, s32[3,384]{1,0:T(4,128)}, u32[]{:S(2)}) copy-start(s32[3,384]{1,0:T(4,128)} %param.15) | copy-start | bytes 13828
  110.2 16.7 %all-to-all-start.2 = ((bf16[16,24,1152]{2,1,0:T(8,128)(2,1)}), bf16[16,24,1152]{2,1,0:T(8,128)(2,1)S(1)}, u32[]{:S(2)}, u32[]{:S(2)}) async-start(bf16[16,24,1152]{2,1,0:T(8,128)(2,1)} %copy.153), calls=%async_computation.2 | async-start | bytes 1769472 | tf_op jit(solution)/shard_map/all_to_all | solution.py:262
  114.8 25.9 %collective-permute-start.1 = (bf16[24,3,384]{2,1,0:T(4,128)(2,1)}, bf16[24,3,384]{2,1,0:T(4,128)(2,1)S(1)}, u32[]{:S(2)}, u32[]{:S(2)}) collective-permute-start(bf16[24,3,384]{2,1,0:T(4,128)(2,1)} %get-tuple-element.44), channel_id=1, source_target_pairs={{0,1},{1,2},{2,3},{3,4},{4,5},{5,6},{6,7},{7,0},{8,9},{9,10},{10,1... | collective-permute-start | bytes 165896 | tf_op jit(solution)/shard_map/ppermute | solution.py:28
  117.7 23.0 %collective-permute-start = (bf16[24,3,384]{2,1,0:T(4,128)(2,1)}, bf16[24,3,384]{2,1,0:T(4,128)(2,1)S(1)}, u32[]{:S(2)}, u32[]{:S(2)}) collective-permute-start(bf16[24,3,384]{2,1,0:T(4,128)(2,1)} %get-tuple-element.43), channel_id=1, source_target_pairs={{0,7},{1,0},{2,1},{3,2},{4,3},{5,4},{6,5},{7,6},{8,15},{9,8},{10,9... | collective-permute-start | bytes 165896 | tf_op jit(solution)/shard_map/ppermute | solution.py:28
  131.8 7.8 %copy-start.30 = (f32[3,3,7,384]{3,2,1,0:T(8,128)S(1)}, f32[3,3,7,384]{3,2,1,0:T(8,128)}, u32[]{:S(2)}) copy-start(f32[3,3,7,384]{3,2,1,0:T(8,128)} %param.14) | copy-start | bytes 290308
  131.8 47.4 %all-to-all-start.3 = ((bf16[8,90,1152]{2,1,0:T(8,128)(2,1)}), bf16[8,90,1152]{2,1,0:T(8,128)(2,1)}, u32[]{:S(2)}, u32[]{:S(2)}) async-start(bf16[8,90,1152]{2,1,0:T(8,128)(2,1)} %reshape.387), calls=%async_computation.3 | async-start | bytes 3538944 | tf_op jit(solution)/shard_map/all_to_all | solution.py:264
  140.7 0.6 copy-start.23
  140.7 0.7 copy-start.25
  142.1 11.6 %collective-permute-start.3 = (bf16[1,128,384]{2,1,0:T(8,128)(2,1)}, bf16[1,128,384]{2,1,0:T(8,128)(2,1)}, u32[]{:S(2)}, u32[]{:S(2)}) collective-permute-start(bf16[1,128,384]{2,1,0:T(8,128)(2,1)} %get-tuple-element.40), channel_id=1, source_target_pairs={{8,0},{16,8},{24,16},{32,24},{40,32},{48,40},{56,48},{64,56},{72,6... | collective-permute-start | bytes 294920 | tf_op jit(solution)/shard_map/ppermute | solution.py:28
  143.3 7.7 %copy-start.10 = (bf16[24,90,384]{2,0,1:T(8,128)(2,1)S(1)}, bf16[24,90,384]{2,0,1:T(8,128)(2,1)}, u32[]{:S(2)}) copy-start(bf16[24,90,384]{2,0,1:T(8,128)(2,1)} %param.9) | copy-start | bytes 4976644
  143.4 10.3 %collective-permute-start.2 = (bf16[1,128,384]{2,1,0:T(8,128)(2,1)S(1)}, bf16[1,128,384]{2,1,0:T(8,128)(2,1)}, u32[]{:S(2)}, u32[]{:S(2)}) collective-permute-start(bf16[1,128,384]{2,1,0:T(8,128)(2,1)S(1)} %get-tuple-element.39), channel_id=1, source_target_pairs={{0,8},{8,16},{16,24},{24,32},{32,40},{40,48},{48,56},{56,64},{64,7... | collective-permute-start | bytes 294920 | tf_op jit(solution)/shard_map/ppermute | solution.py:28
  151.3 1.5 copy-start.11
  151.3 2.3 copy-start.24
  151.3 2.3 copy-start.26
  238.8 1.7 copy-start.18
  271.8 1.7 copy-start.3
  272.0 2.4 copy-start.6
  272.0 2.4 copy-start.20
  300.8 7.9 %copy-start.4 = (bf16[24,96,384]{2,1,0:T(8,128)(2,1)S(1)}, bf16[24,96,384]{2,1,0:T(8,128)(2,1)}, u32[]{:S(2)}) copy-start(bf16[24,96,384]{2,1,0:T(8,128)(2,1)} %get-tuple-element.12) | copy-start | bytes 5308420
  300.8 77.5 %all-to-all-start.7 = ((bf16[8,90,1152]{2,1,0:T(8,128)(2,1)}), bf16[8,90,1152]{2,1,0:T(8,128)(2,1)}, u32[]{:S(2)}, u32[]{:S(2)}) async-start(bf16[8,90,1152]{2,1,0:T(8,128)(2,1)} %reshape.398), calls=%async_computation.7 | async-start | bytes 3538944 | tf_op jit(solution)/shard_map/all_to_all | solution.py:264
  308.7 238.2 %all-reduce.11.cloned.1.call-start = ((), (), s32[]{:S(2)}) async-start(), calls=%async_computation.8 | async-start | bytes 6488064 | tf_op jit(solution)/shard_map/psum | solution.py:297
  308.8 20.4 %collective-permute-start.5 = (bf16[24,3,384]{2,1,0:T(4,128)(2,1)S(1)}, bf16[24,3,384]{2,1,0:T(4,128)(2,1)S(1)}, u32[]{:S(2)}, u32[]{:S(2)}) collective-permute-start(bf16[24,3,384]{2,1,0:T(4,128)(2,1)S(1)} %get-tuple-element.42), channel_id=1, source_target_pairs={{0,1},{1,2},{2,3},{3,4},{4,5},{5,6},{6,7},{7,0},{8,9},{9,10},{10,1... | collective-permute-start | bytes 165896 | tf_op jit(solution)/shard_map/ppermute | solution.py:28
  310.4 28.2 %copy-start.7 = (bf16[3,384,384]{2,1,0:T(8,128)(2,1)S(1)}, bf16[3,384,384]{2,1,0:T(8,128)(2,1)}, u32[]{:S(2)}) copy-start(bf16[3,384,384]{2,1,0:T(8,128)(2,1)} %w_ref.2) | copy-start | bytes 2654212
  310.4 30.3 %copy-start.13 = (bf16[384,384]{1,0:T(8,128)(2,1)S(1)}, bf16[384,384]{1,0:T(8,128)(2,1)}, u32[]{:S(2)}) copy-start(bf16[384,384]{1,0:T(8,128)(2,1)} %param.11) | copy-start | bytes 884740
  310.4 21.0 %collective-permute-start.4 = (bf16[24,3,384]{2,1,0:T(4,128)(2,1)S(1)}, bf16[24,3,384]{2,1,0:T(4,128)(2,1)S(1)}, u32[]{:S(2)}, u32[]{:S(2)}) collective-permute-start(bf16[24,3,384]{2,1,0:T(4,128)(2,1)S(1)} %get-tuple-element.41), channel_id=1, source_target_pairs={{0,7},{1,0},{2,1},{3,2},{4,3},{5,4},{6,5},{7,6},{8,15},{9,8},{10,9... | collective-permute-start | bytes 165896 | tf_op jit(solution)/shard_map/ppermute | solution.py:28
  329.2 2.7 copy-start.27
  331.4 0.6 copy-start.28
  332.7 10.6 %collective-permute-start.7 = (bf16[1,128,384]{2,1,0:T(8,128)(2,1)}, bf16[1,128,384]{2,1,0:T(8,128)(2,1)}, u32[]{:S(2)}, u32[]{:S(2)}) collective-permute-start(bf16[1,128,384]{2,1,0:T(8,128)(2,1)} %get-tuple-element.38), channel_id=1, source_target_pairs={{8,0},{16,8},{24,16},{32,24},{40,32},{48,40},{56,48},{64,56},{72,6... | collective-permute-start | bytes 294920 | tf_op jit(solution)/shard_map/ppermute | solution.py:28
  334.0 9.3 %collective-permute-start.6 = (bf16[1,128,384]{2,1,0:T(8,128)(2,1)}, bf16[1,128,384]{2,1,0:T(8,128)(2,1)}, u32[]{:S(2)}, u32[]{:S(2)}) collective-permute-start(bf16[1,128,384]{2,1,0:T(8,128)(2,1)} %get-tuple-element.37), channel_id=1, source_target_pairs={{0,8},{8,16},{16,24},{24,32},{32,40},{40,48},{48,56},{56,64},{64,7... | collective-permute-start | bytes 294920 | tf_op jit(solution)/shard_map/ppermute | solution.py:28
  347.3 26.6 %copy-start.15 = (f32[384,384]{1,0:T(8,128)S(1)}, f32[384,384]{1,0:T(8,128)}, u32[]{:S(2)}) copy-start(f32[384,384]{1,0:T(8,128)} %get-tuple-element.16) | copy-start | bytes 1769476
  373.9 3.1 copy-start.29
  378.3 5.1 copy-start.14
  395.4 1.5 copy-start.8
  395.4 3.2 copy-start.9
  546.9 2.8 copy-start.16
  549.6 2.6 copy-start.1
  549.7 1.9 copy-start.22
Sparse Core Ops, SparseCore 0:
  395.5 151.2 all-reduce.10

commit v2 on v1

--- a/solution.py
+++ b/solution.py
@@ -129,6 +129,218 @@
     out = ct_ref[...].astype(F32) + adj_ref[...] + dot(gm, wt_ref[...]).reshape(adj_ref.shape)
     out_ref[...] = out.astype(BF)[:, :cells]
     gmw_ref[...] += dot(f_ref[...].reshape(flat), gm, ((0,), (0,)))
+
+
+def block_swap(parts):
+    group = lax.broadcasted_iota(jnp.int32, parts[0].shape, 1) // 16
+    for k in range(3):
+        high = (group >> k) & 1 == 1
+        width = 16 << k
+        fresh = list(parts)
+        for a in range(8):
+            if (a >> k) & 1 == 0:
+                b = a + (1 << k)
+                fresh[a] = jnp.where(high, pltpu.roll(parts[b], width, 1), parts[a])
+                fresh[b] = jnp.where(high, parts[b], pltpu.roll(parts[a], 128 - width, 1))
+        parts = fresh
+    return parts
+
+
+def tile_swap(x):
+    row = lax.broadcasted_iota(jnp.int32, x.shape, 1)
+    group = lax.broadcasted_iota(jnp.int32, x.shape, 2) // 16
+    for k in range(3):
+        row_bit = (row >> k) & 1
+        group_bit = (group >> k) & 1
+        width = 16 << k
+        down = pltpu.roll(pltpu.roll(x, 8 - (1 << k), 1), width, 2)
+        up = down if k == 2 else pltpu.roll(pltpu.roll(x, 1 << k, 1), 128 - width, 2)
+        x = jnp.where(row_bit == group_bit, x, jnp.where(group_bit == 1, down, up))
+    return x
+
+
+PAD = 80
+
+
+def exchange(axis, me, parts, send, recv, send_sem, recv_sem):
+    def copy(v, peer, slot):
+        return pltpu.make_async_remote_copy(
+            src_ref=send.at[v, peer],
+            dst_ref=recv.at[v, slot],
+            send_sem=send_sem.at[v, peer],
+            recv_sem=recv_sem.at[v, slot],
+            device_id={axis: peer},
+            device_id_type=pl.DeviceIdType.MESH,
+        )
+
+    def over(body):
+        lax.fori_loop(1, parts, lambda d, carry: (body(lax.rem(me + d, parts)), carry)[1], 0)
+
+    def start(v):
+        over(lambda peer: copy(v, peer, me).start())
+        recv[v, me] = send[v, me]
+
+    def arrive(v):
+        over(lambda peer: copy(v, peer, peer).wait_recv())
+
+    def drain(v):
+        over(lambda peer: copy(v, peer, peer).wait_send())
+
+    return start, arrive, drain
+
+
+def spectral_kernel(
+    x_ref, table_ref, turned_ref, into_ref, back_ref, gain_ref, in_ref, out_ref_scale,
+    grid_ref, bands_ref,
+    send1, recv1, send2, recv2, send3, recv3, send4, recv4, modes, rows_ref,
+    s1, r1, s2, r2, s3, r3, s4, r4,
+):
+    lat, lon = lax.axis_index("lat"), lax.axis_index("lon")
+    lons, lats = lax.axis_size("lon"), lax.axis_size("lat")
+    barrier = pltpu.get_barrier_semaphore()
+
+    def greet(axis, me, parts):
+        def body(d, carry):
+            pl.semaphore_signal(
+                barrier, inc=1, device_id={axis: lax.rem(me + d, parts)}, device_id_type=pl.DeviceIdType.MESH
+            )
+            return carry
+
+        lax.fori_loop(1, parts, body, 0)
+
+    greet("lon", lon, lons)
+    greet("lat", lat, lats)
+
+    start1, arrive1, drain1 = exchange("lon", lon, lons, send1, recv1, s1, r1)
+    start2, arrive2, drain2 = exchange("lat", lat, lats, send2, recv2, s2, r2)
+    start3, arrive3, drain3 = exchange("lat", lat, lats, send3, recv3, s3, r3)
+    start4, arrive4, drain4 = exchange("lon", lon, lons, send4, recv4, s4, r4)
+    order = lax.broadcasted_iota(jnp.int32, (192, 128), 1) // 32
+    blank = jnp.zeros((8, 128), F32)
+
+    def tiles(body):
+        def step(n, carry):
+            body(n // 6, pl.multiple_of(n % 6 * 16, 16))
+            return carry
+
+        lax.fori_loop(0, 18, step, 0)
+
+    def split(v):
+        def body(g, j):
+            parts = [x_ref[g * 8 + n, pl.ds(j, 16), v * 128 : (v + 1) * 128].astype(F32) for n in range(8)]
+            lanes = pl.ds(pl.multiple_of(g * 128, 128), 128)
+            for p, part in enumerate(block_swap(parts)):
+                send1[v, p, pl.ds(j, 16), lanes] = part.astype(BF)
+
+        tiles(body)
+
+    def analyse(v):
+        modes[...] = dot(into_ref[...], recv1[v].reshape(768, 384))
+
+        def step(b, carry):
+            block = modes[pl.ds(pl.multiple_of(b * 24, 8), 24), :]
+            turned = [tile_swap(block[:, g * 128 : (g + 1) * 128].reshape(3, 8, 128)) for g in range(3)]
+            pieces = [turned[g][o] for o in range(3) for g in range(3)] + [blank]
+            send2[v, b] = jnp.concatenate(pieces, axis=0).astype(BF)
+            return carry
+
+        lax.fori_loop(0, lats, step, 0)
+
+    def filter_bands(v):
+        def gather(b, carry):
+            rows = pl.ds(pl.multiple_of(b * 24, 8), 24)
+            block = recv2[v, b].astype(F32)
+            for o in range(3):
+                rows_ref[o, rows] = block[o * 24 : (o + 1) * 24] * in_ref[o, rows]
+            return carry
+
+        lax.fori_loop(0, lats, gather, 0)
+        for o in range(3):
+            every = dot(table_ref[o], rows_ref[o].astype(BF))
+            band = every[:192]
+            for m in range(1, 4):
+                band = jnp.where(order == m, every[m * 192 : (m + 1) * 192], band)
+            bands_ref[o, :, v * 128 : (v + 1) * 128] = band
+            band = band * gain_ref[:, v * 128 : (v + 1) * 128]
+            spread = jnp.concatenate([jnp.where(order == m, band, 0.0).astype(BF) for m in range(4)], axis=0)
+            rows_ref[o] = dot(turned_ref[o], spread) * out_ref_scale[o]
+
+        def scatter(b, carry):
+            rows = pl.ds(pl.multiple_of(b * 24, 8), 24)
+            send3[v, b] = jnp.concatenate([rows_ref[o, rows] for o in range(3)] + [blank], axis=0).astype(BF)
+            return carry
+
+        lax.fori_loop(0, lats, scatter, 0)
+
+    def synthesise(v):
+        def step(b, carry):
+            block = recv3[v, b].astype(F32)[:72].reshape(9, 8, 128)
+            turned = tile_swap(block)
+            wide = [jnp.concatenate([turned[o * 3 + g] for o in range(3)], axis=0) for g in range(3)]
+            modes[pl.ds(pl.multiple_of(b * 24, 8), 24), :] = jnp.concatenate(wide, axis=1)
+            return carry
+
+        lax.fori_loop(0, lats, step, 0)
+        send4[v] = dot(back_ref[...], modes[...].astype(BF)).astype(BF).reshape(8, ROWS, 384)
+
+    def join(v):
+        def body(g, j):
+            lanes = pl.ds(pl.multiple_of(g * 128, 128), 128)
+            parts = [recv4[v, p, pl.ds(j, 16), lanes].astype(F32) for p in range(8)]
+            for n, part in enumerate(block_swap(parts)):
+                grid_ref[g * 8 + n, pl.ds(j, 16), v * 128 : (v + 1) * 128] = part.astype(BF)
+
+        tiles(body)
+
+    for v in range(3):
+        split(v)
+        if v == 0:
+            pl.semaphore_wait(barrier, lons + lats - 2)
+        start1(v)
+
+    def two(v):
+        arrive1(v)
+        analyse(v)
+        start2(v)
+
+    def three(v):
+        arrive2(v)
+        filter_bands(v)
+        start3(v)
+
+    def four(v):
+        arrive3(v)
+        synthesise(v)
+        start4(v)
+
+    def five(v):
+        arrive4(v)
+        join(v)
+
+    for stage, v in ((two, 0), (three, 0), (two, 1), (four, 0), (three, 1), (two, 2), (four, 1), (three, 2), (five, 0), (four, 2), (five, 1), (five, 2)):
+        stage(v)
+    for v in range(3):
+        for drain in (drain1, drain2, drain3, drain4):
+            drain(v)
+
+
+def spectral_call(x, table, turned, into, back, gain, scale_in, scale_out):
+    shape = jax.ShapeDtypeStruct
+    lons, lats = lax.axis_size("lon"), lax.axis_size("lat")
+    lon_buf = pltpu.VMEM((3, lons, ROWS, 384), BF)
+    lat_buf = pltpu.VMEM((3, lats, PAD, 128), BF)
+    lon_sem = pltpu.SemaphoreType.DMA((3, lons))
+    lat_sem = pltpu.SemaphoreType.DMA((3, lats))
+    return pl.pallas_call(
+        spectral_kernel,
+        out_shape=[shape(x.shape, BF), shape((3, 192, 384), F32)],
+        in_specs=[VMEM] * 8,
+        out_specs=[VMEM] * 2,
+        scratch_shapes=[lon_buf, lon_buf] + [lat_buf] * 4 + [lon_buf, lon_buf]
+        + [pltpu.VMEM((384, 384), F32), pltpu.VMEM((3, 384, 128), F32)]
+        + [lon_sem, lon_sem, lat_sem, lat_sem, lat_sem, lat_sem, lon_sem, lon_sem],
+        compiler_params=pltpu.CompilerParams(collective_id=1, has_side_effects=True, vmem_limit_bytes=56 << 20),
+    )(x, table, turned, into, back, gain, scale_in, scale_out)
 
 
 def legendre_kernel(m_ref, x_ref, diag_ref, out_ref):
@@ -224,7 +436,6 @@
     lat_parts, lon_parts = lax.axis_size("lat"), lax.axis_size("lon")
     lat, lon = lax.axis_index("lat"), lax.axis_index("lon")
     lat_count, lon_count = rows * lat_parts, cells * lon_parts
-    share = chans // lon_parts
     degrees = degree_gain.shape[0]
     slots = ORDERS // lat_parts
     shape = jax.ShapeDtypeStruct
@@ -239,31 +450,21 @@
     my_orders = lat * slots + jnp.arange(slots, dtype=jnp.int32)
     table = legendre_rows(my_orders, lat_count, degrees)
     waves = fourier(lon_count, all_orders.reshape(-1)).reshape(lon_count, 2 * ORDERS)
+    waves = jnp.pad(waves.reshape(lon_parts, cells, -1), ((0, 0), (0, ROWS - cells), (0, 0))).reshape(lon_parts * ROWS, -1)
+    table = table.reshape(3, 4 * degrees, lat_count)
+    turned = jnp.transpose(table, (0, 2, 1))
     quad = 2.0 * math.pi / lon_count * (math.pi / lat_count) * jnp.sin(
         colatitudes(jnp.arange(lat_count, dtype=jnp.int32), lat_count)
     )
-    quad = quad.reshape(1, lat_count, 1, 1)
-    mode_weight = jnp.where(my_orders == 0, 1.0, 2.0).astype(F32)[:, None, None, None]
-    gain = lax.dynamic_slice_in_dim(degree_gain, lon * share, share, 1)[None, :, None, :]
+    quad = jnp.broadcast_to(quad[None, :, None], (3, lat_count, 128))
+    mode_weight = jnp.where(my_orders == 0, 1.0, 2.0).astype(F32).reshape(3, 1, 4, 1)
+    mode_weight = jnp.broadcast_to(mode_weight, (3, lat_count, 4, 32)).reshape(3, lat_count, 128)
+    groups = degree_gain.reshape(degrees, 3, lon_parts, 16)
+    gain = lax.dynamic_slice_in_dim(groups, lon, 1, 2)
+    gain = jnp.broadcast_to(gain, groups.shape).reshape(degrees, chans)
 
     def spectral(grid, scale_in, scale_out):
-        send = grid.reshape(rows, cells, lon_parts, share).transpose(2, 1, 0, 3).reshape(lon_parts, cells, rows * share)
-        columns = lax.all_to_all(send, "lon", 0, 0, tiled=True).reshape(lon_count, rows * share)
-        modes = dot(waves, columns, ((0,), (0,))).astype(BF)
-        modes = lax.all_to_all(modes.reshape(lat_parts, 2 * slots, rows * share), "lat", 0, 0, tiled=True)
-        modes = modes.reshape(lat_parts, slots, 2, rows, share).transpose(1, 0, 3, 2, 4)
-        modes = modes.reshape(slots, lat_count, 2, share)
-        modes = (modes.astype(F32) * scale_in).astype(BF)
-        bands = jnp.einsum("sli,sipc->slpc", table, modes, preferred_element_type=F32)
-        filtered = (gain * bands).astype(BF)
-        synth = jnp.einsum("sli,slpc->sipc", table, filtered, preferred_element_type=F32)
-        synth = (synth * scale_out).astype(BF)
-        synth = synth.reshape(slots, lat_parts, rows, 2, share).transpose(1, 0, 3, 2, 4)
-        synth = lax.all_to_all(synth.reshape(lat_parts, 2 * slots, rows * share), "lat", 0, 0, tiled=True)
-        back = dot(waves, synth.reshape(2 * ORDERS, rows * share)).astype(BF)
-        back = lax.all_to_all(back.reshape(lon_parts, cells, rows * share), "lon", 0, 0, tiled=True)
-        back = back.reshape(lon_parts, cells, rows, share).transpose(2, 1, 0, 3).reshape(rows, cells, chans)
-        return bands, back
+        return spectral_call(grid, table, turned, waves.T, waves, gain, scale_in, scale_out)
 
     padding = ((0, 0), (0, ROWS - cells), (0, 0))
     field_pad = jnp.pad(field, padding)
@@ -276,10 +477,10 @@
         in_specs=[VMEM] * 3,
     )(ext, own_taps, kernel_weights)
     mixed = jnp.dot(field.reshape(-1, chans), spectral_weight, preferred_element_type=F32).astype(BF).reshape(field.shape)
-    bands, spec_out = spectral(mixed, quad, mode_weight)
+    spec_out, bands = spectral(jnp.pad(mixed, padding), quad, mode_weight)
     output_field, grad_pre, grad_out_w = by_rows(
         functools.partial(pointwise, cells),
-        [kernel_mix, jnp.pad(spec_out, padding), field_pad, cot_pad],
+        [kernel_mix, spec_out, field_pad, cot_pad],
         [out_weight, out_weight.T],
         [shape(field.shape, BF), shape((rows, ROWS, chans), BF)],
         [shape((chans, chans), F32)],
@@ -291,20 +492,22 @@
         [pltpu.VMEM((3 * ROWS, 3 * EXT), BF), pltpu.VMEM((3, 4, ROWS, chans), BF)],
         in_specs=[VMEM] * 4,
     )(extend(grad_pre_cut), adj_taps, jnp.transpose(kernel_weights, (0, 2, 1)), field_pad)
-    grad_bands, grad_mixed = spectral(grad_pre_cut, mode_weight, quad)
-    gain_part = jnp.sum(bands * grad_bands, axis=(0, 2))
-    gain_place = lax.dynamic_update_slice(jnp.zeros((degrees, chans), F32), gain_part, (0, lon * share))
-    early = lax.psum((jnp.concatenate([grad_kernel_w, grad_out_w[None]]), gain_place), ("lat", "lon"))
+    grad_mixed, grad_bands = spectral(grad_pre, mode_weight, quad)
+    gain_part = jnp.sum(bands * grad_bands, axis=0).reshape(degrees, 3, 8, 16).sum(axis=2, keepdims=True)
+    gain_place = lax.dynamic_update_slice(jnp.zeros(groups.shape, F32), gain_part, (0, 0, lon, 0)).reshape(degrees, chans)
+    early = lax.psum(jnp.concatenate([grad_kernel_w, grad_out_w[None]]), ("lat", "lon"))
     grad_field, grad_mix_w = by_rows(
         functools.partial(finish, cells),
-        [adj, jnp.pad(grad_mixed, padding), field_pad, cot_pad],
+        [adj, grad_mixed, field_pad, cot_pad],
         [spectral_weight.T],
         [shape(field.shape, BF)],
         [shape((chans, chans), F32)],
     )
-    grad_mix_w = lax.psum(grad_mix_w, ("lat", "lon"))
-    weight_grads = jnp.concatenate([early[0][:3], grad_mix_w[None], early[0][3:]]) / math.sqrt(lat_count * lon_count)
-    return output_field, grad_field, weight_grads, early[1]
+    late = jnp.concatenate([grad_mix_w, gain_place])
+    late, early = lax.optimization_barrier((late, early))
+    late = lax.psum(late, ("lat", "lon"))
+    weight_grads = jnp.concatenate([early[:3], late[None, :chans], early[3:]]) / math.sqrt(lat_count * lon_count)
+    return output_field, grad_field, weight_grads, late[chans:]
 
 
 def solution(mesh):

time: 561 us -> 563 us (level)
  Pallas kernels: 66.6 us -> 244 us
  local copies, waits for them, and re-layouts: 126 us -> 46.5 us
  blocking collectives: 62 us -> 0 us
  starting transfers between devices: 49.7 us -> 13.9 us
  matrix products: 14.9 us -> 3.51 us
  waiting for transfers between devices: 204 us -> 214 us
    pallas_call x0 -> x2, Pallas kernels: none -> 177 us  [spectral_call(): pl.pallas_call(spectral_kernel, out_shape=[shape(x.shape, BF), shape((3,...]
    psum x1 -> x2, waiting for transfers between devices: 147 us -> 210 us  [the longest x1 147 us: local(): late = lax.psum(late, ('lat', 'lon'))]
    all_to_all x3 -> x0, blocking collectives: 62 us -> none  [the longest x1 28.3 us: spectral(): lax.all_to_all(send, 'lon', 0, 0, tiled=True)]
    all_to_all x5 -> x0, waiting for transfers between devices: 36.7 us -> none  [the longest x1 18.3 us: spectral(): lax.all_to_all(send, 'lon', 0, 0, tiled=True)]
    all_to_all x5 -> x0, starting transfers between devices: 33.1 us -> none  [the longest x2 15.7 us: spectral(): lax.all_to_all(back.reshape(lon_parts, cells, rows * share), 'lon', 0, 0,...]
    convert_element_type x9 -> x0, local copies, waits for them, and re-layouts: 32.4 us -> none  [the longest x6 23.8 us: spectral(): modes = (modes.astype(F32) * scale_in).astype(BF)]
    reshape x12 -> x4, local copies, waits for them, and re-layouts: 29.8 us -> 5.41 us  [the longest x1 2.47 us: local(): table = table.reshape(3, 4 * degrees, lat_count)]
    ppermute x8, waiting for transfers between devices: 21 us -> 3.64 us  [ring(): return lax.ppermute(x, axis, pairs)]
  transfers between devices with their start and end apart: 14 -> 10, of which waited for: 6 -> 4; matrix products, arithmetic and copies ran while one was open for 7% -> 9% of each run, Pallas kernels for 9% -> 33%
where the time goes in v2:
time: 563 us; the launch traced here: 562 us
  Pallas kernels  244 us (43%)
  waiting for transfers between devices  214 us (38%)
  local copies, waits for them, and re-layouts  46.5 us (8%)
  other arithmetic  26.5 us (5%)
  between operations  14.5 us (3%)
  starting transfers between devices  13.9 us (2%)
    pallas_call x2, Pallas kernels, spectral_call(): pl.pallas_call(spectral_kernel, out_shape=[shape(x.shape, BF), shape((3,...  177 us
    psum x1, waiting for transfers between devices, local(): late = lax.psum(late, ('lat', 'lon'))  147 us
    psum x1, waiting for transfers between devices, local(): lax.psum(jnp.concatenate([grad_kernel_w, grad_out_w[None]]), ('lat', 'lon'))  63 us
    pallas_call x1, Pallas kernels, local(): call(functools.partial(stencil_backward, cells), [shape((rows, ROWS, chan...  26.7 us
    pallas_call x1, Pallas kernels, local(): call(functools.partial(stencil_forward, cells), shape((rows, ROWS, chans)...  21.6 us
    unnamed x59, local copies, waits for them, and re-layouts  17.8 us
    pallas_call x2, Pallas kernels, by_rows(): pl.pallas_call(body, grid=(args[0].shape[0] // group,), in_specs=[cut(a)...  16 us
    ppermute x8, starting transfers between devices, ring(): return lax.ppermute(x, axis, pairs)  13.8 us
  transfers between devices with their start and end apart: 10, of which 4 were waited for; matrix products, arithmetic and copies ran while one was open for 9% of the time, Pallas kernels for 33%

profile of v2, /device:TPU:1, one launch (start us, length us, event | category | flops | bytes accessed | tf_op | source)
XLA Modules:
  0.0 562.2 jit_solution(10987211847523330383)
XLA Ops:
  7.2 1.7 copy.79
  8.9 0.7 fusion.30
  9.7 1.4 collective-permute-start
  11.1 1.3 collective-permute-start.1
  13.0 3.2 negate_convert_fusion
  16.7 0.8 copy.104
  17.6 0.8 copy.103
  18.4 0.8 copy.106
  19.2 0.8 copy.105
  20.1 1.9 copy.87
  22.1 2.3 shard_map.112
  24.4 1.6 slice_bitcast_fusion
  26.1 0.8 dynamic-slice_bitcast_fusion
  26.9 1.9 pad_maximum_fusion.6
  28.9 3.5 convolution_convert_fusion
  32.4 0.8 pad_maximum_fusion.8
  33.4 0.7 pad.30.taps_ref
  34.1 1.8 copy.92
  36.0 0.9 copy.89.gain_ref
  36.9 0.6 copy.85
  37.5 1.0 convert_element_type.72
  38.5 1.3 copy.107
  39.9 1.4 pad.34.f_ref.field_ref
  41.3 0.9 pad.33.clone
  42.2 2.1 copy.88.into_ref
  44.3 1.9 reshape.319
  46.2 3.0 pad.31.x_ref
  49.5 1.5 pad.35.ct_ref
  51.0 0.8 copy-done.5
  52.2 2.5 copy.84
  54.7 1.7 fusion.6
  56.4 3.6 collective-permute-start.2
  60.0 1.5 collective-permute-start.3
  61.5 0.9 broadcast_in_dim.69.out_ref_scale.in_ref
  62.4 0.9 broadcast_in_dim.64.in_ref.out_ref_scale
  63.3 88.3 %shard_map.113 = (bf16[24,96,384]{2,1,0:T(8,128)(2,1)}, f32[3,192,384]{2,1,0:T(8,128)}) custom-call(bf16[24,96,384]{2,1,0:T(8,128)(2,1)} %pad.31.x_ref, bf16[3,768,384]{2,1,0:T(8,128)(2,1)} %bitcast.33, bf16[3,384,768]{2,1,0:T(8,128)(2,1)} %bitcast.37, bf16[384,768]{1,0:T(8,128)(2,1)} %copy.88.into_ref, bf16[768,384]{1,0:T(8,128)(2,1)} %bitcast.40, ...), custom_call_target="tpu_custom_call" | custom-call | tf_op jit(solution)/shard_map/pallas_call | solution.py:334
  151.6 3.8 fusion.2.ext_ref
  155.5 21.6 %shard_map.111.km_ref = f32[24,96,384]{2,1,0:T(8,128)} custom-call(bf16[26,128,384]{2,1,0:T(8,128)(2,1)} %fusion.2.ext_ref, f32[24,16,128]{2,1,0:T(8,128)} %pad.30.taps_ref, bf16[3,384,384]{2,1,0:T(8,128)(2,1)} %w_ref.2), custom_call_target="tpu_custom_call" | custom-call | tf_op jit(solution)/shard_map/pallas_call | solution.py:473
  177.1 8.4 %shard_map.114 = (bf16[24,90,384]{2,1,0:T(8,128)(2,1)}, bf16[24,96,384]{2,1,0:T(8,128)(2,1)}, f32[384,384]{1,0:T(8,128)}) custom-call(f32[24,96,384]{2,1,0:T(8,128)} %shard_map.111.km_ref, bf16[24,96,384]{2,1,0:T(8,128)(2,1)} %get-tuple-element.17.so_ref, bf16[24,96,384]{2,1,0:T(8,128)(2,1)} %pad.34.f_ref.field_ref, bf16[24,96,384]{2,1,0:T(8,128)(2,1)} %pad.35.ct_ref, ...), custom_call_target="tpu_custom_call" | custom-call | tf_op jit(solution)/shard_map/pallas_call | solution.py:424
  185.5 1.1 fusion.29
  186.6 1.7 collective-permute-start.5
  188.4 2.3 collective-permute-done.4
  190.7 2.2 fusion.7
  192.9 0.7 fusion.27
  193.6 2.8 collective-permute-start.6
  196.5 1.5 collective-permute-start.7
  198.0 2.2 copy.95
  200.1 0.7 pad.36.taps_ref
  200.8 1.3 collective-permute-done.7
  202.1 4.0 fusion.5.ext_ref
  206.1 26.7 %shard_map.115 = (f32[24,96,384]{2,1,0:T(8,128)}, f32[3,384,384]{2,1,0:T(8,128)}) custom-call(bf16[26,128,384]{2,1,0:T(8,128)(2,1)} %fusion.5.ext_ref, f32[24,16,128]{2,1,0:T(8,128)} %pad.36.taps_ref, bf16[3,384,384]{2,1,0:T(8,128)(2,1)} %bitcast.42, bf16[24,96,384]{2,1,0:T(8,128)(2,1)} %pad.34.f_ref.field_ref), custom_call_target="tpu_custom_call" | custom-call | tf_op jit(solution)/shard_map/pallas_call | solution.py:489
  232.8 3.1 pad_maximum_fusion.4
  236.0 0.9 copy.98
  236.9 88.9 %shard_map.116 = (bf16[24,96,384]{2,1,0:T(8,128)(2,1)}, f32[3,192,384]{2,1,0:T(8,128)}) custom-call(bf16[24,96,384]{2,1,0:T(8,128)(2,1)} %get-tuple-element.19.x_ref, bf16[3,768,384]{2,1,0:T(8,128)(2,1)} %bitcast.34, bf16[3,384,768]{2,1,0:T(8,128)(2,1)} %bitcast.38, bf16[384,768]{1,0:T(8,128)(2,1)} %copy.88.into_ref, bf16[768,384]{1,0:T(8,128)(2,1)} %bitcast.41, ...), custom_call_target="tpu_custom_call" | custom-call | tf_op jit(solution)/shard_map/pallas_call | solution.py:334
  325.8 1.3 multiply_reduce_fusion
  327.5 7.6 %shard_map.117 = (bf16[24,90,384]{2,1,0:T(8,128)(2,1)}, f32[384,384]{1,0:T(8,128)}) custom-call(f32[24,96,384]{2,1,0:T(8,128)} %get-tuple-element.20.adj_ref, bf16[24,96,384]{2,1,0:T(8,128)(2,1)} %get-tuple-element.21.gm_ref, bf16[24,96,384]{2,1,0:T(8,128)(2,1)} %pad.34.f_ref.field_ref, bf16[24,96,384]{2,1,0:T(8,128)(2,1)} %pad.35.ct_ref, ...), custom_call_target="tpu_custom_call" | custom-call | tf_op jit(solution)/shard_map/pallas_call | solution.py:424
  335.1 2.2 pad_maximum_fusion.5
  337.3 63.0 %all-reduce.11.cloned.1.call-done = f32[4,384,384]{2,1,0:T(8,128)} async-done(((f32[4,384,384]{2,1,0:T(8,128)}), f32[4,384,384]{2,1,0:T(8,128)}) %all-reduce.11.cloned.1.call-update) | async-done | bytes 2359312 | tf_op jit(solution)/shard_map/psum | solution.py:498
  400.4 1.7 copy.101
  402.1 1.7 copy.102
  403.9 146.8 %all-reduce.13.cloned.1.call-done = f32[576,384]{1,0:T(8,128)} async-done(((f32[576,384]{1,0:T(8,128)}), f32[576,384]{1,0:T(8,128)}) %all-reduce.13.cloned.1.call-update) | async-done | bytes 884752 | tf_op jit(solution)/shard_map/psum | solution.py:508
  550.7 1.1 slice_bitcast_fusion.1
  551.8 1.9 maximum_multiply_fusion
  553.7 1.7 slice.114
  (98 shorter events, 2.8 us)
Async XLA Ops:
  7.2 5.4 copy-start.22
  7.2 5.5 copy-start.21
  7.2 393.2 %all-reduce.11.cloned.1.call-start = ((), (), s32[]{:S(2)}) async-start(), calls=%async_computation | async-start | bytes 4718592 | tf_op jit(solution)/shard_map/psum | solution.py:498
  9.7 45.0 %collective-permute-start = (bf16[24,3,384]{2,1,0:T(4,128)(2,1)}, bf16[24,3,384]{2,1,0:T(4,128)(2,1)}, u32[]{:S(2)}, u32[]{:S(2)}) collective-permute-start(bf16[24,3,384]{2,1,0:T(4,128)(2,1)} %get-tuple-element.52), channel_id=1, source_target_pairs={{0,7},{1,0},{2,1},{3,2},{4,3},{5,4},{6,5},{7,6},{8,15},{9,8},{10,9... | collective-permute-start | bytes 165896 | tf_op jit(solution)/shard_map/ppermute | solution.py:28
  11.1 43.6 %collective-permute-start.1 = (bf16[24,3,384]{2,1,0:T(4,128)(2,1)}, bf16[24,3,384]{2,1,0:T(4,128)(2,1)}, u32[]{:S(2)}, u32[]{:S(2)}) collective-permute-start(bf16[24,3,384]{2,1,0:T(4,128)(2,1)} %get-tuple-element.53), channel_id=1, source_target_pairs={{0,1},{1,2},{2,3},{3,4},{4,5},{5,6},{6,7},{7,0},{8,9},{9,10},{10,1... | collective-permute-start | bytes 165896 | tf_op jit(solution)/shard_map/ppermute | solution.py:28
  28.8 3.5 copy-start.15
  28.8 3.5 copy-start.16
  28.9 3.5 copy-start.17
  28.9 3.5 copy-start.18
  32.4 4.5 copy-start.7
  39.9 1.4 copy-start.8
  39.9 4.4 copy-start.4
  46.2 3.0 copy-start.11
  49.5 2.3 copy-start.5
  52.2 4.2 copy-start
  54.7 136.0 %copy-start.2 = (bf16[24,32,384]{2,1,0:T(8,128)(2,1)}, bf16[24,32,384]{2,1,0:T(8,128)(2,1)S(1)}, u32[]{:S(2)}) copy-start(bf16[24,32,384]{2,1,0:T(8,128)(2,1)S(1)} %broadcast.352) | copy-start | bytes 1769476
  56.4 95.2 %collective-permute-start.2 = (bf16[1,128,384]{2,1,0:T(8,128)(2,1)S(1)}, bf16[1,128,384]{2,1,0:T(8,128)(2,1)S(1)}, u32[]{:S(2)}, u32[]{:S(2)}) collective-permute-start(bf16[1,128,384]{2,1,0:T(8,128)(2,1)S(1)} %get-tuple-element.48), channel_id=1, source_target_pairs={{0,8},{8,16},{16,24},{24,32},{32,40},{40,48},{48,56},{56,64},{64,7... | collective-permute-start | bytes 294920 | tf_op jit(solution)/shard_map/ppermute | solution.py:28
  60.0 91.6 %collective-permute-start.3 = (bf16[1,128,384]{2,1,0:T(8,128)(2,1)S(1)}, bf16[1,128,384]{2,1,0:T(8,128)(2,1)S(1)}, u32[]{:S(2)}, u32[]{:S(2)}) collective-permute-start(bf16[1,128,384]{2,1,0:T(8,128)(2,1)S(1)} %get-tuple-element.49), channel_id=1, source_target_pairs={{8,0},{16,8},{24,16},{32,24},{40,32},{48,40},{56,48},{64,56},{72,6... | collective-permute-start | bytes 294920 | tf_op jit(solution)/shard_map/ppermute | solution.py:28
  186.6 4.1 collective-permute-start.4
  186.6 4.1 collective-permute-start.5
  190.7 2.9 copy-start.20
  190.7 7.3 %copy-start.6 = (bf16[3,384,384]{2,1,0:T(8,128)(2,1)S(1)}, bf16[3,384,384]{2,1,0:T(8,128)(2,1)}, u32[]{:S(2)}) copy-start(bf16[3,384,384]{2,1,0:T(8,128)(2,1)} %w_ref.2) | copy-start | bytes 2654212
  190.7 9.4 %copy-start.14 = (f32[24,9,128]{2,1,0:T(8,128)S(1)}, f32[24,9,128]{2,1,0:T(8,128)}, u32[]{:S(2)}) copy-start(f32[24,9,128]{2,1,0:T(8,128)} %get-tuple-element.57) | copy-start | bytes 331780
  190.7 11.4 %copy-start.1 = (bf16[24,96,384]{2,1,0:T(8,128)(2,1)S(1)}, bf16[24,96,384]{2,1,0:T(8,128)(2,1)}, u32[]{:S(2)}) copy-start(bf16[24,96,384]{2,1,0:T(8,128)(2,1)} %get-tuple-element.19.x_ref) | copy-start | bytes 5308420
  192.9 9.2 %copy-start.3 = (bf16[24,32,384]{2,1,0:T(8,128)(2,1)S(1)}, bf16[24,32,384]{2,1,0:T(8,128)(2,1)}, u32[]{:S(2)}) copy-start(bf16[24,32,384]{2,1,0:T(8,128)(2,1)} %copy-done.2) | copy-start | bytes 1769476
  193.6 7.2 %collective-permute-start.6 = (bf16[1,128,384]{2,1,0:T(8,128)(2,1)}, bf16[1,128,384]{2,1,0:T(8,128)(2,1)}, u32[]{:S(2)}, u32[]{:S(2)}) collective-permute-start(bf16[1,128,384]{2,1,0:T(8,128)(2,1)} %get-tuple-element.46), channel_id=1, source_target_pairs={{0,8},{8,16},{16,24},{24,32},{32,40},{40,48},{48,56},{56,64},{64,7... | collective-permute-start | bytes 294920 | tf_op jit(solution)/shard_map/ppermute | solution.py:28
  196.5 5.7 %collective-permute-start.7 = (bf16[1,128,384]{2,1,0:T(8,128)(2,1)}, bf16[1,128,384]{2,1,0:T(8,128)(2,1)}, u32[]{:S(2)}, u32[]{:S(2)}) collective-permute-start(bf16[1,128,384]{2,1,0:T(8,128)(2,1)} %get-tuple-element.47), channel_id=1, source_target_pairs={{8,0},{16,8},{24,16},{32,24},{40,32},{48,40},{56,48},{64,56},{72,6... | collective-permute-start | bytes 294920 | tf_op jit(solution)/shard_map/ppermute | solution.py:28
  206.1 26.7 %copy-start.19 = (f32[384,384]{1,0:T(8,128)S(1)}, f32[384,384]{1,0:T(8,128)}, u32[]{:S(2)}) copy-start(f32[384,384]{1,0:T(8,128)} %get-tuple-element.27) | copy-start | bytes 1769476
  232.8 3.2 copy-start.12
  235.9 314.7 %all-reduce.13.cloned.1.call-start = ((), (), s32[]{:S(2)}) async-start(), calls=%async_computation.1 | async-start | bytes 1769472 | tf_op jit(solution)/shard_map/psum | solution.py:508
  236.9 88.9 %copy-start.13 = (f32[3,192,384]{2,1,0:T(8,128)S(1)}, f32[3,192,384]{2,1,0:T(8,128)}, u32[]{:S(2)}) copy-start(f32[3,192,384]{2,1,0:T(8,128)} %get-tuple-element.24) | copy-start | bytes 2654212
  335.1 65.3 %copy-start.9 = (bf16[24,90,384]{2,1,0:T(8,128)(2,1)S(1)}, bf16[24,90,384]{2,1,0:T(8,128)(2,1)}, u32[]{:S(2)}) copy-start(bf16[24,90,384]{2,1,0:T(8,128)(2,1)} %get-tuple-element.42) | copy-start | bytes 4976644
  337.3 64.8 %copy-start.10 = (bf16[24,90,384]{2,1,0:T(8,128)(2,1)S(1)}, bf16[24,90,384]{2,1,0:T(8,128)(2,1)}, u32[]{:S(2)}) copy-start(bf16[24,90,384]{2,1,0:T(8,128)(2,1)} %get-tuple-element.43) | copy-start | bytes 4976644
  403.9 147.9 %slice-start = ((f32[4,384,384]{2,1,0:T(8,128)}), f32[1,384,384]{2,1,0:T(8,128)S(1)}, s32[]{:S(2)}) async-start(f32[4,384,384]{2,1,0:T(8,128)} %all-reduce.11.cloned.1.call-done), calls=%async_computation.2 | async-start | bytes 1179648 | tf_op jit(solution)/shard_map/slice | solution.py:509
  403.9 147.9 %slice-start.1 = ((f32[4,384,384]{2,1,0:T(8,128)}), f32[3,384,384]{2,1,0:T(8,128)S(1)}, s32[]{:S(2)}) async-start(f32[4,384,384]{2,1,0:T(8,128)} %all-reduce.11.cloned.1.call-done), calls=%async_computation.3 | async-start | bytes 3538944 | tf_op jit(solution)/shard_map/slice | solution.py:509
Sparse Core Ops, SparseCore 0:
  236.0 164.2 all-reduce.10
  405.8 144.7 all-reduce.12

commit v3 on v2

v3 whole, which is shorter than its diff:
```python
import functools
import math

import jax
import jax.numpy as jnp
import numpy as np
from jax import lax
from jax.experimental import pallas as pl
from jax.experimental.pallas import tpu as pltpu
from jax.sharding import PartitionSpec as P

ORDERS = 192
BF = jnp.bfloat16
F32 = jnp.float32
VMEM = pl.BlockSpec(memory_space=pltpu.VMEM)
ROWS = 96
EXT = 128


def dot(a, b, dims=((1,), (0,))):
    return lax.dot_general(a, b, (dims, ((), ())), preferred_element_type=F32)


def tap_rows(taps):
    k, r, t, n = taps.shape
    flat = jnp.transpose(taps, (3, 0, 1, 2)).reshape(n, k * r, t)
    wide = jnp.concatenate([flat[:, :, 3:], jnp.zeros((n, k * r, EXT - t), F32), flat[:, :, :3]], axis=2)
    return jnp.pad(wide, ((0, 0), (0, 16 - k * r), (0, 0)))


def band_matrix(taps_ref, i, band_ref, cells):
    keep = lax.broadcasted_iota(jnp.int32, (ROWS, EXT), 0) < cells
    rows = taps_ref[i]
    for k in range(3):
        for r in range(3):
            row = jnp.broadcast_to(rows[3 * k + r : 3 * k + r + 1], (ROWS, EXT))
            block = pltpu.roll(row, 0, 1, stride=1, stride_axis=0)
            band_ref[k * ROWS : (k + 1) * ROWS, r * EXT : (r + 1) * EXT] = jnp.where(keep, block, 0.0).astype(BF)


def padded(pad_ref, ref, cells):
    pad_ref[:, 80:] = jnp.zeros_like(pad_ref[:, 80:])
    pad_ref[:, :cells] = ref[...]
    return pad_ref[...].reshape(-1, pad_ref.shape[2])


def pointwise(cells, km_ref, so_ref, f_ref, ct_ref, w_ref, wt_ref, out_ref, gp_ref, gow_ref, pad_ref):
    @pl.when(pl.program_id(0) == 0)
    def _():
        gow_ref[...] = jnp.zeros_like(gow_ref)

    group, rows, chans = km_ref.shape
    v = (km_ref[...] + so_ref[...].astype(F32)).reshape(group * rows, chans)
    ct = padded(pad_ref, ct_ref, cells)
    square = v * v
    s = jnp.tanh(0.7978845608 * v * (1.0 + 0.044715 * square))
    half = 0.5 * (1.0 + s)
    hidden = (v * half).astype(BF)
    slope = half + 0.5 * v * (1.0 - s * s) * (0.7978845608 * (1.0 + 3.0 * 0.044715 * square))
    mixed = dot(hidden, w_ref[...]).reshape(km_ref.shape)[:, :cells]
    out_ref[...] = (f_ref[...].astype(F32) + mixed).astype(BF)
    gp_ref[...] = (dot(ct, wt_ref[...]) * slope).astype(BF).reshape(km_ref.shape)
    gow_ref[...] += dot(hidden, ct, ((0,), (0,)))


def block_swap(parts):
    group = lax.broadcasted_iota(jnp.int32, parts[0].shape, 1) // 16
    for k in range(3):
        high = (group >> k) & 1 == 1
        width = 16 << k
        fresh = list(parts)
        for a in range(8):
            if (a >> k) & 1 == 0:
                b = a + (1 << k)
                fresh[a] = jnp.where(high, pltpu.roll(parts[b], width, 1), parts[a])
                fresh[b] = jnp.where(high, parts[b], pltpu.roll(parts[a], 128 - width, 1))
        parts = fresh
    return parts


def tile_swap(x):
    row = lax.broadcasted_iota(jnp.int32, x.shape, 1)
    group = lax.broadcasted_iota(jnp.int32, x.shape, 2) // 16
    for k in range(3):
        row_bit = (row >> k) & 1
        group_bit = (group >> k) & 1
        width = 16 << k
        down = pltpu.roll(pltpu.roll(x, 8 - (1 << k), 1), width, 2)
        up = down if k == 2 else pltpu.roll(pltpu.roll(x, 1 << k, 1), 128 - width, 2)
        x = jnp.where(row_bit == group_bit, x, jnp.where(group_bit == 1, down, up))
    return x


PAD = 80
MESH = pl.DeviceIdType.MESH


def transfer(axis, me, parts, source, target, send_sem, recv_sem):
    def copy(peer, slot):
        return pltpu.make_async_remote_copy(
            src_ref=source(peer),
            dst_ref=target(slot),
            send_sem=send_sem(peer),
            recv_sem=recv_sem(slot),
            device_id={axis: peer},
            device_id_type=MESH,
        )

    def over(body):
        lax.fori_loop(1, parts, lambda d, carry: (body(lax.rem(me + d, parts)), carry)[1], 0)

    def start():
        over(lambda peer: copy(peer, me).start())

    def arrive():
        over(lambda peer: copy(peer, peer).wait_recv())

    def drain():
        over(lambda peer: copy(peer, peer).wait_send())

    return start, arrive, drain


def greet():
    barrier = pltpu.get_barrier_semaphore()
    total = 0
    for axis in ("lon", "lat"):
        me, parts = lax.axis_index(axis), lax.axis_size(axis)

        def body(d, carry, axis=axis, me=me, parts=parts):
            pl.semaphore_signal(barrier, inc=1, device_id={axis: lax.rem(me + d, parts)}, device_id_type=MESH)
            return carry

        lax.fori_loop(1, parts, body, 0)
        total += parts - 1
    return lambda: pl.semaphore_wait(barrier, total)


def reducer(flat, got1, part, got2, whole, sems):
    s1, r1, s2, r2, s3, r3 = sems
    lat, lon = lax.axis_index("lat"), lax.axis_index("lon")
    lats, lons = lax.axis_size("lat"), lax.axis_size("lon")
    n = part.shape[0]

    def block(ref, b):
        return ref.at[pl.ds(pl.multiple_of(b * n, 16), n)]

    first = transfer("lat", lat, lats, lambda p: block(flat, p), lambda s: got1.at[s], lambda p: s1.at[p], lambda s: r1.at[s])
    second = transfer("lon", lon, lons, lambda p: part, lambda s: got2.at[s], lambda p: s2.at[p], lambda s: r2.at[s])
    third = transfer(
        "lat", lat, lats, lambda p: block(whole, lat), lambda s: block(whole, s), lambda p: s3.at[p], lambda s: r3.at[s]
    )

    def total(ref):
        add = lambda s, carry: carry + ref[s].astype(F32)
        return lax.fori_loop(1, ref.shape[0], add, ref[0].astype(F32)).astype(BF)

    def begin():
        first[0]()
        got1[lat] = flat[pl.ds(pl.multiple_of(lat * n, 16), n)]

    def across():
        first[1]()
        part[...] = total(got1)
        second[0]()
        got2[lon] = part[...]

    def spread():
        second[1]()
        whole[pl.ds(pl.multiple_of(lat * n, 16), n)] = total(got2)
        third[0]()

    def end():
        third[1]()
        for t in (first, second, third):
            t[2]()

    return begin, across, spread, end


def reducer_scratch(lats, lons, n):
    lat_sem, lon_sem = pltpu.SemaphoreType.DMA((lats,)), pltpu.SemaphoreType.DMA((lons,))
    return [
        pltpu.VMEM((lats * n, 128), BF),
        pltpu.VMEM((lats, n, 128), BF),
        pltpu.VMEM((n, 128), BF),
        pltpu.VMEM((lons, n, 128), BF),
        pltpu.VMEM((lats * n, 128), BF),
        lat_sem, lat_sem, lon_sem, lon_sem, lat_sem, lat_sem,
    ]


EARLY = 288
LATE = 112


def pass_kernel(forward, cells, *refs):
    refs = list(refs)

    def take(n):
        head = refs[:n]
        del refs[:n]
        return head

    x_ref, table_ref, turned_ref, into_ref, back_ref, gain_ref, in_scale, out_scale, taps_ref, kernel_ref = take(10)
    if forward:
        (mix_ref,) = take(1)
        grid_ref, stencil_ref, bands_ref = take(3)
    else:
        field_ref, gow_ref, bands_ref = take(3)
        grid_ref, stencil_ref, early_ref, gain_out = take(4)
    send1, recv1, send2, recv2, send3, recv3, send4, recv4 = take(8)
    modes, rows_ref, ext, from_left, from_right, band_ref, spare = take(7)
    s1, r1, s2, r2, s3, r3, s4, r4, hs, hr = take(10)
    if not forward:
        part_ref, pad_ref, grad_ref = take(3)
        red = take(11)
        begin, across, spread, end = reducer(*red[:5], red[5:])
    lat, lon = lax.axis_index("lat"), lax.axis_index("lon")
    lons, lats = lax.axis_size("lon"), lax.axis_size("lat")
    rows = x_ref.shape[0]
    chans = x_ref.shape[2]
    enter = greet()

    def way(axis, me, parts, send, recv, ss, rs):
        def at(v):
            start, arrive, drain = transfer(
                axis, me, parts,
                lambda p: send.at[v, p], lambda s: recv.at[v, s], lambda p: ss.at[v, p], lambda s: rs.at[v, s],
            )

            def go():
                start()
                recv[v, me] = send[v, me]

            return go, arrive, drain

        return [at(v) for v in range(3)]

    lon_in = way("lon", lon, lons, send1, recv1, s1, r1)
    lat_in = way("lat", lat, lats, send2, recv2, s2, r2)
    lat_out = way("lat", lat, lats, send3, recv3, s3, r3)
    lon_out = way("lon", lon, lons, send4, recv4, s4, r4)
    order = lax.broadcasted_iota(jnp.int32, (192, 128), 1) // 32
    lane_group = lax.broadcasted_iota(jnp.int32, (192, 128), 1) // 16
    blank = jnp.zeros((8, 128), F32)

    def sideways(source, target, n, step):
        return pltpu.make_async_remote_copy(
            src_ref=source, dst_ref=target, send_sem=hs.at[n], recv_sem=hr.at[n],
            device_id={"lon": lax.rem(lon + step + lons, lons)}, device_id_type=MESH,
        )

    def vertical(source, target, n, step):
        return pltpu.make_async_remote_copy(
            src_ref=source, dst_ref=target, send_sem=hs.at[n], recv_sem=hr.at[n],
            device_id={"lat": lax.rem(lat + step + lats, lats)}, device_id_type=MESH,
        )

    to_right = sideways(ext.at[pl.ds(1, rows), pl.ds(80, 16)], from_left, 0, 1)
    to_left = sideways(ext.at[pl.ds(1, rows), pl.ds(0, 16)], from_right, 1, -1)
    to_below = vertical(ext.at[rows], ext.at[0], 2, 1)
    to_above = vertical(ext.at[1], ext.at[rows + 1], 3, -1)

    def fill(i, carry):
        if forward:
            ext[1 + i, 80:96] = jnp.zeros((16, chans), BF)
        ext[1 + i, : x_ref.shape[1]] = x_ref[i]
        return carry

    def halo_columns():
        for c in (to_right, to_left):
            c.wait()
        place = lax.broadcasted_iota(jnp.int32, (16, chans), 0)

        def step(i, carry):
            own = ext[1 + i, 80:96].astype(F32)
            right = pltpu.roll(from_right[i].astype(F32), 10, 0)
            left = pltpu.roll(from_left[i].astype(F32), 6, 0)
            ext[1 + i, 80:96] = jnp.where(place < 10, own, jnp.where(place < 13, right, 0.0)).astype(BF)
            ext[1 + i, 96:112] = jnp.zeros((16, chans), BF)
            ext[1 + i, 112:128] = jnp.where(place >= 13, left, 0.0).astype(BF)
            return carry

        lax.fori_loop(0, rows, step, 0)

        @pl.when(lat < lats - 1)
        def _():
            to_below.start()

        @pl.when(lat > 0)
        def _():
            to_above.start()

        @pl.when(lat == 0)
        def _():
            ext[0] = jnp.zeros((EXT, chans), BF)

        @pl.when(lat == lats - 1)
        def _():
            ext[rows + 1] = jnp.zeros((EXT, chans), BF)

    def halo_rows():
        @pl.when(lat > 0)
        def _():
            to_below.wait_recv()

        @pl.when(lat < lats - 1)
        def _():
            to_above.wait_recv()

    def halo_drain():
        @pl.when(lat < lats - 1)
        def _():
            to_below.wait_send()

        @pl.when(lat > 0)
        def _():
            to_above.wait_send()

    def stencil(first):
        def step(a, carry):
            i = first + a
            band_matrix(taps_ref, i, band_ref, cells)
            source = ext[pl.ds(i, 3)].reshape(3 * EXT, chans)
            total = None
            for k in range(3):
                part = dot(band_ref[k * ROWS : (k + 1) * ROWS], source).astype(BF)
                if not forward:
                    part_ref[k, a] = part
                part = dot(part, kernel_ref[k])
                total = part if total is None else total + part
            stencil_ref[i] = total
            if not forward:
                pad_ref[a, 80:96] = jnp.zeros((16, chans), BF)
                pad_ref[a, :cells] = field_ref[i]
            return carry

        lax.fori_loop(0, 4, step, 0)
        if not forward:
            own = pad_ref[...].reshape(4 * ROWS, chans)
            for k in range(3):
                add = dot(own, part_ref[k].reshape(4 * ROWS, chans), ((0,), (0,)))
                grad_ref[k] = add if first == START else grad_ref[k] + add

    def tiles(body):
        def step(n, carry):
            body(n // 6, pl.multiple_of(n % 6 * 16, 16))
            return carry

        lax.fori_loop(0, 18, step, 0)

    def split(v):
        lanes_v = slice(v * 128, (v + 1) * 128)
        if forward:
            def mix(g, carry):
                block = ext[pl.ds(1 + g * 8, 8), 0:ROWS].reshape(8 * ROWS, chans)
                spare[pl.ds(g * 8, 8)] = dot(block, mix_ref[:, lanes_v]).reshape(8, ROWS, 128)
                return carry

            lax.fori_loop(0, 3, mix, 0)

        def body(g, j):
            if forward:
                parts = [spare[g * 8 + n, pl.ds(j, 16)] for n in range(8)]
            else:
                parts = [ext[1 + g * 8 + n, pl.ds(j, 16), lanes_v].astype(F32) for n in range(8)]
            lanes = pl.ds(pl.multiple_of(g * 128, 128), 128)
            for p, part in enumerate(block_swap(parts)):
                send1[v, p, pl.ds(j, 16), lanes] = part.astype(BF)

        tiles(body)
        lon_in[v][0]()

    def analyse(v):
        lon_in[v][1]()
        modes[...] = dot(into_ref[...], recv1[v].reshape(lons * ROWS, 384))

        def step(b, carry):
            block = modes[pl.ds(pl.multiple_of(b * 24, 8), 24), :]
            turned = [tile_swap(block[:, g * 128 : (g + 1) * 128].reshape(3, 8, 128)) for g in range(3)]
            pieces = [turned[g][o] for o in range(3) for g in range(3)] + [blank]
            send2[v, b] = jnp.concatenate(pieces, axis=0).astype(BF)
            return carry

        lax.fori_loop(0, lats, step, 0)
        lat_in[v][0]()

    def filter_bands(v):
        lat_in[v][1]()
        lanes = slice(v * 128, (v + 1) * 128)

        def gather(b, carry):
            at = pl.ds(pl.multiple_of(b * 24, 8), 24)
            block = recv2[v, b].astype(F32)
            for o in range(3):
                rows_ref[o, at] = block[o * 24 : (o + 1) * 24] * in_scale[o, at]
            return carry

        lax.fori_loop(0, lats, gather, 0)
        gain_sum = None
        for o in range(3):
            every = dot(table_ref[o], rows_ref[o].astype(BF))
            band = every[:192]
            for m in range(1, 4):
                band = jnp.where(order == m, every[m * 192 : (m + 1) * 192], band)
            if forward:
                bands_ref[o, :, lanes] = band
            else:
                term = band * bands_ref[o, :, lanes]
                gain_sum = term if gain_sum is None else gain_sum + term
            band = band * gain_ref[:, lanes]
            spread_out = jnp.concatenate([jnp.where(order == m, band, 0.0).astype(BF) for m in range(4)], axis=0)
            rows_ref[o] = dot(turned_ref[o], spread_out) * out_scale[o]

        def scatter(b, carry):
            at = pl.ds(pl.multiple_of(b * 24, 8), 24)
            send3[v, b] = jnp.concatenate([rows_ref[o, at] for o in range(3)] + [blank], axis=0).astype(BF)
            return carry

        lax.fori_loop(0, lats, scatter, 0)
        lat_out[v][0]()
        if not forward:
            for width in (16, 32, 64):
                gain_sum = gain_sum + pltpu.roll(gain_sum, width, 1)
            gain_out[:, lanes] = jnp.where(lane_group == lon, gain_sum, 0.0)

    def synthesise(v):
        lat_out[v][1]()

        def step(b, carry):
            turned = tile_swap(recv3[v, b].astype(F32)[:72].reshape(9, 8, 128))
            wide = [jnp.concatenate([turned[o * 3 + g] for o in range(3)], axis=0) for g in range(3)]
            modes[pl.ds(pl.multiple_of(b * 24, 8), 24), :] = jnp.concatenate(wide, axis=1)
            return carry

        lax.fori_loop(0, lats, step, 0)
        send4[v] = dot(back_ref[...], modes[...].astype(BF)).astype(BF).reshape(lons, ROWS, 384)
        lon_out[v][0]()

    def join(v):
        lon_out[v][1]()

        def body(g, j):
            lanes = pl.ds(pl.multiple_of(g * 128, 128), 128)
            parts = [recv4[v, p, pl.ds(j, 16), lanes].astype(F32) for p in range(8)]
            for n, part in enumerate(block_swap(parts)):
                grid_ref[g * 8 + n, pl.ds(j, 16), v * 128 : (v + 1) * 128] = part.astype(BF)

        tiles(body)

    def early_begin():
        flat = red[0]
        for k in range(4):
            for v in range(3):
                block = (grad_ref[k] if k < 3 else gow_ref[...])[:, v * 128 : (v + 1) * 128]
                flat[(k * 3 + v) * 384 : (k * 3 + v + 1) * 384] = block.astype(BF)
        begin()

    def early_end():
        end()
        whole = red[4]
        for k in range(4):
            for v in range(3):
                early_ref[k, :, v * 128 : (v + 1) * 128] = whole[(k * 3 + v) * 384 : (k * 3 + v + 1) * 384].astype(F32)

    lax.fori_loop(0, rows, fill, 0)
    enter()
    to_right.start()
    to_left.start()
    for v in range(3):
        split(v)
    halo_columns()
    START = 4
    stencil(4)
    stencil(8)
    analyse(0)
    stencil(12)
    filter_bands(0)
    analyse(1)
    stencil(16)
    synthesise(0)
    filter_bands(1)
    halo_rows()
    if not forward:
        stencil(20)
        stencil(0)
        early_begin()
    analyse(2)
    if forward:
        stencil(20)
    synthesise(1)
    filter_bands(2)
    if not forward:
        across()
    if forward:
        stencil(0)
    join(0)
    synthesise(2)
    if not forward:
        spread()
    join(1)
    join(2)
    if not forward:
        early_end()
    halo_drain()
    for road in (lon_in, lat_in, lat_out, lon_out):
        for v in range(3):
            road[v][2]()


def pass_call(forward, cells, args, outs):
    lons, lats = lax.axis_size("lon"), lax.axis_size("lat")
    rows, _, chans = args[0].shape
    lon_buf = pltpu.VMEM((3, lons, ROWS, 384), BF)
    lat_buf = pltpu.VMEM((3, lats, PAD, 128), BF)
    lon_sem = pltpu.SemaphoreType.DMA((3, lons))
    lat_sem = pltpu.SemaphoreType.DMA((3, lats))
    scratch = [lon_buf, lon_buf] + [lat_buf] * 4 + [lon_buf, lon_buf]
    scratch += [
        pltpu.VMEM((384, 384), F32),
        pltpu.VMEM((3, 384, 128), F32),
        pltpu.VMEM((rows + 2, EXT, chans), BF),
        pltpu.VMEM((rows, 16, chans), BF),
        pltpu.VMEM((rows, 16, chans), BF),
        pltpu.VMEM((3 * ROWS, 3 * EXT), BF),
        pltpu.VMEM((rows, ROWS, 128) if forward else (8, 128), F32),
    ]
    scratch += [lon_sem, lon_sem, lat_sem, lat_sem, lat_sem, lat_sem, lon_sem, lon_sem]
    scratch += [pltpu.SemaphoreType.DMA((4,)), pltpu.SemaphoreType.DMA((4,))]
    if not forward:
        scratch += [pltpu.VMEM((3, 4, ROWS, chans), BF), pltpu.VMEM((4, ROWS, chans), BF), pltpu.VMEM((3, chans, chans), F32)]
        scratch += reducer_scratch(lats, lons, EARLY)
    return pl.pallas_call(
        functools.partial(pass_kernel, forward, cells),
        out_shape=outs,
        in_specs=[VMEM] * len(args),
        out_specs=[VMEM] * len(outs),
        scratch_shapes=scratch,
        compiler_params=pltpu.CompilerParams(
            collective_id=1 if forward else 2, has_side_effects=True, vmem_limit_bytes=60 << 20
        ),
    )(*args)


def finish(cells, adj_ref, gm_ref, f_ref, ct_ref, wt_ref, gain_ref, out_ref, gmw_ref, gain_out, pad_ref, *red):
    begin, across, spread, end = reducer(*red[:5], red[5:])
    flat, whole = red[0], red[4]
    enter = greet()
    rows, chans = adj_ref.shape[0], adj_ref.shape[2]
    group = pad_ref.shape[0]

    def weigh(n, carry):
        some = pl.ds(n * group, group)
        own = padded(pad_ref, f_ref.at[some], cells)
        add = dot(own, gm_ref[some].reshape(group * ROWS, chans), ((0,), (0,)))
        gmw_ref[...] = gmw_ref[...] + add
        return carry

    gmw_ref[...] = jnp.zeros_like(gmw_ref)
    lax.fori_loop(0, rows // group, weigh, 0)
    for v in range(3):
        lanes = slice(v * 128, (v + 1) * 128)
        flat[v * 576 : v * 576 + 384] = gmw_ref[:, lanes].astype(BF)
        flat[v * 576 + 384 : (v + 1) * 576] = gain_ref[:, lanes].astype(BF)
    flat[1728:] = jnp.zeros((64, 128), BF)
    enter()
    begin()

    def field_rows(first):
        def step(n, carry):
            some = pl.ds(first + n * group, group)
            add = adj_ref[some] + dot(gm_ref[some].reshape(group * ROWS, chans), wt_ref[...]).reshape(group, ROWS, chans)
            out_ref[some] = (ct_ref[some].astype(F32) + add[:, :cells]).astype(BF)
            return carry

        lax.fori_loop(0, 2, step, 0)

    field_rows(0)
    across()
    field_rows(8)
    spread()
    field_rows(16)
    end()
    for v in range(3):
        lanes = slice(v * 128, (v + 1) * 128)
        gmw_ref[:, lanes] = whole[v * 576 : v * 576 + 384].astype(F32)
        gain_out[:, lanes] = whole[v * 576 + 384 : (v + 1) * 576].astype(F32)


def fourier_tables(lon_count, cells, lat_parts):
    j = np.arange(lon_count)
    angles = (j[:, None] * np.arange(ORDERS)[None, :] % lon_count) * (2.0 * np.pi / lon_count)
    waves = np.stack([np.cos(angles), -np.sin(angles)], axis=-1).reshape(lon_count // cells, cells, 2 * ORDERS)
    waves = np.pad(waves, ((0, 0), (0, ROWS - cells), (0, 0))).reshape(-1, 2 * ORDERS)
    return jnp.asarray(waves.T, BF), jnp.asarray(waves, BF)


def legendre_kernel(m_ref, x_ref, diag_ref, out_ref):
    m = m_ref[...]
    x = x_ref[...]
    diag = diag_ref[...]
    reps = x.shape[1] // m.shape[1]

    def wide(a):
        return jnp.concatenate([a] * reps, axis=1)

    mw = wide(m)

    def step(l, carry):
        prev, before, a_prev = carry
        lf = l.astype(F32)
        above = lf > m
        den = jnp.where(above, lf * lf - m * m, 1.0)
        a = jnp.where(above, jnp.sqrt((4.0 * lf * lf - 1.0) / den), 1.0)
        cur = wide(a) * (x * prev - before * wide(1.0 / a_prev))
        cur = jnp.where(lf == mw, diag, jnp.where(lf > mw, cur, 0.0))
        out_ref[l] = cur.astype(BF)
        return cur, prev, a

    blank = x * 0.0
    lax.fori_loop(0, out_ref.shape[0], step, (blank, blank, m * 0.0 + 1.0), unroll=4)


def colatitudes(row_index, lat_count):
    return (row_index.astype(F32) + 0.5) * (math.pi / lat_count)


def legendre_rows(orders, lat_count, degrees):
    slots = 16
    m = jnp.pad(orders, (0, slots - orders.shape[0])).astype(F32)[:, None]
    colat = colatitudes(jnp.arange(lat_count, dtype=jnp.int32), lat_count)[None, :]
    log_start = 0.5 * (lax.lgamma(m + 1.5) - lax.lgamma(m + 1.0) - lax.lgamma(F32(1.5) + 0.0 * m))
    diag = jnp.exp(log_start + m * jnp.log(jnp.sin(colat))) / math.sqrt(4.0 * math.pi)
    x = jnp.broadcast_to(jnp.cos(colat), diag.shape)
    table = pl.pallas_call(
        legendre_kernel,
        out_shape=jax.ShapeDtypeStruct((degrees, slots, lat_count), BF),
        in_specs=[VMEM] * 3,
        out_specs=VMEM,
        compiler_params=pltpu.CompilerParams(vmem_limit_bytes=40 << 20),
    )(jnp.broadcast_to(m, (slots, 128)), x, diag)
    return jnp.transpose(table[:, : orders.shape[0]], (1, 0, 2))


def tap_table(kernel_basis, lon_reach):
    count = kernel_basis.shape[2]
    offsets = jnp.abs(jnp.arange(count, dtype=jnp.int32) - count // 2)
    mask = offsets[None, :, None] <= lon_reach[:, None, :]
    return kernel_basis * mask[None].astype(F32)


def by_rows(body, args, whole, outs, totals, scratch, group=4):
    def cut(a):
        return pl.BlockSpec((group,) + a.shape[1:], lambda g: (g, 0, 0))

    def full(a):
        return pl.BlockSpec(a.shape, lambda g: (0,) * len(a.shape))

    return pl.pallas_call(
        body,
        grid=(args[0].shape[0] // group,),
        in_specs=[cut(a) for a in args] + [full(a) for a in whole],
        out_specs=[cut(a) for a in outs] + [full(a) for a in totals],
        out_shape=list(outs) + list(totals),
        scratch_shapes=scratch,
        compiler_params=pltpu.CompilerParams(vmem_limit_bytes=56 << 20),
    )(*args, *whole)


def local(field, cotangent, kernel_weights, spectral_weight, out_weight, degree_gain, kernel_basis, lon_reach):
    rows, cells, chans = field.shape
    lat_parts, lon_parts = lax.axis_size("lat"), lax.axis_size("lon")
    lat, lon = lax.axis_index("lat"), lax.axis_index("lon")
    lat_count, lon_count = rows * lat_parts, cells * lon_parts
    degrees = degree_gain.shape[0]
    slots = ORDERS // lat_parts
    shape = jax.ShapeDtypeStruct

    taps = tap_table(kernel_basis, lon_reach)
    near = lax.dynamic_slice_in_dim(jnp.pad(taps, ((0, 0), (0, 0), (0, 0), (1, 1))), lat * rows, rows + 2, 3)
    own_taps = tap_rows(near[:, :, :, 1 : rows + 1])
    turned = near[:, ::-1, ::-1]
    adj_taps = tap_rows(jnp.stack([turned[:, r, :, r : r + rows] for r in range(3)], axis=1))

    my_orders = lat * slots + jnp.arange(slots, dtype=jnp.int32)
    table = legendre_rows(my_orders, lat_count, degrees)
    into, back = fourier_tables(lon_count, cells, lat_parts)
    table = table.reshape(3, 4 * degrees, lat_count)
    turned = jnp.transpose(table, (0, 2, 1))
    quad = 2.0 * math.pi / lon_count * (math.pi / lat_count) * jnp.sin(
        colatitudes(jnp.arange(lat_count, dtype=jnp.int32), lat_count)
    )
    quad = jnp.broadcast_to(quad[None, :, None], (3, lat_count, 128))
    mode_weight = jnp.where(my_orders == 0, 1.0, 2.0).astype(F32).reshape(3, 1, 4, 1)
    mode_weight = jnp.broadcast_to(mode_weight, (3, lat_count, 4, 32)).reshape(3, lat_count, 128)
    groups = degree_gain.reshape(degrees, 3, lon_parts, 16)
    gain = lax.dynamic_slice_in_dim(groups, lon, 1, 2)
    gain = jnp.broadcast_to(gain, groups.shape).reshape(degrees, chans)

    shared = [table, turned, into, back, gain]
    wide = (rows, ROWS, chans)
    spec_out, kernel_mix, bands = pass_call(
        True,
        cells,
        [field, *shared, quad, mode_weight, own_taps, kernel_weights, spectral_weight],
        [shape(wide, BF), shape(wide, F32), shape((3, degrees, chans), F32)],
    )
    output_field, grad_pre, grad_out_w = by_rows(
        functools.partial(pointwise, cells),
        [kernel_mix, spec_out, field, cotangent],
        [out_weight, out_weight.T],
        [shape(field.shape, BF), shape(wide, BF)],
        [shape((chans, chans), F32)],
        [pltpu.VMEM((4, ROWS, chans), BF)],
    )
    turned_weights = jnp.transpose(kernel_weights, (0, 2, 1))
    grad_mixed, adj, early, gain_place = pass_call(
        False,
        cells,
        [grad_pre, *shared, mode_weight, quad, adj_taps, turned_weights, field, grad_out_w, bands],
        [shape(wide, BF), shape(wide, F32), shape((4, chans, chans), F32), shape((degrees, chans), F32)],
    )
    grad_field, grad_mix_w, gain_total = pl.pallas_call(
        functools.partial(finish, cells),
        out_shape=[shape(field.shape, BF), shape((chans, chans), F32), shape((degrees, chans), F32)],
        in_specs=[VMEM] * 6,
        out_specs=[VMEM] * 3,
        scratch_shapes=[pltpu.VMEM((4, ROWS, chans), BF)] + reducer_scratch(lat_parts, lon_parts, LATE),
        compiler_params=pltpu.CompilerParams(collective_id=3, has_side_effects=True, vmem_limit_bytes=56 << 20),
    )(adj, grad_mixed, field, cotangent, spectral_weight.T, gain_place)
    weight_grads = jnp.concatenate([early[:3], grad_mix_w[None], early[3:]]) / math.sqrt(lat_count * lon_count)
    return output_field, grad_field, weight_grads, gain_total


def solution(mesh):
    placed = (P("lat", "lon", None), P("lat", "lon", None), P(), P(), P(), P(), P(), P())
    return jax.shard_map(
        local,
        mesh=mesh,
        in_specs=placed,
        out_specs=(P("lat", "lon", None), P("lat", "lon", None), P(), P()),
        check_vma=False,
    )
```

time: 563 us -> 296 us (0.53)
  waiting for transfers between devices: 214 us -> 0 us
  other arithmetic: 26.5 us -> 2.46 us
  Pallas kernels: 244 us -> 267 us
  local copies, waits for them, and re-layouts: 46.5 us -> 25.5 us
  starting transfers between devices: 13.9 us -> 0 us
  between operations: 14.5 us -> 0.91 us
    psum x2 -> x0, waiting for transfers between devices: 210 us -> none  [the longest x1 147 us: local(): late = lax.psum(late, ('lat', 'lon'))]
    pallas_call x4 -> x3, Pallas kernels: 225 us -> 256 us  [the longest x2 223 us: pass_call(): pl.pallas_call(functools.partial(pass_kernel, forward, cells), out_shape=...]
    concatenate x6 -> x0, other arithmetic: 16.9 us -> none  [the longest x2 7.8 us: extend(): return jnp.concatenate([above, wide, below], axis=0)]
    ppermute x8 -> x0, starting transfers between devices: 13.8 us -> none  [ring(): return lax.ppermute(x, axis, pairs)]
    pallas_call x2 -> x1, Pallas kernels: 16 us -> 8.44 us  [by_rows(): pl.pallas_call(body, grid=(args[0].shape[0] // group,), in_specs=[cut(a)...]
    pad x4 -> x0, local copies, waits for them, and re-layouts: 6.77 us -> none  [the longest x1 3.01 us: local(): spec_out, bands = spectral(jnp.pad(mixed, padding), quad, mode_weight)]
    unnamed x59 -> x35, local copies, waits for them, and re-layouts: 17.8 us -> 17.4 us
  transfers between devices with their start and end apart: 10 -> 0, of which waited for: 4 -> 0; matrix products, arithmetic and copies ran while one was open for 9% -> 0% of each run, Pallas kernels for 33% -> 0%
where the time goes in v3:
time: 296 us; the launch traced here: 295 us
  Pallas kernels  267 us (90%)
  local copies, waits for them, and re-layouts  25.5 us (9%)
    pallas_call x2, Pallas kernels, pass_call(): pl.pallas_call(functools.partial(pass_kernel, forward, cells), out_shape=...  223 us
    pallas_call x1, Pallas kernels, local(): pl.pallas_call(functools.partial(finish, cells), out_shape=[shape(field.s...  32.4 us
    unnamed x35, local copies, waits for them, and re-layouts  17.4 us
    pallas_call x1, Pallas kernels, by_rows(): pl.pallas_call(body, grid=(args[0].shape[0] // group,), in_specs=[cut(a)...  8.44 us

profile of v3, /device:TPU:1, one launch (start us, length us, event | category | flops | bytes accessed | tf_op | source)
XLA Modules:
  0.0 295.4 jit_solution(6380888415326738181)
XLA Ops:
  0.6 2.9 copy.34.refs_0_.f_ref.refs_10_
  3.5 0.1 broadcast_in_dim.50.m_ref
  3.7 0.1 subtract_multiply_fusion
  3.8 0.1 exponential_multiply_fusion.diag_ref
  3.9 2.3 shard_map.129
  6.2 0.2 slice_bitcast_fusion
  6.5 0.4 copy.29
  6.9 0.0 copy-start
  6.9 0.0 copy-start.8
  6.9 2.5 copy.30
  9.4 0.0 copy-start.10
  9.4 0.0 copy-start.9
  9.4 0.0 copy-done.8
  9.4 0.2 copy.31
  9.7 0.0 copy-done
  9.7 0.9 copy.35.refs_5_
  10.6 1.0 broadcast_in_dim.54.refs_6_.refs_7_
  11.6 0.1 broadcast_in_dim.57
  11.6 0.1 broadcast_in_dim.58
  11.7 0.9 broadcast_in_dim.59.refs_7_.refs_6_
  12.6 0.0 copy-done.10
  12.6 0.1 compare_convert_fusion
  12.7 0.0 copy-done.9
  12.7 0.1 pad_dynamic-slice_fusion.1
  12.9 0.2 copy.52
  13.1 0.2 copy.51
  13.3 0.1 pad.29.clone
  13.3 0.1 pad_dynamic-slice_fusion.2
  13.4 0.2 copy.50
  13.6 0.2 copy.49
  13.8 0.2 pad_maximum_fusion.1
  14.0 0.7 pad.17.refs_8_
  14.7 0.0 copy-start.3
  14.7 104.0 %shard_map.130 = (bf16[24,96,384]{2,1,0:T(8,128)(2,1)}, f32[24,96,384]{2,1,0:T(8,128)}, f32[3,192,384]{2,1,0:T(8,128)}) custom-call(bf16[24,90,384]{2,1,0:T(8,128)(2,1)} %copy.34.refs_0_.f_ref.refs_10_, bf16[3,768,384]{2,1,0:T(8,128)(2,1)} %bitcast.19, bf16[3,384,768]{2,1,0:T(8,128)(2,1)} %bitcast.21, bf16[384,768]{1,0:T(8,128)(2,1)} %constant.106.clone.refs_3_, ...), custom_call_target="tpu_custom_call" | custom-call | tf_op jit(solution)/shard_map/pallas_call | solution.py:534
  118.7 0.0 copy-start.4
  118.7 0.0 copy-done.3
  118.7 1.4 copy.38.ct_ref
  120.1 0.0 copy-done.4
  120.2 0.9 copy.36
  121.0 8.4 %shard_map.131 = (bf16[24,90,384]{2,1,0:T(8,128)(2,1)}, bf16[24,96,384]{2,1,0:T(8,128)(2,1)}, f32[384,384]{1,0:T(8,128)}) custom-call(f32[24,96,384]{2,1,0:T(8,128)} %get-tuple-element.17.km_ref, bf16[24,96,384]{2,1,0:T(8,128)(2,1)} %get-tuple-element.18.so_ref, bf16[24,90,384]{2,1,0:T(8,128)(2,1)} %copy.34.refs_0_.f_ref.refs_10_, ...), custom_call_target="tpu_custom_call" | custom-call | tf_op jit(solution)/shard_map/pallas_call | solution.py:660
  129.5 0.0 copy-start.1
  129.5 3.3 %copy.47 = bf16[24,90,384]{2,0,1:T(8,128)(2,1)} copy(bf16[24,90,384]{2,1,0:T(8,128)(2,1)} %get-tuple-element.34) | data formatting | bytes 3317760
  132.8 0.7 pad.18.refs_8_
  133.5 0.0 copy-done.1
  133.5 2.1 copy.41
  135.6 0.0 copy-start.5
  135.6 119.4 %shard_map.132 = (bf16[24,96,384]{2,1,0:T(8,128)(2,1)}, f32[24,96,384]{2,1,0:T(8,128)}, f32[4,384,384]{2,1,0:T(8,128)}, f32[192,384]{1,0:T(8,128)}) custom-call(bf16[24,96,384]{2,1,0:T(8,128)(2,1)} %get-tuple-element.20.refs_0_, bf16[3,768,384]{2,1,0:T(8,128)(2,1)} %bitcast.20, bf16[3,384,768]{2,1,0:T(8,128)(2,1)} %bitcast.22, ...), custom_call_target="tpu_custom_call" | custom-call | tf_op jit(solution)/shard_map/pallas_call | solution.py:534
  255.0 0.0 copy-done.5
  255.0 0.9 copy.44
  255.9 32.4 %shard_map.133 = (bf16[24,90,384]{2,1,0:T(8,128)(2,1)}, f32[384,384]{1,0:T(8,128)}, f32[192,384]{1,0:T(8,128)}) custom-call(f32[24,96,384]{2,1,0:T(8,128)} %get-tuple-element.23.adj_ref, bf16[24,96,384]{2,1,0:T(8,128)(2,1)} %get-tuple-element.24.gm_ref, bf16[24,90,384]{2,1,0:T(8,128)(2,1)} %copy.34.refs_0_.f_ref.refs_10_, bf16[24,90,384]{2,1,0:T(8,128)(2,1)} %copy.38.ct_ref, ...), custom_call_target="tpu_custom_call" | custom-call | tf_op jit(solution)/shard_map/pallas_call | solution.py:724
  288.4 0.0 copy-start.2
  288.4 3.4 %copy.48 = bf16[24,90,384]{2,0,1:T(8,128)(2,1)} copy(bf16[24,90,384]{2,1,0:T(8,128)(2,1)} %get-tuple-element.35) | data formatting | bytes 3317760
  291.7 0.0 copy-done.2
  291.7 0.0 copy-start.6
  291.8 0.1 slice.54
  291.9 0.9 copy-done.6
  292.8 0.0 copy-start.7
  292.8 1.9 maximum_multiply_fusion
  294.7 0.0 copy-done.7
  294.7 0.7 copy.54
  (21 shorter events, 0.3 us)
Async XLA Ops:
  6.9 2.8 copy-start
  6.9 2.5 copy-start.8
  9.4 3.2 %copy-start.10 = (s32[3,384]{1,0:T(4,128)S(1)}, s32[3,384]{1,0:T(4,128)}, u32[]{:S(2)}) copy-start(s32[3,384]{1,0:T(4,128)} %param.17) | copy-start | bytes 13828
  9.4 3.3 %copy-start.9 = (f32[3,3,7,384]{3,2,1,0:T(8,128)S(1)}, f32[3,3,7,384]{3,2,1,0:T(8,128)}, u32[]{:S(2)}) copy-start(f32[3,3,7,384]{3,2,1,0:T(8,128)} %param.16) | copy-start | bytes 290308
  14.7 104.0 %copy-start.3 = (bf16[24,90,384]{2,0,1:T(8,128)(2,1)S(1)}, bf16[24,90,384]{2,0,1:T(8,128)(2,1)}, u32[]{:S(2)}) copy-start(bf16[24,90,384]{2,0,1:T(8,128)(2,1)} %param.11) | copy-start | bytes 4976644
  118.7 1.5 copy-start.4
  129.5 4.0 %copy-start.1 = (bf16[3,384,384]{2,1,0:T(8,128)(2,1)S(1)}, bf16[3,384,384]{2,1,0:T(8,128)(2,1)}, u32[]{:S(2)}) copy-start(bf16[3,384,384]{2,1,0:T(8,128)(2,1)} %refs_9_.1) | copy-start | bytes 2654212
  135.6 119.4 %copy-start.5 = (bf16[384,384]{1,0:T(8,128)(2,1)S(1)}, bf16[384,384]{1,0:T(8,128)(2,1)}, u32[]{:S(2)}) copy-start(bf16[384,384]{1,0:T(8,128)(2,1)} %refs_10_.2) | copy-start | bytes 884740
  288.4 3.4 %copy-start.2 = (f32[4,384,384]{2,1,0:T(8,128)S(1)}, f32[4,384,384]{2,1,0:T(8,128)}, u32[]{:S(2)}) copy-start(f32[4,384,384]{2,1,0:T(8,128)} %get-tuple-element.27) | copy-start | bytes 7077892
  291.7 1.1 copy-start.6
  292.8 1.9 copy-start.7

commit v4 on v3

--- a/solution.py
+++ b/solution.py
@@ -202,20 +202,29 @@
         del refs[:n]
         return head
 
-    x_ref, table_ref, turned_ref, into_ref, back_ref, gain_ref, in_scale, out_scale, taps_ref, kernel_ref = take(10)
+    x_ref, into_ref = take(2)
     if forward:
         (mix_ref,) = take(1)
+    late_in = take(8 if forward else 13)
+    if forward:
         grid_ref, stencil_ref, bands_ref = take(3)
     else:
-        field_ref, gow_ref, bands_ref = take(3)
-        grid_ref, stencil_ref, early_ref, gain_out = take(4)
+        out_ref, early_ref, gmw_ref, gain_total = take(4)
+    late_ref = take(len(late_in))
+    (late_sem,) = take(1)
+    table_ref, turned_ref, back_ref, gain_ref, in_scale, out_scale, taps_ref, kernel_ref = late_ref[:8]
+    if not forward:
+        field_ref, gow_ref, bands_ref, ct_ref, wt_ref = late_ref[8:]
     send1, recv1, send2, recv2, send3, recv3, send4, recv4 = take(8)
-    modes, rows_ref, ext, from_left, from_right, band_ref, spare = take(7)
+    modes, rows_ref, ext, from_left, from_right, band_ref, spare, part_ref = take(8)
     s1, r1, s2, r2, s3, r3, s4, r4, hs, hr = take(10)
     if not forward:
-        part_ref, pad_ref, grad_ref = take(3)
+        pad_ref, grad_ref, grid_ref, stencil_ref, gain_out = take(5)
         red = take(11)
         begin, across, spread, end = reducer(*red[:5], red[5:])
+        red2 = take(11)
+        begin2, across2, spread2, end2 = reducer(*red2[:5], red2[5:])
+    late_copies = [pltpu.make_async_copy(a, b, late_sem.at[n]) for n, (a, b) in enumerate(zip(late_in, late_ref))]
     lat, lon = lax.axis_index("lat"), lax.axis_index("lon")
     lons, lats = lax.axis_size("lon"), lax.axis_size("lat")
     rows = x_ref.shape[0]
@@ -282,7 +291,7 @@
             ext[1 + i, 112:128] = jnp.where(place >= 13, left, 0.0).astype(BF)
             return carry
 
-        lax.fori_loop(0, rows, step, 0)
+        lax.fori_loop(0, rows, step, 0, unroll=2)
 
         @pl.when(lat < lats - 1)
         def _():
@@ -319,26 +328,24 @@
             to_above.wait_send()
 
     def stencil(first):
-        def step(a, carry):
-            i = first + a
-            band_matrix(taps_ref, i, band_ref, cells)
-            source = ext[pl.ds(i, 3)].reshape(3 * EXT, chans)
-            total = None
-            for k in range(3):
-                part = dot(band_ref[k * ROWS : (k + 1) * ROWS], source).astype(BF)
-                if not forward:
-                    part_ref[k, a] = part
-                part = dot(part, kernel_ref[k])
-                total = part if total is None else total + part
-            stencil_ref[i] = total
-            if not forward:
-                pad_ref[a, 80:96] = jnp.zeros((16, chans), BF)
-                pad_ref[a, :cells] = field_ref[i]
-            return carry
-
-        lax.fori_loop(0, 4, step, 0)
+        def step(n, carry):
+            for a in range(2):
+                i = first + 2 * n + a
+                band_matrix(taps_ref, i, band_ref.at[a], cells)
+                source = ext[pl.ds(i, 3)].reshape(3 * EXT, chans)
+                part = dot(band_ref[a], source).astype(BF)
+                for k in range(3):
+                    part_ref[k, 2 * n + a] = part[k * ROWS : (k + 1) * ROWS]
+            return carry
+
+        lax.fori_loop(0, 2, step, 0)
+        total = None
+        for k in range(3):
+            part = dot(part_ref[k].reshape(4 * ROWS, chans), kernel_ref[k])
+            total = part if total is None else total + part
+        stencil_ref[first : first + 4] = total.reshape(4, ROWS, chans)
         if not forward:
-            own = pad_ref[...].reshape(4 * ROWS, chans)
+            own = pad_ref[first : first + 4].reshape(4 * ROWS, chans)
             for k in range(3):
                 add = dot(own, part_ref[k].reshape(4 * ROWS, chans), ((0,), (0,)))
                 grad_ref[k] = add if first == START else grad_ref[k] + add
@@ -348,7 +355,7 @@
             body(n // 6, pl.multiple_of(n % 6 * 16, 16))
             return carry
 
-        lax.fori_loop(0, 18, step, 0)
+        lax.fori_loop(0, 18, step, 0, unroll=3)
 
     def split(v):
         lanes_v = slice(v * 128, (v + 1) * 128)
@@ -383,7 +390,7 @@
             send2[v, b] = jnp.concatenate(pieces, axis=0).astype(BF)
             return carry
 
-        lax.fori_loop(0, lats, step, 0)
+        lax.fori_loop(0, lats, step, 0, unroll=4)
         lat_in[v][0]()
 
     def filter_bands(v):
@@ -397,7 +404,7 @@
                 rows_ref[o, at] = block[o * 24 : (o + 1) * 24] * in_scale[o, at]
             return carry
 
-        lax.fori_loop(0, lats, gather, 0)
+        lax.fori_loop(0, lats, gather, 0, unroll=4)
         gain_sum = None
         for o in range(3):
             every = dot(table_ref[o], rows_ref[o].astype(BF))
@@ -418,7 +425,7 @@
             send3[v, b] = jnp.concatenate([rows_ref[o, at] for o in range(3)] + [blank], axis=0).astype(BF)
             return carry
 
-        lax.fori_loop(0, lats, scatter, 0)
+        lax.fori_loop(0, lats, scatter, 0, unroll=4)
         lat_out[v][0]()
         if not forward:
             for width in (16, 32, 64):
@@ -434,7 +441,7 @@
             modes[pl.ds(pl.multiple_of(b * 24, 8), 24), :] = jnp.concatenate(wide, axis=1)
             return carry
 
-        lax.fori_loop(0, lats, step, 0)
+        lax.fori_loop(0, lats, step, 0, unroll=4)
         send4[v] = dot(back_ref[...], modes[...].astype(BF)).astype(BF).reshape(lons, ROWS, 384)
         lon_out[v][0]()
 
@@ -464,128 +471,150 @@
             for v in range(3):
                 early_ref[k, :, v * 128 : (v + 1) * 128] = whole[(k * 3 + v) * 384 : (k * 3 + v + 1) * 384].astype(F32)
 
-    lax.fori_loop(0, rows, fill, 0)
+    def own_rows(i, carry):
+        pad_ref[i, 80:96] = jnp.zeros((16, chans), BF)
+        pad_ref[i, :cells] = field_ref[i]
+        return carry
+
+    def weigh(v):
+        lanes = slice(v * 128, (v + 1) * 128)
+
+        def step(n, carry):
+            some = pl.ds(n * 8, 8)
+            own = pad_ref[some].reshape(8 * ROWS, chans)
+            return carry + dot(own, grid_ref[some, :, lanes].reshape(8 * ROWS, 128), ((0,), (0,)))
+
+        own = pad_ref[0:8].reshape(8 * ROWS, chans)
+        first = dot(own, grid_ref[0:8, :, lanes].reshape(8 * ROWS, 128), ((0,), (0,)))
+        gmw_ref[:, lanes] = lax.fori_loop(1, 3, step, first)
+
+    def late_begin():
+        flat = red2[0]
+        for v in range(3):
+            lanes = slice(v * 128, (v + 1) * 128)
+            flat[v * 576 : v * 576 + 384] = gmw_ref[:, lanes].astype(BF)
+            flat[v * 576 + 384 : (v + 1) * 576] = gain_out[:, lanes].astype(BF)
+        flat[1728:] = jnp.zeros((64, 128), BF)
+        begin2()
+
+    def late_end():
+        end2()
+        whole = red2[4]
+        for v in range(3):
+            lanes = slice(v * 128, (v + 1) * 128)
+            gmw_ref[:, lanes] = whole[v * 576 : v * 576 + 384].astype(F32)
+            gain_total[:, lanes] = whole[v * 576 + 384 : (v + 1) * 576].astype(F32)
+
+    def field_rows(first):
+        def step(n, carry):
+            some = pl.ds(first + n * 4, 4)
+            mixed = dot(grid_ref[some].reshape(4 * ROWS, chans), wt_ref[...]).reshape(4, ROWS, chans)
+            add = stencil_ref[some] + mixed
+            out_ref[some] = (ct_ref[some].astype(F32) + add[:, :cells]).astype(BF)
+            return carry
+
+        lax.fori_loop(0, 2, step, 0)
+
+    for c in late_copies:
+        c.start()
+    lax.fori_loop(0, rows, fill, 0, unroll=2)
     enter()
     to_right.start()
     to_left.start()
     for v in range(3):
         split(v)
+    for c in late_copies:
+        c.wait()
     halo_columns()
     START = 4
+    if not forward:
+        lax.fori_loop(0, rows, own_rows, 0, unroll=2)
     stencil(4)
+    analyse(0)
     stencil(8)
-    analyse(0)
-    stencil(12)
     filter_bands(0)
     analyse(1)
-    stencil(16)
+    stencil(12)
     synthesise(0)
     filter_bands(1)
     halo_rows()
     if not forward:
+        stencil(16)
         stencil(20)
         stencil(0)
         early_begin()
     analyse(2)
     if forward:
-        stencil(20)
+        stencil(16)
     synthesise(1)
     filter_bands(2)
     if not forward:
         across()
     if forward:
+        stencil(20)
         stencil(0)
     join(0)
+    if not forward:
+        weigh(0)
     synthesise(2)
     if not forward:
         spread()
     join(1)
+    if not forward:
+        weigh(1)
+        early_end()
     join(2)
     if not forward:
-        early_end()
+        weigh(2)
+        late_begin()
+        field_rows(0)
+        across2()
+        field_rows(8)
+        spread2()
+        field_rows(16)
+        late_end()
     halo_drain()
     for road in (lon_in, lat_in, lat_out, lon_out):
         for v in range(3):
             road[v][2]()
 
 
-def pass_call(forward, cells, args, outs):
+def pass_call(forward, cells, first, late, outs):
     lons, lats = lax.axis_size("lon"), lax.axis_size("lat")
-    rows, _, chans = args[0].shape
+    rows, _, chans = first[0].shape
     lon_buf = pltpu.VMEM((3, lons, ROWS, 384), BF)
     lat_buf = pltpu.VMEM((3, lats, PAD, 128), BF)
     lon_sem = pltpu.SemaphoreType.DMA((3, lons))
     lat_sem = pltpu.SemaphoreType.DMA((3, lats))
-    scratch = [lon_buf, lon_buf] + [lat_buf] * 4 + [lon_buf, lon_buf]
+    scratch = [pltpu.VMEM(a.shape, a.dtype) for a in late] + [pltpu.SemaphoreType.DMA((len(late),))]
+    scratch += [lon_buf, lon_buf] + [lat_buf] * 4 + [lon_buf, lon_buf]
     scratch += [
         pltpu.VMEM((384, 384), F32),
         pltpu.VMEM((3, 384, 128), F32),
         pltpu.VMEM((rows + 2, EXT, chans), BF),
         pltpu.VMEM((rows, 16, chans), BF),
         pltpu.VMEM((rows, 16, chans), BF),
-        pltpu.VMEM((3 * ROWS, 3 * EXT), BF),
+        pltpu.VMEM((2, 3 * ROWS, 3 * EXT), BF),
         pltpu.VMEM((rows, ROWS, 128) if forward else (8, 128), F32),
+        pltpu.VMEM((3, 4, ROWS, chans), BF),
     ]
     scratch += [lon_sem, lon_sem, lat_sem, lat_sem, lat_sem, lat_sem, lon_sem, lon_sem]
     scratch += [pltpu.SemaphoreType.DMA((4,)), pltpu.SemaphoreType.DMA((4,))]
     if not forward:
-        scratch += [pltpu.VMEM((3, 4, ROWS, chans), BF), pltpu.VMEM((4, ROWS, chans), BF), pltpu.VMEM((3, chans, chans), F32)]
-        scratch += reducer_scratch(lats, lons, EARLY)
+        wide = (rows, ROWS, chans)
+        scratch += [pltpu.VMEM(wide, BF), pltpu.VMEM((3, chans, chans), F32), pltpu.VMEM(wide, BF), pltpu.VMEM(wide, F32)]
+        scratch += [pltpu.VMEM((192, chans), F32)]
+        scratch += reducer_scratch(lats, lons, EARLY) + reducer_scratch(lats, lons, LATE)
     return pl.pallas_call(
         functools.partial(pass_kernel, forward, cells),
         out_shape=outs,
-        in_specs=[VMEM] * len(args),
+        in_specs=[VMEM] * len(first) + [pl.BlockSpec(memory_space=pl.ANY)] * len(late),
         out_specs=[VMEM] * len(outs),
         scratch_shapes=scratch,
         compiler_params=pltpu.CompilerParams(
             collective_id=1 if forward else 2, has_side_effects=True, vmem_limit_bytes=60 << 20
         ),
-    )(*args)
-
-
-def finish(cells, adj_ref, gm_ref, f_ref, ct_ref, wt_ref, gain_ref, out_ref, gmw_ref, gain_out, pad_ref, *red):
-    begin, across, spread, end = reducer(*red[:5], red[5:])
-    flat, whole = red[0], red[4]
-    enter = greet()
-    rows, chans = adj_ref.shape[0], adj_ref.shape[2]
-    group = pad_ref.shape[0]
-
-    def weigh(n, carry):
-        some = pl.ds(n * group, group)
-        own = padded(pad_ref, f_ref.at[some], cells)
-        add = dot(own, gm_ref[some].reshape(group * ROWS, chans), ((0,), (0,)))
-        gmw_ref[...] = gmw_ref[...] + add
-        return carry
-
-    gmw_ref[...] = jnp.zeros_like(gmw_ref)
-    lax.fori_loop(0, rows // group, weigh, 0)
-    for v in range(3):
-        lanes = slice(v * 128, (v + 1) * 128)
-        flat[v * 576 : v * 576 + 384] = gmw_ref[:, lanes].astype(BF)
-        flat[v * 576 + 384 : (v + 1) * 576] = gain_ref[:, lanes].astype(BF)
-    flat[1728:] = jnp.zeros((64, 128), BF)
-    enter()
-    begin()
-
-    def field_rows(first):
-        def step(n, carry):
-            some = pl.ds(first + n * group, group)
-            add = adj_ref[some] + dot(gm_ref[some].reshape(group * ROWS, chans), wt_ref[...]).reshape(group, ROWS, chans)
-            out_ref[some] = (ct_ref[some].astype(F32) + add[:, :cells]).astype(BF)
-            return carry
-
-        lax.fori_loop(0, 2, step, 0)
-
-    field_rows(0)
-    across()
-    field_rows(8)
-    spread()
-    field_rows(16)
-    end()
-    for v in range(3):
-        lanes = slice(v * 128, (v + 1) * 128)
-        gmw_ref[:, lanes] = whole[v * 576 : v * 576 + 384].astype(F32)
-        gain_out[:, lanes] = whole[v * 576 + 384 : (v + 1) * 576].astype(F32)
+    )(*first, *late)
 
 
 def fourier_tables(lon_count, cells, lat_parts):
@@ -698,12 +727,12 @@
     gain = lax.dynamic_slice_in_dim(groups, lon, 1, 2)
     gain = jnp.broadcast_to(gain, groups.shape).reshape(degrees, chans)
 
-    shared = [table, turned, into, back, gain]
     wide = (rows, ROWS, chans)
     spec_out, kernel_mix, bands = pass_call(
         True,
         cells,
-        [field, *shared, quad, mode_weight, own_taps, kernel_weights, spectral_weight],
+        [field, into, spectral_weight],
+        [table, turned, back, gain, quad, mode_weight, own_taps, kernel_weights],
         [shape(wide, BF), shape(wide, F32), shape((3, degrees, chans), F32)],
     )
     output_field, grad_pre, grad_out_w = by_rows(
@@ -715,20 +744,14 @@
         [pltpu.VMEM((4, ROWS, chans), BF)],
     )
     turned_weights = jnp.transpose(kernel_weights, (0, 2, 1))
-    grad_mixed, adj, early, gain_place = pass_call(
+    grad_field, early, grad_mix_w, gain_total = pass_call(
         False,
         cells,
-        [grad_pre, *shared, mode_weight, quad, adj_taps, turned_weights, field, grad_out_w, bands],
-        [shape(wide, BF), shape(wide, F32), shape((4, chans, chans), F32), shape((degrees, chans), F32)],
+        [grad_pre, into],
+        [table, turned, back, gain, mode_weight, quad, adj_taps, turned_weights]
+        + [field, grad_out_w, bands, cotangent, spectral_weight.T],
+        [shape(field.shape, BF), shape((4, chans, chans), F32), shape((chans, chans), F32), shape((degrees, chans), F32)],
     )
-    grad_field, grad_mix_w, gain_total = pl.pallas_call(
-        functools.partial(finish, cells),
-        out_shape=[shape(field.shape, BF), shape((chans, chans), F32), shape((degrees, chans), F32)],
-        in_specs=[VMEM] * 6,
-        out_specs=[VMEM] * 3,
-        scratch_shapes=[pltpu.VMEM((4, ROWS, chans), BF)] + reducer_scratch(lat_parts, lon_parts, LATE),
-        compiler_params=pltpu.CompilerParams(collective_id=3, has_side_effects=True, vmem_limit_bytes=56 << 20),
-    )(adj, grad_mixed, field, cotangent, spectral_weight.T, gain_place)
     weight_grads = jnp.concatenate([early[:3], grad_mix_w[None], early[3:]]) / math.sqrt(lat_count * lon_count)
     return output_field, grad_field, weight_grads, gain_total
 

time: 296 us -> 273 us (0.922); the launches traced: 295 us -> 269 us
  Pallas kernels: 267 us -> 240 us
    pallas_call x1 -> x0, Pallas kernels: 32.4 us -> none  [local(): pl.pallas_call(functools.partial(finish, cells), out_shape=[shape(field.s...]
    pallas_call x2, Pallas kernels: 223 us -> 229 us  [pass_call(): pl.pallas_call(functools.partial(pass_kernel, forward, cells), out_shape=...]
where the time goes in v4:
time: 273 us; the launch traced here: 269 us
  Pallas kernels  240 us (88%)
  local copies, waits for them, and re-layouts  25.5 us (9%)
    pallas_call x2, Pallas kernels, pass_call(): pl.pallas_call(functools.partial(pass_kernel, forward, cells), out_shape=...  229 us
    unnamed x35, local copies, waits for them, and re-layouts  17.5 us
    pallas_call x1, Pallas kernels, by_rows(): pl.pallas_call(body, grid=(args[0].shape[0] // group,), in_specs=[cut(a)...  8.46 us

profile of v4, /device:TPU:1, one launch (start us, length us, event | category | flops | bytes accessed | tf_op | source)
XLA Modules:
  0.0 269.2 jit_solution(5757730509865296764)
XLA Ops:
  0.6 2.9 %copy.33.refs_0_.f_ref.refs_10_ = bf16[24,90,384]{2,1,0:T(8,128)(2,1)} copy(bf16[24,90,384]{2,0,1:T(8,128)(2,1)} %param.10) | data formatting | bytes 3317760 | tf_op args[0]
  3.5 0.1 broadcast_in_dim.50.m_ref
  3.7 0.1 subtract_multiply_fusion
  3.8 0.1 exponential_multiply_fusion.diag_ref
  3.9 2.3 shard_map.129
  6.2 0.2 slice_bitcast_fusion
  6.5 0.4 copy.28
  6.9 0.0 copy-start
  6.9 0.0 copy-start.8
  6.9 2.5 copy.29
  9.4 0.0 copy-start.10
  9.4 0.0 copy-start.9
  9.4 0.0 copy-done.8
  9.4 0.2 copy.30
  9.6 0.0 copy-done
  9.6 0.9 copy.34.refs_6_.refs_5_
  10.5 0.9 broadcast_in_dim.54.refs_7_
  11.5 0.1 broadcast_in_dim.57
  11.5 0.1 broadcast_in_dim.58
  11.6 0.9 broadcast_in_dim.59.refs_8_.refs_6_
  12.5 0.0 copy-done.10
  12.5 0.1 compare_convert_fusion
  12.6 0.0 copy-done.9
  12.6 0.1 pad_dynamic-slice_fusion.1
  12.8 0.2 copy.50
  13.0 0.2 copy.49
  13.2 0.1 pad.29.clone
  13.3 0.1 pad_dynamic-slice_fusion.2
  13.4 0.2 copy.48
  13.6 0.2 copy.47
  13.7 0.2 pad_maximum_fusion.1
  13.9 0.7 pad.17.refs_9_
  14.6 0.0 copy-start.3
  14.6 92.5 %shard_map.130 = (bf16[24,96,384]{2,1,0:T(8,128)(2,1)}, f32[24,96,384]{2,1,0:T(8,128)}, f32[3,192,384]{2,1,0:T(8,128)}) custom-call(bf16[24,90,384]{2,1,0:T(8,128)(2,1)} %copy.33.refs_0_.f_ref.refs_10_, bf16[384,768]{1,0:T(8,128)(2,1)} %constant.106.clone.refs_1_, bf16[384,384]{1,0:T(8,128)(2,1)} %refs_2_.1, bf16[3,768,384]{2,1,0:T(8,128)(2,1)} %bitcast.19, ...), custom_call_target="tpu_custom_call" | custom-call | tf_op jit(solution)/shard_map/pallas_call | solution.py:608
  107.1 0.0 copy-start.4
  107.1 0.0 copy-done.3
  107.1 1.6 copy.37.ct_ref.refs_13_
  108.7 0.0 copy-done.4
  108.7 0.9 copy.35
  109.6 8.5 %shard_map.131 = (bf16[24,90,384]{2,1,0:T(8,128)(2,1)}, bf16[24,96,384]{2,1,0:T(8,128)(2,1)}, f32[384,384]{1,0:T(8,128)}) custom-call(f32[24,96,384]{2,1,0:T(8,128)} %get-tuple-element.14.km_ref, bf16[24,96,384]{2,1,0:T(8,128)(2,1)} %get-tuple-element.15.so_ref, bf16[24,90,384]{2,1,0:T(8,128)(2,1)} %copy.33.refs_0_.f_ref.refs_10_, ...), custom_call_target="tpu_custom_call" | custom-call | tf_op jit(solution)/shard_map/pallas_call | solution.py:689
  118.1 0.0 copy-start.1
  118.1 0.0 copy-start.5
  118.1 3.3 %copy.45 = bf16[24,90,384]{2,0,1:T(8,128)(2,1)} copy(bf16[24,90,384]{2,1,0:T(8,128)(2,1)} %get-tuple-element.28) | data formatting | bytes 3317760
  121.4 0.7 pad.18.refs_8_
  122.1 0.0 copy-done.1
  122.1 2.1 copy.40
  124.2 0.0 copy-done.5
  124.2 0.9 copy.41
  125.1 136.9 %shard_map.132 = (bf16[24,90,384]{2,1,0:T(8,128)(2,1)}, f32[4,384,384]{2,1,0:T(8,128)}, f32[384,384]{1,0:T(8,128)}, f32[192,384]{1,0:T(8,128)}) custom-call(bf16[24,96,384]{2,1,0:T(8,128)(2,1)} %get-tuple-element.17.refs_0_, bf16[384,768]{1,0:T(8,128)(2,1)} %constant.106.clone.refs_1_, bf16[3,768,384]{2,1,0:T(8,128)(2,1)} %bitcast.20, ...), custom_call_target="tpu_custom_call" | custom-call | tf_op jit(solution)/shard_map/pallas_call | solution.py:608
  262.0 0.0 copy-start.2
  262.0 3.4 %copy.46 = bf16[24,90,384]{2,0,1:T(8,128)(2,1)} copy(bf16[24,90,384]{2,1,0:T(8,128)(2,1)} %get-tuple-element.29) | data formatting | bytes 3317760
  265.4 0.0 copy-done.2
  265.4 0.0 copy-start.6
  265.4 0.1 slice.54
  265.5 0.9 copy-done.6
  266.4 0.0 copy-start.7
  266.4 1.9 maximum_multiply_fusion
  268.3 0.0 copy-done.7
  268.3 0.7 copy.52
  (21 shorter events, 0.3 us)
Async XLA Ops:
  6.9 2.7 %copy-start = (bf16[12,192,384]{2,1,0:T(8,128)(2,1)}, bf16[12,192,384]{2,1,0:T(8,128)(2,1)S(1)}, u32[]{:S(2)}) copy-start(bf16[12,192,384]{2,1,0:T(8,128)(2,1)S(1)} %copy.28) | copy-start | bytes 5308420
  6.9 2.5 copy-start.8
  9.4 3.2 %copy-start.10 = (s32[3,384]{1,0:T(4,128)S(1)}, s32[3,384]{1,0:T(4,128)}, u32[]{:S(2)}) copy-start(s32[3,384]{1,0:T(4,128)} %param.17) | copy-start | bytes 13828
  9.4 3.3 %copy-start.9 = (f32[3,3,7,384]{3,2,1,0:T(8,128)S(1)}, f32[3,3,7,384]{3,2,1,0:T(8,128)}, u32[]{:S(2)}) copy-start(f32[3,3,7,384]{3,2,1,0:T(8,128)} %param.16) | copy-start | bytes 290308
  14.6 92.5 %copy-start.3 = (bf16[24,90,384]{2,0,1:T(8,128)(2,1)S(1)}, bf16[24,90,384]{2,0,1:T(8,128)(2,1)}, u32[]{:S(2)}) copy-start(bf16[24,90,384]{2,0,1:T(8,128)(2,1)} %param.11) | copy-start | bytes 4976644
  107.1 1.6 copy-start.4
  118.1 4.0 %copy-start.1 = (bf16[3,384,384]{2,1,0:T(8,128)(2,1)S(1)}, bf16[3,384,384]{2,1,0:T(8,128)(2,1)}, u32[]{:S(2)}) copy-start(bf16[3,384,384]{2,1,0:T(8,128)(2,1)} %refs_10_.2) | copy-start | bytes 2654212
  118.1 6.2 %copy-start.5 = (bf16[384,384]{1,0:T(8,128)(2,1)S(1)}, bf16[384,384]{1,0:T(8,128)(2,1)}, u32[]{:S(2)}) copy-start(bf16[384,384]{1,0:T(8,128)(2,1)} %refs_2_.1) | copy-start | bytes 884740
  262.0 3.4 %copy-start.2 = (f32[4,384,384]{2,1,0:T(8,128)S(1)}, f32[4,384,384]{2,1,0:T(8,128)}, u32[]{:S(2)}) copy-start(f32[4,384,384]{2,1,0:T(8,128)} %get-tuple-element.21) | copy-start | bytes 7077892
  265.4 1.1 copy-start.6
  266.4 1.9 copy-start.7

commit v5 on v4

--- a/solution.py
+++ b/solution.py
@@ -95,28 +95,27 @@
 MESH = pl.DeviceIdType.MESH
 
 
-def transfer(axis, me, parts, source, target, send_sem, recv_sem):
-    def copy(peer, slot):
-        return pltpu.make_async_remote_copy(
-            src_ref=source(peer),
-            dst_ref=target(slot),
-            send_sem=send_sem(peer),
-            recv_sem=recv_sem(slot),
-            device_id={axis: peer},
-            device_id_type=MESH,
-        )
-
-    def over(body):
-        lax.fori_loop(1, parts, lambda d, carry: (body(lax.rem(me + d, parts)), carry)[1], 0)
-
+def transfer(axis, me, parts, source, target, bulk, send_sem, recv_sem):
     def start():
-        over(lambda peer: copy(peer, me).start())
+        def step(d, carry):
+            peer = lax.rem(me + d, parts)
+            pltpu.make_async_remote_copy(
+                src_ref=source(peer),
+                dst_ref=target(me),
+                send_sem=send_sem,
+                recv_sem=recv_sem,
+                device_id={axis: peer},
+                device_id_type=MESH,
+            ).start()
+            return carry
+
+        lax.fori_loop(1, parts, step, 0, unroll=7 if parts == 8 else 5)
 
     def arrive():
-        over(lambda peer: copy(peer, peer).wait_recv())
+        pltpu.make_async_copy(bulk, bulk, recv_sem).wait()
 
     def drain():
-        over(lambda peer: copy(peer, peer).wait_send())
+        pltpu.make_async_copy(bulk, bulk, send_sem).wait()
 
     return start, arrive, drain
 
@@ -131,7 +130,7 @@
             pl.semaphore_signal(barrier, inc=1, device_id={axis: lax.rem(me + d, parts)}, device_id_type=MESH)
             return carry
 
-        lax.fori_loop(1, parts, body, 0)
+        lax.fori_loop(1, parts, body, 0, unroll=7 if parts == 8 else 5)
         total += parts - 1
     return lambda: pl.semaphore_wait(barrier, total)
 
@@ -145,10 +144,13 @@
     def block(ref, b):
         return ref.at[pl.ds(pl.multiple_of(b * n, 16), n)]
 
-    first = transfer("lat", lat, lats, lambda p: block(flat, p), lambda s: got1.at[s], lambda p: s1.at[p], lambda s: r1.at[s])
-    second = transfer("lon", lon, lons, lambda p: part, lambda s: got2.at[s], lambda p: s2.at[p], lambda s: r2.at[s])
+    first = transfer(
+        "lat", lat, lats, lambda p: block(flat, p), lambda s: got1.at[s], got1.at[pl.ds(0, lats - 1)], s1.at[0], r1.at[0]
+    )
+    second = transfer("lon", lon, lons, lambda p: part, lambda s: got2.at[s], got2.at[pl.ds(0, lons - 1)], s2.at[0], r2.at[0])
     third = transfer(
-        "lat", lat, lats, lambda p: block(whole, lat), lambda s: block(whole, s), lambda p: s3.at[p], lambda s: r3.at[s]
+        "lat", lat, lats, lambda p: block(whole, lat), lambda s: block(whole, s),
+        whole.at[pl.ds(0, (lats - 1) * n)], s3.at[0], r3.at[0],
     )
 
     def total(ref):
@@ -179,14 +181,14 @@
 
 
 def reducer_scratch(lats, lons, n):
-    lat_sem, lon_sem = pltpu.SemaphoreType.DMA((lats,)), pltpu.SemaphoreType.DMA((lons,))
+    sem = pltpu.SemaphoreType.DMA((1,))
     return [
         pltpu.VMEM((lats * n, 128), BF),
         pltpu.VMEM((lats, n, 128), BF),
         pltpu.VMEM((n, 128), BF),
         pltpu.VMEM((lons, n, 128), BF),
         pltpu.VMEM((lats * n, 128), BF),
-        lat_sem, lat_sem, lon_sem, lon_sem, lat_sem, lat_sem,
+        *[sem] * 6,
     ]
 
 
@@ -235,7 +237,7 @@
         def at(v):
             start, arrive, drain = transfer(
                 axis, me, parts,
-                lambda p: send.at[v, p], lambda s: recv.at[v, s], lambda p: ss.at[v, p], lambda s: rs.at[v, s],
+                lambda p: send.at[v, p], lambda s: recv.at[v, s], recv.at[v, pl.ds(0, parts - 1)], ss.at[v], rs.at[v],
             )
 
             def go():
@@ -530,29 +532,26 @@
     if not forward:
         lax.fori_loop(0, rows, own_rows, 0, unroll=2)
     stencil(4)
+    stencil(8)
     analyse(0)
-    stencil(8)
+    stencil(12)
+    stencil(16)
     filter_bands(0)
     analyse(1)
-    stencil(12)
+    halo_rows()
+    stencil(20)
+    if not forward:
+        stencil(0)
+        early_begin()
     synthesise(0)
     filter_bands(1)
-    halo_rows()
-    if not forward:
-        stencil(16)
-        stencil(20)
-        stencil(0)
-        early_begin()
     analyse(2)
     if forward:
-        stencil(16)
+        stencil(0)
     synthesise(1)
     filter_bands(2)
     if not forward:
         across()
-    if forward:
-        stencil(20)
-        stencil(0)
     join(0)
     if not forward:
         weigh(0)
@@ -562,7 +561,6 @@
     join(1)
     if not forward:
         weigh(1)
-        early_end()
     join(2)
     if not forward:
         weigh(2)
@@ -572,6 +570,7 @@
         field_rows(8)
         spread2()
         field_rows(16)
+        early_end()
         late_end()
     halo_drain()
     for road in (lon_in, lat_in, lat_out, lon_out):
@@ -584,8 +583,7 @@
     rows, _, chans = first[0].shape
     lon_buf = pltpu.VMEM((3, lons, ROWS, 384), BF)
     lat_buf = pltpu.VMEM((3, lats, PAD, 128), BF)
-    lon_sem = pltpu.SemaphoreType.DMA((3, lons))
-    lat_sem = pltpu.SemaphoreType.DMA((3, lats))
+    lon_sem = lat_sem = pltpu.SemaphoreType.DMA((3,))
     scratch = [pltpu.VMEM(a.shape, a.dtype) for a in late] + [pltpu.SemaphoreType.DMA((len(late),))]
     scratch += [lon_buf, lon_buf] + [lat_buf] * 4 + [lon_buf, lon_buf]
     scratch += [

time: 273 us -> 247 us (0.905)
  Pallas kernels: 240 us -> 213 us
    pallas_call x2, Pallas kernels: 229 us -> 203 us  [pass_call(): pl.pallas_call(functools.partial(pass_kernel, forward, cells), out_shape=...]
where the time goes in v5:
time: 247 us; the launch traced here: 243 us
  Pallas kernels  213 us (86%)
  local copies, waits for them, and re-layouts  25.5 us (10%)
    pallas_call x2, Pallas kernels, pass_call(): pl.pallas_call(functools.partial(pass_kernel, forward, cells), out_shape=...  203 us
    unnamed x35, local copies, waits for them, and re-layouts  17.5 us
    pallas_call x1, Pallas kernels, by_rows(): pl.pallas_call(body, grid=(args[0].shape[0] // group,), in_specs=[cut(a)...  8.46 us

profile of v5, /device:TPU:1, one launch (start us, length us, event | category | flops | bytes accessed | tf_op | source)
XLA Modules:
  0.0 242.5 jit_solution(2914750624390685422)
XLA Ops:
  0.6 2.9 %copy.33.refs_0_.f_ref.refs_10_ = bf16[24,90,384]{2,1,0:T(8,128)(2,1)} copy(bf16[24,90,384]{2,0,1:T(8,128)(2,1)} %param.10) | data formatting | bytes 3317760 | tf_op args[0]
  3.5 0.1 broadcast_in_dim.50.m_ref
  3.7 0.1 subtract_multiply_fusion
  3.8 0.1 exponential_multiply_fusion.diag_ref
  3.9 2.3 shard_map.129
  6.2 0.2 slice_bitcast_fusion
  6.5 0.4 copy.28
  6.9 0.0 copy-start
  6.9 0.0 copy-start.8
  6.9 2.5 %copy.29 = bf16[3,768,384]{1,2,0:T(8,128)(2,1)} copy(bf16[3,768,384]{2,1,0:T(8,128)(2,1)S(1)} %bitcast.18) | data formatting | bytes 3538944 | tf_op jit(solution)/shard_map/reshape | solution.py:716
  9.4 0.0 copy-start.10
  9.4 0.0 copy-start.9
  9.4 0.0 copy-done.8
  9.4 0.2 copy.30
  9.6 0.0 copy-done
  9.6 0.9 copy.34.refs_6_.refs_5_
  10.5 0.9 broadcast_in_dim.54.refs_7_
  11.5 0.1 broadcast_in_dim.57
  11.5 0.1 broadcast_in_dim.58
  11.6 0.9 broadcast_in_dim.59.refs_8_.refs_6_
  12.5 0.0 copy-done.10
  12.5 0.1 compare_convert_fusion
  12.6 0.0 copy-done.9
  12.6 0.1 pad_dynamic-slice_fusion.1
  12.8 0.2 copy.50
  13.0 0.2 copy.49
  13.2 0.1 pad.29.clone
  13.3 0.1 pad_dynamic-slice_fusion.2
  13.4 0.2 copy.48
  13.6 0.2 copy.47
  13.7 0.2 pad_maximum_fusion.1
  13.9 0.7 pad.17.refs_9_
  14.6 0.0 copy-start.3
  14.6 84.3 %shard_map.130 = (bf16[24,96,384]{2,1,0:T(8,128)(2,1)}, f32[24,96,384]{2,1,0:T(8,128)}, f32[3,192,384]{2,1,0:T(8,128)}) custom-call(bf16[24,90,384]{2,1,0:T(8,128)(2,1)} %copy.33.refs_0_.f_ref.refs_10_, bf16[384,768]{1,0:T(8,128)(2,1)} %constant.106.clone.refs_1_, bf16[384,384]{1,0:T(8,128)(2,1)} %refs_2_.1, bf16[3,768,384]{2,1,0:T(8,128)(2,1)} %bitcast.19, ...), custom_call_target="tpu_custom_call" | custom-call | tf_op jit(solution)/shard_map/pallas_call | solution.py:606
  98.9 0.0 copy-start.4
  98.9 0.0 copy-done.3
  98.9 1.6 copy.37.ct_ref.refs_13_
  100.4 0.0 copy-done.4
  100.4 0.9 copy.35
  101.3 8.5 %shard_map.131 = (bf16[24,90,384]{2,1,0:T(8,128)(2,1)}, bf16[24,96,384]{2,1,0:T(8,128)(2,1)}, f32[384,384]{1,0:T(8,128)}) custom-call(f32[24,96,384]{2,1,0:T(8,128)} %get-tuple-element.14.km_ref, bf16[24,96,384]{2,1,0:T(8,128)(2,1)} %get-tuple-element.15.so_ref, bf16[24,90,384]{2,1,0:T(8,128)(2,1)} %copy.33.refs_0_.f_ref.refs_10_, ...), custom_call_target="tpu_custom_call" | custom-call | tf_op jit(solution)/shard_map/pallas_call | solution.py:687
  109.8 0.0 copy-start.1
  109.8 0.0 copy-start.5
  109.8 3.3 %copy.45 = bf16[24,90,384]{2,0,1:T(8,128)(2,1)} copy(bf16[24,90,384]{2,1,0:T(8,128)(2,1)} %get-tuple-element.28) | data formatting | bytes 3317760
  113.1 0.7 pad.18.refs_8_
  113.8 0.0 copy-done.1
  113.8 2.1 copy.40
  116.0 0.0 copy-done.5
  116.0 0.9 copy.41
  116.9 118.4 %shard_map.132 = (bf16[24,90,384]{2,1,0:T(8,128)(2,1)}, f32[4,384,384]{2,1,0:T(8,128)}, f32[384,384]{1,0:T(8,128)}, f32[192,384]{1,0:T(8,128)}) custom-call(bf16[24,96,384]{2,1,0:T(8,128)(2,1)} %get-tuple-element.17.refs_0_, bf16[384,768]{1,0:T(8,128)(2,1)} %constant.106.clone.refs_1_, bf16[3,768,384]{2,1,0:T(8,128)(2,1)} %bitcast.20, ...), custom_call_target="tpu_custom_call" | custom-call | tf_op jit(solution)/shard_map/pallas_call | solution.py:606
  235.3 0.0 copy-start.2
  235.3 3.4 %copy.46 = bf16[24,90,384]{2,0,1:T(8,128)(2,1)} copy(bf16[24,90,384]{2,1,0:T(8,128)(2,1)} %get-tuple-element.29) | data formatting | bytes 3317760
  238.7 0.0 copy-done.2
  238.7 0.0 copy-start.6
  238.7 0.1 slice.54
  238.8 0.9 copy-done.6
  239.7 0.0 copy-start.7
  239.7 1.9 maximum_multiply_fusion
  241.6 0.0 copy-done.7
  241.6 0.7 copy.52
  (21 shorter events, 0.3 us)
Async XLA Ops:
  6.9 2.7 %copy-start = (bf16[12,192,384]{2,1,0:T(8,128)(2,1)}, bf16[12,192,384]{2,1,0:T(8,128)(2,1)S(1)}, u32[]{:S(2)}) copy-start(bf16[12,192,384]{2,1,0:T(8,128)(2,1)S(1)} %copy.28) | copy-start | bytes 5308420
  6.9 2.5 %copy-start.8 = (f32[192,384]{1,0:T(8,128)S(1)}, f32[192,384]{1,0:T(8,128)}, u32[]{:S(2)}) copy-start(f32[192,384]{1,0:T(8,128)} %param.15) | copy-start | bytes 884740
  9.4 3.2 %copy-start.10 = (s32[3,384]{1,0:T(4,128)S(1)}, s32[3,384]{1,0:T(4,128)}, u32[]{:S(2)}) copy-start(s32[3,384]{1,0:T(4,128)} %param.17) | copy-start | bytes 13828
  9.4 3.3 %copy-start.9 = (f32[3,3,7,384]{3,2,1,0:T(8,128)S(1)}, f32[3,3,7,384]{3,2,1,0:T(8,128)}, u32[]{:S(2)}) copy-start(f32[3,3,7,384]{3,2,1,0:T(8,128)} %param.16) | copy-start | bytes 290308
  14.6 84.3 %copy-start.3 = (bf16[24,90,384]{2,0,1:T(8,128)(2,1)S(1)}, bf16[24,90,384]{2,0,1:T(8,128)(2,1)}, u32[]{:S(2)}) copy-start(bf16[24,90,384]{2,0,1:T(8,128)(2,1)} %param.11) | copy-start | bytes 4976644
  98.9 1.6 copy-start.4
  109.8 4.0 %copy-start.1 = (bf16[3,384,384]{2,1,0:T(8,128)(2,1)S(1)}, bf16[3,384,384]{2,1,0:T(8,128)(2,1)}, u32[]{:S(2)}) copy-start(bf16[3,384,384]{2,1,0:T(8,128)(2,1)} %refs_10_.2) | copy-start | bytes 2654212
  109.8 6.2 %copy-start.5 = (bf16[384,384]{1,0:T(8,128)(2,1)S(1)}, bf16[384,384]{1,0:T(8,128)(2,1)}, u32[]{:S(2)}) copy-start(bf16[384,384]{1,0:T(8,128)(2,1)} %refs_2_.1) | copy-start | bytes 884740
  235.3 3.4 %copy-start.2 = (f32[4,384,384]{2,1,0:T(8,128)S(1)}, f32[4,384,384]{2,1,0:T(8,128)}, u32[]{:S(2)}) copy-start(f32[4,384,384]{2,1,0:T(8,128)} %get-tuple-element.21) | copy-start | bytes 7077892
  238.7 1.1 copy-start.6
  239.7 1.9 copy-start.7
